TPU v7x, 32 devices: a whole 2x2x4 slice. The times are simulated.
32 devices in a mesh: rep: 8 (over y, x, core), shard: 4 (over z).
Axes of the slice: x: 2, y: 2, z: 4, core: 2. Of those that a mesh axis runs over, the one named last changes fastest.
Arguments:
- hidden_in: bfloat16 [8192, 1600], P(('rep', 'shard'))
- cotangent: bfloat16 [8192, 1600], P(('rep', 'shard')), may hold values from -6 to 6
- slot_index: int32 [8192], P('rep'), may hold values from 0 to 1023, as said below
- seq_lengths: int32 [8, 2], P('rep'), may hold values from 384 to 640, as said below
- attn_gain: bfloat16 [1600], P('shard'), may hold values from 0.5 to 1.5
- attn_shift: bfloat16 [1600], P('shard'), may hold values from -4 to 4
- attn_weight: bfloat16 [1600, 4800], P('shard'), may hold values from -0.15625 to 0.15625
- query_bias: bfloat16 [1600], P('shard'), may hold values from -4 to 4
- value_bias: bfloat16 [1600], P('shard'), may hold values from -0.3125 to 0.3125
- out_weight: bfloat16 [1600, 1600], P('shard'), may hold values from -3 to 3
- out_bias: bfloat16 [1600], P('shard'), may hold values from -4 to 4
- mlp_gain: bfloat16 [1600], P('shard'), may hold values from 0.5 to 1.5
- mlp_shift: bfloat16 [1600], P('shard'), may hold values from -4 to 4
- up_weight: bfloat16 [1600, 6400], P('shard'), may hold values from -0.15625 to 0.15625
- up_bias: bfloat16 [6400], P('shard'), may hold values from -4 to 4
- down_weight: bfloat16 [6400, 1600], P('shard'), may hold values from -0.078125 to 0.078125
- down_bias: bfloat16 [1600], P('shard'), may hold values from -4 to 4
Outputs:
- block_out: bfloat16 [8192, 1600], P(('rep', 'shard'))
- input_grad: float32 [8192, 1600], P(('rep', 'shard'))
- grad_attn_gain: float32 [1600], P('shard')
- grad_attn_shift: float32 [1600], P('shard')
- grad_attn_weight: float32 [1600, 4800], P('shard')
- grad_query_bias: float32 [1600], P('shard')
- grad_value_bias: float32 [1600], P('shard')
- grad_out_weight: float32 [1600, 1600], P('shard')
- grad_out_bias: float32 [1600], P('shard')
- grad_mlp_gain: float32 [1600], P('shard')
- grad_mlp_shift: float32 [1600], P('shard')
- grad_up_weight: float32 [1600, 6400], P('shard')
- grad_up_bias: float32 [6400], P('shard')
- grad_down_weight: float32 [6400, 1600], P('shard')
- grad_down_bias: float32 [1600], P('shard')
Inputs may be any that keep to these rules, and one draw needn't show every extreme that they name: `slot_index`: within each group (one index of rep), entry s is the place in the group's pack of the token in slot s; the 1024 entries are a permutation that keeps aligned blocks of 128 slots whole and in order. Device k of shard holds slots k * 256 to (k + 1) * 256 - 1 of its group. `seq_lengths`: each row sums to 1024; the longer sequence of a group has min(1024, 512) tokens or more.
All inputs are finite; a program needn't handle non-finite values.
Results may differ from a plain program's by a relative error of at most 0.02.
Values may be sent and summed in bfloat16 or wider, within the bound.
No kernel may reach another device: no remote copies, remote signals or barrier semaphores. Data moves between devices by JAX's collectives and lax.ppermute only.
A program may use at most 384 MiB of HBM per device.

v0:
```python
import jax
import jax.numpy as jnp
from jax import lax
from jax.sharding import PartitionSpec as P

H = 25


EPSILON = 1e-05


def layer_norm(stream, gain_vec, shift_vec):
    average = jnp.mean(stream, axis=-1, keepdims=True)
    centred = stream - average
    variance = jnp.mean(centred * centred, axis=-1, keepdims=True)
    return centred * lax.rsqrt(variance + EPSILON) * gain_vec + shift_vec


def gelu_tanh(value_in):
    return jax.nn.gelu(value_in, approximate=True)


def doc_numbers(pack_ids, seq_sizes):
    ends_at = jnp.cumsum(seq_sizes)
    return jnp.sum((pack_ids[:, None] >= ends_at[None, :]).astype(jnp.int32), axis=1)


def contract_rows(left_op, right_op):
    return lax.dot_general(
        left_op, right_op, (((0,), (0,)), ((), ())), preferred_element_type=jnp.float32
    )


def times_transposed(left_op, right_op):
    return lax.dot_general(
        left_op, right_op, (((1,), (1,)), ((), ())), preferred_element_type=jnp.float32
    )


def column_sum(values_in):
    return jnp.sum(values_in.astype(jnp.float32), axis=0)


def per_device(
    hidden_in,
    cotangent,
    slot_index,
    seq_lengths,
    attn_gain,
    attn_shift,
    attn_weight,
    query_bias,
    value_bias,
    out_weight,
    out_bias,
    mlp_gain,
    mlp_shift,
    up_weight,
    up_bias,
    down_weight,
    down_bias,
):
    tok_rows, model_width = hidden_in.shape
    head_size = model_width // H
    group_size = slot_index.shape[0]
    key_rows = min(512, group_size)
    key_blocks = group_size // key_rows
    shard_pos = lax.axis_index("shard")
    doc_ids = doc_numbers(slot_index, seq_lengths[0])
    own_pack = lax.dynamic_slice_in_dim(slot_index, shard_pos * tok_rows, tok_rows)
    own_doc = lax.dynamic_slice_in_dim(doc_ids, shard_pos * tok_rows, tok_rows)
    block_pack = slot_index.reshape(key_blocks, key_rows)
    block_doc = doc_ids.reshape(key_blocks, key_rows)

    def split_heads(rows_in):
        return rows_in.reshape(rows_in.shape[0], H, head_size)

    def key_layout(rows_in):
        return rows_in.reshape(key_blocks, key_rows, H, head_size)

    attn_params = (
        lax.all_gather(attn_weight, "shard", axis=0, tiled=True),
        lax.all_gather(out_weight, "shard", axis=0, tiled=True),
        lax.all_gather(attn_gain, "shard", axis=0, tiled=True),
        lax.all_gather(attn_shift, "shard", axis=0, tiled=True),
        lax.all_gather(query_bias, "shard", axis=0, tiled=True),
        lax.all_gather(value_bias, "shard", axis=0, tiled=True),
        lax.all_gather(out_bias, "shard", axis=0, tiled=True),
    )
    stream = hidden_in.astype(jnp.float32)
    normed_a = layer_norm(
        stream, attn_params[2].astype(jnp.float32), attn_params[3].astype(jnp.float32)
    ).astype(jnp.bfloat16)
    mixed_rows = jnp.dot(normed_a, attn_params[0], preferred_element_type=jnp.float32)
    query_low = (mixed_rows[:, :model_width] + attn_params[4].astype(jnp.float32)).astype(
        jnp.bfloat16
    )
    key_low = mixed_rows[:, model_width : 2 * model_width].astype(jnp.bfloat16)
    value_low = (mixed_rows[:, 2 * model_width :] + attn_params[5].astype(jnp.float32)).astype(
        jnp.bfloat16
    )
    keys_all, values_all = (
        lax.all_gather(key_low, "shard", axis=0, tiled=True),
        lax.all_gather(value_low, "shard", axis=0, tiled=True),
    )
    queries = split_heads(query_low)

    def masked_scores(key_block, pack_block, doc_block):
        visible = (own_doc[:, None] == doc_block[None, :]) & (
            pack_block[None, :] <= own_pack[:, None]
        )
        raw = (
            jnp.einsum("thd,khd->htk", queries, key_block, preferred_element_type=jnp.float32)
            * 0.125
        )
        return jnp.where(visible[None], raw, -1000000000.0)

    def stats_step(carried, inputs):
        row_max, row_sum = carried
        key_block, pack_block, doc_block = inputs
        scores = masked_scores(key_block, pack_block, doc_block)
        new_max = jnp.maximum(row_max, jnp.max(scores, axis=-1))
        row_sum = row_sum * jnp.exp(row_max - new_max) + jnp.sum(
            jnp.exp(scores - new_max[:, :, None]), axis=-1
        )
        return ((new_max, row_sum), None)

    start_stats = (
        jnp.full((H, tok_rows), -1e30, jnp.float32),
        jnp.zeros((H, tok_rows), jnp.float32),
    )
    (row_max, row_sum), _ = lax.scan(
        stats_step, start_stats, (key_layout(keys_all), block_pack, block_doc)
    )
    log_total = row_max + jnp.log(row_sum)

    def mix_step(carried, inputs):
        key_block, value_block, pack_block, doc_block = inputs
        scores = masked_scores(key_block, pack_block, doc_block)
        soft_low = jnp.exp(scores - log_total[:, :, None]).astype(jnp.bfloat16)
        return (
            carried
            + jnp.einsum("htk,khd->thd", soft_low, value_block, preferred_element_type=jnp.float32),
            None,
        )

    attended_heads, _ = lax.scan(
        mix_step,
        jnp.zeros((tok_rows, H, head_size), jnp.float32),
        (key_layout(keys_all), key_layout(values_all), block_pack, block_doc),
    )
    attended = attended_heads.reshape(tok_rows, model_width)
    attended_low = attended.astype(jnp.bfloat16)
    middle = (
        stream
        + jnp.dot(attended_low, attn_params[1], preferred_element_type=jnp.float32)
        + attn_params[6].astype(jnp.float32)
    )
    mlp_params = (
        lax.all_gather(up_weight, "shard", axis=0, tiled=True),
        lax.all_gather(down_weight, "shard", axis=0, tiled=True),
        lax.all_gather(mlp_gain, "shard", axis=0, tiled=True),
        lax.all_gather(mlp_shift, "shard", axis=0, tiled=True),
        lax.all_gather(up_bias, "shard", axis=0, tiled=True),
        lax.all_gather(down_bias, "shard", axis=0, tiled=True),
    )
    normed_b = layer_norm(
        middle, mlp_params[2].astype(jnp.float32), mlp_params[3].astype(jnp.float32)
    ).astype(jnp.bfloat16)
    pre_act = jnp.dot(normed_b, mlp_params[0], preferred_element_type=jnp.float32) + mlp_params[
        4
    ].astype(jnp.float32)
    act_low = gelu_tanh(pre_act).astype(jnp.bfloat16)
    block_out = (
        middle
        + jnp.dot(act_low, mlp_params[1], preferred_element_type=jnp.float32)
        + mlp_params[5].astype(jnp.float32)
    ).astype(jnp.bfloat16)
    mlp_back = (
        lax.all_gather(up_weight, "shard", axis=0, tiled=True),
        lax.all_gather(down_weight, "shard", axis=0, tiled=True),
        lax.all_gather(mlp_gain, "shard", axis=0, tiled=True),
        lax.all_gather(mlp_shift, "shard", axis=0, tiled=True),
        lax.all_gather(up_bias, "shard", axis=0, tiled=True),
        lax.all_gather(down_bias, "shard", axis=0, tiled=True),
    )
    act_grad = times_transposed(cotangent, mlp_back[1])
    _, gelu_back = jax.vjp(gelu_tanh, pre_act)
    pre_grad = gelu_back(act_grad)[0].astype(jnp.bfloat16)
    normed_b_grad = times_transposed(pre_grad, mlp_back[0])
    _, second_back = jax.vjp(
        layer_norm, middle, mlp_back[2].astype(jnp.float32), mlp_back[3].astype(jnp.float32)
    )
    middle_part, grad_mlp_gain, grad_mlp_shift = second_back(normed_b_grad)
    middle_grad = cotangent.astype(jnp.float32) + middle_part
    grad_down = contract_rows(act_low, cotangent)
    grad_down_bias = column_sum(cotangent)
    grad_up_bias = column_sum(pre_grad)
    grad_up = contract_rows(normed_b, pre_grad)
    mlp_owned = (
        lax.psum_scatter(
            grad_down.astype(jnp.bfloat16), "shard", scatter_dimension=0, tiled=True
        ).astype(jnp.float32),
        lax.psum_scatter(
            grad_up.astype(jnp.bfloat16), "shard", scatter_dimension=0, tiled=True
        ).astype(jnp.float32),
        lax.psum_scatter(
            grad_up_bias.astype(jnp.bfloat16), "shard", scatter_dimension=0, tiled=True
        ).astype(jnp.float32),
        lax.psum_scatter(
            grad_down_bias.astype(jnp.bfloat16), "shard", scatter_dimension=0, tiled=True
        ).astype(jnp.float32),
        lax.psum_scatter(
            grad_mlp_gain.astype(jnp.bfloat16), "shard", scatter_dimension=0, tiled=True
        ).astype(jnp.float32),
        lax.psum_scatter(
            grad_mlp_shift.astype(jnp.bfloat16), "shard", scatter_dimension=0, tiled=True
        ).astype(jnp.float32),
    )
    attn_back = (
        lax.all_gather(attn_weight, "shard", axis=0, tiled=True),
        lax.all_gather(out_weight, "shard", axis=0, tiled=True),
        lax.all_gather(attn_gain, "shard", axis=0, tiled=True),
        lax.all_gather(attn_shift, "shard", axis=0, tiled=True),
        lax.all_gather(query_bias, "shard", axis=0, tiled=True),
        lax.all_gather(value_bias, "shard", axis=0, tiled=True),
        lax.all_gather(out_bias, "shard", axis=0, tiled=True),
    )
    branch_grad = middle_grad.astype(jnp.bfloat16)
    attended_grad = times_transposed(branch_grad, attn_back[1]).astype(jnp.bfloat16)
    grad_heads = split_heads(attended_grad)
    row_delta = jnp.einsum("thd,thd->ht", grad_heads.astype(jnp.float32), attended_heads)

    def grad_step(carried, inputs):
        key_block, value_block, pack_block, doc_block = inputs
        scores = masked_scores(key_block, pack_block, doc_block)
        soft_vals = jnp.exp(scores - log_total[:, :, None])
        soft_low = soft_vals.astype(jnp.bfloat16)
        value_grad = jnp.einsum(
            "htk,thd->khd", soft_low, grad_heads, preferred_element_type=jnp.float32
        )
        prob_grad = jnp.einsum(
            "thd,khd->htk", grad_heads, value_block, preferred_element_type=jnp.float32
        )
        score_grad = (soft_vals * (prob_grad - row_delta[:, :, None])).astype(jnp.bfloat16)
        carried = (
            carried
            + jnp.einsum("htk,khd->thd", score_grad, key_block, preferred_element_type=jnp.float32)
            * 0.125
        )
        key_grad = (
            jnp.einsum("htk,thd->khd", score_grad, queries, preferred_element_type=jnp.float32)
            * 0.125
        )
        return (carried, (key_grad, value_grad))

    query_grad, (key_grad_blocks, value_grad_blocks) = lax.scan(
        grad_step,
        jnp.zeros((tok_rows, H, head_size), jnp.float32),
        (key_layout(keys_all), key_layout(values_all), block_pack, block_doc),
    )
    own_key_grad, own_value_grad = (
        lax.psum_scatter(
            key_grad_blocks.reshape(group_size, model_width).astype(jnp.bfloat16),
            "shard",
            scatter_dimension=0,
            tiled=True,
        ).astype(jnp.float32),
        lax.psum_scatter(
            value_grad_blocks.reshape(group_size, model_width).astype(jnp.bfloat16),
            "shard",
            scatter_dimension=0,
            tiled=True,
        ).astype(jnp.float32),
    )
    query_grad_low = query_grad.reshape(tok_rows, model_width).astype(jnp.bfloat16)
    key_grad_low = own_key_grad.astype(jnp.bfloat16)
    value_grad_low = own_value_grad.astype(jnp.bfloat16)
    mixed_grad = jnp.concatenate([query_grad_low, key_grad_low, value_grad_low], axis=1)
    normed_a_grad = times_transposed(mixed_grad, attn_back[0])
    _, first_back = jax.vjp(
        layer_norm, stream, attn_back[2].astype(jnp.float32), attn_back[3].astype(jnp.float32)
    )
    stream_part, grad_attn_gain, grad_attn_shift = first_back(normed_a_grad)
    input_grad = middle_grad + stream_part
    grad_out_w = contract_rows(attended_low, branch_grad)
    grad_out_bias = column_sum(branch_grad)
    grad_query_bias = column_sum(query_grad_low)
    grad_value_bias = column_sum(value_grad_low)
    grad_mix = contract_rows(normed_a, mixed_grad)
    attn_owned = (
        lax.psum_scatter(
            grad_attn_gain.astype(jnp.bfloat16), "shard", scatter_dimension=0, tiled=True
        ).astype(jnp.float32),
        lax.psum_scatter(
            grad_attn_shift.astype(jnp.bfloat16), "shard", scatter_dimension=0, tiled=True
        ).astype(jnp.float32),
        lax.psum_scatter(
            grad_mix.astype(jnp.bfloat16), "shard", scatter_dimension=0, tiled=True
        ).astype(jnp.float32),
        lax.psum_scatter(
            grad_query_bias.astype(jnp.bfloat16), "shard", scatter_dimension=0, tiled=True
        ).astype(jnp.float32),
        lax.psum_scatter(
            grad_value_bias.astype(jnp.bfloat16), "shard", scatter_dimension=0, tiled=True
        ).astype(jnp.float32),
        lax.psum_scatter(
            grad_out_w.astype(jnp.bfloat16), "shard", scatter_dimension=0, tiled=True
        ).astype(jnp.float32),
        lax.psum_scatter(
            grad_out_bias.astype(jnp.bfloat16), "shard", scatter_dimension=0, tiled=True
        ).astype(jnp.float32),
    )
    mlp_final = (
        lax.psum(mlp_owned[0].astype(jnp.bfloat16), "rep").astype(jnp.float32),
        lax.psum(mlp_owned[1].astype(jnp.bfloat16), "rep").astype(jnp.float32),
        lax.psum(mlp_owned[2].astype(jnp.bfloat16), "rep").astype(jnp.float32),
        lax.psum(mlp_owned[3].astype(jnp.bfloat16), "rep").astype(jnp.float32),
        lax.psum(mlp_owned[4].astype(jnp.bfloat16), "rep").astype(jnp.float32),
        lax.psum(mlp_owned[5].astype(jnp.bfloat16), "rep").astype(jnp.float32),
    )
    attn_final = (
        lax.psum(attn_owned[0].astype(jnp.bfloat16), "rep").astype(jnp.float32),
        lax.psum(attn_owned[1].astype(jnp.bfloat16), "rep").astype(jnp.float32),
        lax.psum(attn_owned[2].astype(jnp.bfloat16), "rep").astype(jnp.float32),
        lax.psum(attn_owned[3].astype(jnp.bfloat16), "rep").astype(jnp.float32),
        lax.psum(attn_owned[4].astype(jnp.bfloat16), "rep").astype(jnp.float32),
        lax.psum(attn_owned[5].astype(jnp.bfloat16), "rep").astype(jnp.float32),
        lax.psum(attn_owned[6].astype(jnp.bfloat16), "rep").astype(jnp.float32),
    )
    return (
        block_out,
        input_grad,
        attn_final[0],
        attn_final[1],
        attn_final[2],
        attn_final[3],
        attn_final[4],
        attn_final[5],
        attn_final[6],
        mlp_final[4],
        mlp_final[5],
        mlp_final[1],
        mlp_final[2],
        mlp_final[0],
        mlp_final[3],
    )


def solution(mesh):
    return jax.shard_map(
        per_device,
        mesh=mesh,
        in_specs=(
            P(("rep", "shard"), None),
            P(("rep", "shard"), None),
            P("rep"),
            P("rep", None),
            P("shard"),
            P("shard"),
            P("shard", None),
            P("shard"),
            P("shard"),
            P("shard", None),
            P("shard"),
            P("shard"),
            P("shard"),
            P("shard", None),
            P("shard"),
            P("shard", None),
            P("shard"),
        ),
        out_specs=(
            P(("rep", "shard"), None),
            P(("rep", "shard"), None),
            P("shard"),
            P("shard"),
            P("shard", None),
            P("shard"),
            P("shard"),
            P("shard", None),
            P("shard"),
            P("shard"),
            P("shard"),
            P("shard", None),
            P("shard"),
            P("shard", None),
            P("shard"),
        ),
        check_vma=False,
    )
```

profile of v0, /device:TPU:0, one launch (start us, length us, event | category | flops | bytes accessed | tf_op | source)
XLA Modules:
  0.0 2787.2 jit_solution(5856353526497810987)
XLA Ops:
  12.1 21.7 all-reduce.21
  34.4 245.2 %all-gather.7.cloned.1.call-done = bf16[1600,4800]{1,0:T(8,128)(2,1)} async-done(((bf16[400,4800]{1,0:T(8,128)(2,1)}), bf16[1600,4800]{1,0:T(8,128)(2,1)}) %all-gather.7.cloned.1.call-update) | async-done | bytes 15360016 | tf_op jit(solution)/shard_map/all_gather | solution.py:82
  279.6 14.8 fusion.76
  303.9 58.2 %all-gather.9.cloned.1.call-done = bf16[1024,1600]{0,1:T(8,128)(2,1)} async-done(((bf16[256,1600]{0,1:T(8,128)(2,1)}), bf16[1024,1600]{0,1:T(8,128)(2,1)}) %all-gather.9.cloned.1.call-update) | async-done | bytes 3276816 | tf_op jit(solution)/shard_map/all_gather | solution.py:104
  371.9 56.1 %all-gather.11.cloned.1.call-done = bf16[1024,1600]{0,1:T(8,128)(2,1)} async-done(((bf16[256,1600]{0,1:T(8,128)(2,1)}), bf16[1024,1600]{0,1:T(8,128)(2,1)}) %all-gather.11.cloned.1.call-update) | async-done | bytes 3276816 | tf_op jit(solution)/shard_map/all_gather | solution.py:103
  439.4 31.6 %while.39 = (s32[]{:T(128)}, f32[25,256]{1,0:T(8,128)S(1)}, f32[25,256]{1,0:T(8,128)S(1)}, s32[256]{0:T(256)S(1)}, s32[2,512]{1,0:T(2,128)S(1)}, /*index=5*/s32[...) while((s32[]{:T(128)}, f32[25,256]{1,0:T(8,128)S(1)}, ...), condition=%wide.region_7.8_spmd.clone, body=%wide.region_4.7_spmd.clone.sunk | while | flops 442793216 | bytes 29412488 | solution.py:132
  471.0 15.4 while.40
  488.9 38.1 %all-gather.13.cloned.1.call-done = bf16[1600,1600]{1,0:T(8,128)(2,1)} async-done(((bf16[400,1600]{1,0:T(8,128)(2,1)}), bf16[1600,1600]{1,0:T(8,128)(2,1)}) %all-gather.13.cloned.1.call-update) | async-done | bytes 5120016 | tf_op jit(solution)/shard_map/all_gather | solution.py:83
  533.9 355.2 %all-gather.17.cloned.1.call-done = bf16[6400,1600]{1,0:T(8,128)(2,1)} async-done(((bf16[1600,1600]{1,0:T(8,128)(2,1)}), bf16[6400,1600]{1,0:T(8,128)(2,1)}) %all-gather.17.cloned.1.call-update) | async-done | bytes 20480016 | tf_op jit(solution)/shard_map/all_gather | solution.py:161
  902.0 335.9 %all-gather.15.cloned.1.call-done = bf16[1600,6400]{1,0:T(8,128)(2,1)} async-done(((bf16[400,6400]{1,0:T(8,128)(2,1)}), bf16[1600,6400]{1,0:T(8,128)(2,1)}) %all-gather.15.cloned.1.call-update) | async-done | bytes 20480016 | tf_op jit(solution)/shard_map/all_gather | solution.py:160
  1237.9 22.9 fusion.79
  1260.8 13.9 multiply_reduce_fusion
  1282.4 72.2 %while.41 = (s32[]{:T(128)}, f32[256,25,64]{0,2,1:T(8,128)}, bf16[2,512,25,64]{1,3,2,0:T(8,128)(2,1)}, bf16[2,512,25,64]{1,3,2,0:T(8,128)(2,1)}, bf16[2,512,25,6...) while((s32[]{:T(128)}, f32[256,25,64]{0,2,1:T(8,128)}, ...), condition=%wide.region_15.16_spmd.clone, body=%wide.region_14.15_spmd.clone.sunk | while | flops 2122530816 | bytes 231342608 | solution.py:257
  1377.7 45.9 %reduce-scatter.9.cloned.1.call-done = bf16[256,1600]{0,1:T(8,128)(2,1)} async-done(((bf16[1024,1600]{0,1:T(8,128)(2,1)}), bf16[256,1600]{0,1:T(8,128)(2,1)}) %reduce-scatter.9.cloned.1.call-update) | async-done | bytes 819216 | tf_op jit(solution)/shard_map/reduce_scatter | solution.py:269
  1423.6 64.7 %reduce-scatter.7.cloned.1.call-done = bf16[256,1600]{0,1:T(8,128)(2,1)} async-done(((bf16[1024,1600]{0,1:T(8,128)(2,1)}), bf16[256,1600]{0,1:T(8,128)(2,1)}) %reduce-scatter.7.cloned.1.call-update) | async-done | bytes 819216 | tf_op jit(solution)/shard_map/reduce_scatter | solution.py:263
  1513.0 13.5 convolution_convert_fusion
  1526.9 59.8 %reduce-scatter.13.cloned.1.call-done = bf16[400,1600]{1,0:T(8,128)(2,1)} async-done(((bf16[1600,1600]{1,0:T(8,128)(2,1)}), bf16[400,1600]{1,0:T(8,128)(2,1)}) %reduce-scatter.13.cloned.1.call-update) | async-done | bytes 1280016 | tf_op jit(solution)/shard_map/reduce_scatter | solution.py:307
  1586.7 263.1 %reduce-scatter.11.cloned.1.call-done = bf16[400,4800]{1,0:T(8,128)(2,1)} async-done(((bf16[1600,4800]{1,0:T(8,128)(2,1)}), bf16[400,4800]{1,0:T(8,128)(2,1)}) %reduce-scatter.11.cloned.1.call-update) | async-done | bytes 3840016 | tf_op jit(solution)/shard_map/reduce_scatter | solution.py:298
  1849.8 343.2 %reduce-scatter.15.cloned.1.call-done = bf16[400,6400]{1,0:T(8,128)(2,1)} async-done(((bf16[1600,6400]{1,0:T(8,128)(2,1)}), bf16[400,6400]{1,0:T(8,128)(2,1)}) %reduce-scatter.15.cloned.1.call-update) | async-done | bytes 5120016 | tf_op jit(solution)/shard_map/reduce_scatter | solution.py:204
  2193.0 356.4 %reduce-scatter.17.cloned.1.call-done = bf16[1600,1600]{1,0:T(8,128)(2,1)} async-done(((bf16[6400,1600]{1,0:T(8,128)(2,1)}), bf16[1600,1600]{1,0:T(8,128)(2,1)}) %reduce-scatter.17.cloned.1.call-update) | async-done | bytes 5120016 | tf_op jit(solution)/shard_map/reduce_scatter | solution.py:201
  2565.3 19.9 all-reduce.20
  2586.0 24.0 all-reduce.18
  2619.0 17.6 fusion.52
  2636.7 126.4 %all-reduce.24.cloned.1.call-done = (bf16[400,4800]{1,0:T(8,128)(2,1)}, bf16[400,1600]{1,0:T(8,128)(2,1)}, bf16[400,6400]{1,0:T(8,128)(2,1)}, bf16[1600,1600]{1,0:T(8,128)(2,1)}) async-done(((bf16[400,4800]{1,0:T(8,128)(2,1)}, bf16[400,1600]{1,0:T(8,128)(2,1)}, bf16[400,6400]{1,0:T(8,128)(2,1)}, bf16[1600,1600]{1,0:T(8,128)(2,1)}), (bf16[400,4800]{1,0:T(8,128)(2,1)}, bf16[400,1600]{1,0:T(8,128)(2,1)}, ...) | async-done | bytes 15360016 | tf_op jit(solution)/shard_map/psum | solution.py:325
  (316 shorter events, 272.1 us)
Async XLA Ops:
  7.3 272.4 %all-gather.7.cloned.1.call-start = ((), (), s32[]{:S(2)}) async-start(), calls=%async_computation.6 | async-start | bytes 19456000 | tf_op jit(solution)/shard_map/all_gather | solution.py:82
  8.0 354.0 %all-gather.9.cloned.1.call-start = ((), (), s32[]{:S(2)}) async-start(), calls=%async_computation.7 | async-start | bytes 4096000 | tf_op jit(solution)/shard_map/all_gather | solution.py:104
  33.8 260.6 %copy-start.34 = (f32[1600]{0:T(1024)}, f32[1600]{0:T(1024)S(1)}, u32[]{:S(2)}) copy-start(f32[1600]{0:T(1024)S(1)} %convert_element_type.206) | copy-start | bytes 19204
  33.8 260.6 %copy-start.30 = (f32[1600]{0:T(1024)}, f32[1600]{0:T(1024)S(1)}, u32[]{:S(2)}) copy-start(f32[1600]{0:T(1024)S(1)} %convert_element_type.205) | copy-start | bytes 19204
  34.1 260.3 %copy-start.36 = (f32[256]{0:T(256)}, f32[256]{0:T(256)S(1)}, u32[]{:S(2)}) copy-start(f32[256]{0:T(256)S(1)} %broadcast_multiply_fusion.1) | copy-start | bytes 3076
  34.4 260.0 %copy-start.47 = (f32[256]{0:T(256)}, f32[256]{0:T(256)S(1)}, u32[]{:S(2)}) copy-start(f32[256]{0:T(256)S(1)} %fusion.62) | copy-start | bytes 3076
  34.4 260.0 %copy-start.38 = (f32[256]{0:T(256)}, f32[256]{0:T(256)S(1)}, u32[]{:S(2)}) copy-start(f32[256]{0:T(256)S(1)} %fusion.71) | copy-start | bytes 3076
  298.0 129.9 %all-gather.11.cloned.1.call-start = ((), (), s32[]{:S(2)}) async-start(), calls=%async_computation.8 | async-start | bytes 4096000 | tf_op jit(solution)/shard_map/all_gather | solution.py:103
  300.5 226.5 %all-gather.13.cloned.1.call-start = ((), (), s32[]{:S(2)}) async-start(), calls=%async_computation.9 | async-start | bytes 6656000 | tf_op jit(solution)/shard_map/all_gather | solution.py:83
  301.1 588.0 %all-gather.17.cloned.1.call-start = ((), (), s32[]{:S(2)}) async-start(), calls=%async_computation.11 | async-start | bytes 26624000 | tf_op jit(solution)/shard_map/all_gather | solution.py:161
  301.7 936.2 %all-gather.15.cloned.1.call-start = ((), (), s32[]{:S(2)}) async-start(), calls=%async_computation.10 | async-start | bytes 25600000 | tf_op jit(solution)/shard_map/all_gather | solution.py:160
  302.3 1121.4 %reduce-scatter.9.cloned.1.call-start = ((), (), s32[]{:S(2)}) async-start(), calls=%async_computation.13 | async-start | bytes 4096000 | tf_op jit(solution)/shard_map/reduce_scatter | solution.py:269
  303.9 934.0 %copy-start.32 = (f32[1600]{0:T(1024)}, f32[1600]{0:T(1024)S(1)}, u32[]{:S(2)}) copy-start(f32[1600]{0:T(1024)S(1)} %convert_element_type.217) | copy-start | bytes 19204
  533.9 704.0 %copy-start.40 = (f32[6400]{0:T(1024)S(1)}, f32[6400]{0:T(1024)}, u32[]{:S(2)}) copy-start(f32[6400]{0:T(1024)} %convert_element_type.219) | copy-start | bytes 76804
  1362.5 125.8 %reduce-scatter.7.cloned.1.call-start = ((), (), s32[]{:S(2)}) async-start(), calls=%async_computation.12 | async-start | bytes 4096000 | tf_op jit(solution)/shard_map/reduce_scatter | solution.py:263
  1370.6 216.1 %reduce-scatter.13.cloned.1.call-start = ((), (), s32[]{:S(2)}) async-start(), calls=%async_computation.15 | async-start | bytes 6656000 | tf_op jit(solution)/shard_map/reduce_scatter | solution.py:307
  1376.0 112.4 %copy-start.12 = (bf16[256,1600]{0,1:T(8,128)(2,1)S(1)}, bf16[256,1600]{0,1:T(8,128)(2,1)}, u32[]{:S(2)}) copy-start(bf16[256,1600]{0,1:T(8,128)(2,1)} %param.23) | copy-start | bytes 2457604
  1376.0 112.4 %copy-start.31 = (f32[1600]{0:T(1024)S(1)}, f32[1600]{0:T(1024)}, u32[]{:S(2)}) copy-start(f32[1600]{0:T(1024)} %copy-done.30) | copy-start | bytes 19204
  1376.0 112.4 %copy-start.35 = (f32[1600]{0:T(1024)S(1)}, f32[1600]{0:T(1024)}, u32[]{:S(2)}) copy-start(f32[1600]{0:T(1024)} %copy-done.34) | copy-start | bytes 19204
  1376.1 473.7 %reduce-scatter.11.cloned.1.call-start = ((), (), s32[]{:S(2)}) async-start(), calls=%async_computation.14 | async-start | bytes 19456000 | tf_op jit(solution)/shard_map/reduce_scatter | solution.py:298
  1377.7 120.5 %copy-start.28 = (bf16[256,25,64]{0,2,1:T(8,128)(2,1)}, bf16[256,25,64]{0,2,1:T(8,128)(2,1)S(1)}, u32[]{:S(2)}) copy-start(bf16[256,25,64]{0,2,1:T(8,128)(2,1)S(1)} %get-tuple-element.544) | copy-start | bytes 2457604
  1498.3 694.7 %reduce-scatter.15.cloned.1.call-start = ((), (), s32[]{:S(2)}) async-start(), calls=%async_computation.16 | async-start | bytes 25600000 | tf_op jit(solution)/shard_map/reduce_scatter | solution.py:204
  1511.9 1037.5 %reduce-scatter.17.cloned.1.call-start = ((), (), s32[]{:S(2)}) async-start(), calls=%async_computation.17 | async-start | bytes 26624000 | tf_op jit(solution)/shard_map/reduce_scatter | solution.py:201
  1526.6 1236.5 %all-reduce.24.cloned.1.call-start = ((), (), s32[]{:S(2)}) async-start(), calls=%async_computation.18 | async-start | bytes 31334400 | tf_op jit(solution)/shard_map/psum | solution.py:325
  (66 other events, 656.7 us)
Sparse Core Ops, SparseCore 0:
  9.7 269.9 all-gather.6
  298.2 63.8 all-gather.8
  364.2 63.7 all-gather.10
  429.4 97.5 all-gather.12
  528.5 360.5 all-gather.16
  890.5 347.3 all-gather.14
  1362.7 60.9 reduce-scatter.8
  1426.0 62.3 reduce-scatter.6
  1491.3 95.3 reduce-scatter.12
  1588.9 260.8 reduce-scatter.10
  1852.3 340.6 reduce-scatter.14
  2195.2 354.1 reduce-scatter.16
  2553.4 209.5 all-reduce.23
where the time goes:
time: 2800 us; the launch traced here: 2790 us
  waiting for transfers between devices  2350 us (84%)
  matrix products  227 us (8%)
  local copies, waits for them, and re-layouts  68.7 us (2%)
  blocking collectives  65.7 us (2%)
  other arithmetic  54.6 us (2%)
    reduce_scatter x1, waiting for transfers between devices, per_device(): lax.psum_scatter(grad_down.astype(jnp.bfloat16), 'shard', scatter_dimensi...  356 us
    all_gather x1, waiting for transfers between devices, per_device(): lax.all_gather(down_weight, 'shard', axis=0, tiled=True)  355 us
    reduce_scatter x1, waiting for transfers between devices, per_device(): lax.psum_scatter(grad_up.astype(jnp.bfloat16), 'shard', scatter_dimension...  343 us
    all_gather x1, waiting for transfers between devices, per_device(): lax.all_gather(up_weight, 'shard', axis=0, tiled=True)  336 us
    reduce_scatter x1, waiting for transfers between devices, per_device(): lax.psum_scatter(grad_mix.astype(jnp.bfloat16), 'shard', scatter_dimensio...  263 us
    all_gather x1, waiting for transfers between devices, per_device(): lax.all_gather(attn_weight, 'shard', axis=0, tiled=True)  245 us
    psum x1, waiting for transfers between devices, per_device(): lax.psum(attn_owned[2].astype(jnp.bfloat16), 'rep').astype(jnp.float32)  126 us
    reduce_scatter x1, waiting for transfers between devices, per_device(): lax.psum_scatter(key_grad_blocks.reshape(group_size, model_width).astype(...  64.7 us
  transfers between devices with their start and end apart: 13, of which 13 were waited for; matrix products, arithmetic and copies ran while one was open for 7% of the time, Pallas kernels for 0%

commit v1 on v0

v1 whole, which is shorter than its diff:
```python
import functools

import jax
import jax.numpy as jnp
from jax import lax
from jax.experimental import pallas as pl
from jax.experimental.pallas import tpu as pltpu
from jax.sharding import Mesh
from jax.sharding import PartitionSpec as P

H = 25
BLK = 128
TILE = 256
EPSILON = 1e-05
BF = jnp.bfloat16
F32 = jnp.float32
VMEM_LIMIT = 56 * 1024 * 1024
SMALL_ROWS = 8


def dot_nt(a, b):
    return lax.dot_general(a, b, (((1,), (1,)), ((), ())), preferred_element_type=F32)


def dot_tn(a, b):
    return lax.dot_general(a, b, (((0,), (0,)), ((), ())), preferred_element_type=F32)


def dot_nn(a, b):
    return lax.dot_general(a, b, (((1,), (0,)), ((), ())), preferred_element_type=F32)


def head_plan(shards):
    base, extra = H // shards, H % shards
    counts = [base + (1 if s < extra else 0) for s in range(shards)]
    starts = [sum(counts[:s]) for s in range(shards)]
    width = max(counts)
    windows = [min(st, H - width) for st in starts]
    return counts, starts, windows, width


LONG = 20_000_000_000
SHORT = 10_000_000_000


def call(kernel, scalars, grid, ins, outs, scratch=(), flops=1024):
    return pl.pallas_call(
        kernel,
        out_shape=[jax.ShapeDtypeStruct(shape, dtype) for shape, dtype, _ in outs],
        grid_spec=pltpu.PrefetchScalarGridSpec(
            num_scalar_prefetch=len(scalars),
            grid=grid,
            in_specs=[spec for _, spec in ins],
            out_specs=[spec for _, _, spec in outs],
            scratch_shapes=list(scratch),
        ),
        compiler_params=pltpu.CompilerParams(vmem_limit_bytes=VMEM_LIMIT),
        cost_estimate=pl.CostEstimate(flops=flops, bytes_accessed=1024, transcendentals=0),
    )(*scalars, *[array for array, _ in ins])


def whole(array):
    zeros = (0,) * array.ndim
    return pl.BlockSpec(array.shape, lambda *_: zeros, pipeline_mode=pl.Buffered(1))


def fixed(shape):
    zeros = (0,) * len(shape)
    return pl.BlockSpec(shape, lambda *_: zeros)


def tokens(rows):
    return pl.BlockSpec((rows, TILE), lambda i, *_: (0, i))


def slot_block(rows, per, which):
    return pl.BlockSpec(
        (rows, BLK), lambda i, tab, *_: (tab[2 * i + which] // per, lax.rem(tab[2 * i + which], per))
    )


STEP = 80


def sweep(rows, body, carry, step=STEP):
    while rows % step:
        step -= 16
    for at in range(0, rows, step):
        carry = body(pl.ds(at, step), carry)
    return carry


def chunk(rows, lanes):
    step = STEP
    while rows % step:
        step -= 16
    return jnp.zeros((step, lanes), F32)


def column_mean(acc, rows):
    return jnp.sum(acc, axis=0, keepdims=True) * (1.0 / rows)


def norm_stats(load, rows, lanes):
    zero = chunk(rows, lanes)
    mean = column_mean(sweep(rows, lambda at, acc: acc + load(at), zero), rows)

    def spread(at, acc):
        centred = load(at) - mean
        return acc + centred * centred

    return mean, lax.rsqrt(column_mean(sweep(rows, spread, zero), rows) + EPSILON)


def norm_back(load, load_e, gain_ref, col, rows, lanes, write):
    mean, rstd = norm_stats(load, rows, lanes)
    zero = chunk(rows, lanes)

    def both(at):
        return (load(at) - mean) * rstd, load_e(at) * gain_ref[at, col : col + 1]

    def sums(at, carry):
        x, c = both(at)
        return carry[0] + c, carry[1] + c * x

    mean_c, mean_cx = sweep(rows, sums, (zero, zero))
    mean_c, mean_cx = column_mean(mean_c, rows), column_mean(mean_cx, rows)

    def last(at, carry):
        x, c = both(at)
        write(at, rstd * (c - mean_c - x * mean_cx))
        return carry

    sweep(rows, last, 0)


def slot_places(tab_ref, rows, per):
    places = []
    for which in range(2):
        place = tab_ref[2 * pl.program_id(0) + which]
        row = pl.multiple_of((place // per) * rows, 16)
        places.append((row, pl.multiple_of(lax.rem(place, per) * BLK, BLK)))
    return places


def store_slots(out_ref, places, at, value):
    for which, (row, lane) in enumerate(places):
        rows = pl.ds(pl.multiple_of(row + at.start, 16), at.size)
        out_ref[rows, pl.ds(lane, BLK)] = value[:, which * BLK : (which + 1) * BLK].astype(out_ref.dtype)


def clear_first(*refs):
    @pl.when(pl.program_id(0) == 0)
    def _():
        for ref in refs:
            ref[...] = jnp.zeros_like(ref)


def first_norm_kernel(tab_ref, h0_ref, h1_ref, small_ref, na_ref, pack_ref):
    rows = na_ref.shape[0]
    for j, ref in enumerate((h0_ref, h1_ref)):
        load = lambda at, ref=ref: ref[at, :].astype(F32)
        mean, rstd = norm_stats(load, rows, BLK)

        def write(at, carry, load=load, mean=mean, rstd=rstd, j=j):
            x = (load(at) - mean) * rstd
            na_ref[at, j * BLK : (j + 1) * BLK] = (x * small_ref[at, 0:1] + small_ref[at, 1:2]).astype(BF)
            return carry

        pack_ref[:, j * BLK : (j + 1) * BLK] = ref[...]

        sweep(rows, write, 0)


def first_norm_call(tab, hidden_all, small, shards):
    width, tok = small.shape[0], hidden_all.shape[1]
    group = tok * shards
    per = tok // BLK
    return call(
        first_norm_kernel,
        (tab,),
        (group // TILE,),
        [
            (hidden_all, slot_block(width, per, 0)),
            (hidden_all, slot_block(width, per, 1)),
            (small, whole(small)),
        ],
        [((width, group), BF, tokens(width))] * 2,
        flops=LONG,
    )


def tile_variants(tiles):
    return [(i, st) for i in range(tiles) for st in range(i + 1)]


def allowed_mask(first_len, q_base, k_base, k_rows):
    kpos = k_base + lax.broadcasted_iota(jnp.int32, (k_rows, TILE), 0)
    qrow = q_base + lax.broadcasted_iota(jnp.int32, (1, TILE), 1)
    low = jnp.where(qrow >= first_len, first_len, 0)
    return (kpos <= qrow) & (kpos >= low)


def attend_kernel(len_ref, q_ref, k_ref, v_ref, o_ref, ol_ref, lse_ref, *, tiles):
    first_len = len_ref[0]
    for i, st in tile_variants(tiles):
        q_base = i * TILE
        start = jnp.where(q_base >= first_len, first_len // TILE, 0)

        @pl.when(start == st)
        def _():
            rows = pl.ds(q_base, TILE)
            keys = pl.ds(st * TILE, (i + 1 - st) * TILE)
            ok = allowed_mask(first_len, q_base, st * TILE, (i + 1 - st) * TILE)
            s = dot_tn(k_ref[:, keys], q_ref[:, rows] * jnp.asarray(0.125, BF))
            s = jnp.where(ok, s, -1000000000.0)
            top = jnp.max(s, axis=0, keepdims=True)
            e = jnp.exp(s - top)
            tot = jnp.sum(e, axis=0, keepdims=True)
            soft = (e * (1.0 / tot)).astype(BF)
            o = dot_nn(v_ref[:, keys], soft)
            o_ref[:, rows] = o
            ol_ref[:, rows] = o.astype(BF)
            lse_ref[0, :, rows] = top + jnp.log(tot)


def attend(first_len, qkv, heads):
    group = qkv.shape[1]
    rows = heads * 64
    block = lambda off: pl.BlockSpec((64, group), lambda h, t, off=off: (off + h, 0))
    return call(
        functools.partial(attend_kernel, tiles=group // TILE),
        (first_len,),
        (heads,),
        [(qkv, block(0)), (qkv, block(heads)), (qkv, block(2 * heads))],
        [
            ((rows, group), F32, block(0)),
            ((rows, group), BF, block(0)),
            ((heads, 1, group), F32, pl.BlockSpec((1, 1, group), lambda h, t: (h, 0, 0))),
        ],
        flops=LONG,
    )


def attend_back_kernel(
    len_ref, q_ref, k_ref, v_ref, g_ref, o_ref, lse_ref, out_ref, dk_acc, dv_acc, *, tiles
):
    first_len = len_ref[0]
    dk_acc[...] = jnp.zeros_like(dk_acc)
    dv_acc[...] = jnp.zeros_like(dv_acc)
    for i, st in tile_variants(tiles):
        q_base = i * TILE
        start = jnp.where(q_base >= first_len, first_len // TILE, 0)

        @pl.when(start == st)
        def _():
            rows = pl.ds(q_base, TILE)
            keys = pl.ds(st * TILE, (i + 1 - st) * TILE)
            q = q_ref[:, rows] * jnp.asarray(0.125, BF)
            k = k_ref[:, keys]
            v = v_ref[:, keys]
            g = g_ref[:, rows]
            delta = jnp.sum(g.astype(F32) * o_ref[:, rows], axis=0, keepdims=True)
            ok = allowed_mask(first_len, q_base, st * TILE, (i + 1 - st) * TILE)
            s = dot_tn(k, q)
            soft = jnp.exp(jnp.where(ok, s, -1000000000.0) - lse_ref[0, :, rows])
            dp = dot_tn(v, g)
            ds = (soft * (dp - delta)).astype(BF)
            dv_acc[:, keys] += dot_nt(g, soft.astype(BF))
            dk_acc[:, keys] += dot_nt(q, ds)
            out_ref[0, :, rows] = (dot_nn(k, ds) * 0.125).astype(BF)

    out_ref[1] = dk_acc[...].astype(BF)
    out_ref[2] = dv_acc[...].astype(BF)


def attend_back(first_len, qkv, g, o, lse, heads):
    group = qkv.shape[1]
    rows = heads * 64
    block = lambda off: pl.BlockSpec((64, group), lambda h, t, off=off: (off + h, 0))
    return call(
        functools.partial(attend_back_kernel, tiles=group // TILE),
        (first_len,),
        (heads,),
        [
            (qkv, block(0)),
            (qkv, block(heads)),
            (qkv, block(2 * heads)),
            (g, block(0)),
            (o, block(0)),
            (lse, pl.BlockSpec((1, 1, group), lambda h, t: (h, 0, 0))),
        ],
        [((3, rows, group), BF, pl.BlockSpec((3, 64, group), lambda h, t: (0, h, 0)))],
        [pltpu.VMEM((64, group), F32), pltpu.VMEM((64, group), F32)],
        flops=LONG,
    )[0]


def join_kernel(pos_ref, x_ref, out):
    rows = out.shape[0]
    per = x_ref.shape[1] // BLK
    for j in range(out.shape[1] // BLK):
        at = pl.multiple_of(pos_ref[j] * BLK, BLK)
        chunk = (j // per) * rows
        out[:, pl.ds(at, BLK)] = x_ref[chunk : chunk + rows, (j % per) * BLK : (j % per + 1) * BLK]


def join_blocks(pos, x, count):
    rows, tok = x.shape[0] // count, x.shape[1]
    shape = (rows, count * tok)
    return call(join_kernel, (pos,), (1,), [(x, whole(x))], [(shape, x.dtype, fixed(shape))])[0]


def split_kernel(tab_ref, x_ref, out_ref, *, per):
    rows = x_ref.shape[0]
    store_slots(out_ref, slot_places(tab_ref, rows, per), pl.ds(0, rows), x_ref[...])


def split_call(tab, x, shards):
    width, group = x.shape
    tok = group // shards
    shape = (shards * width, tok)
    return call(
        functools.partial(split_kernel, per=tok // BLK),
        (tab,),
        (group // TILE,),
        [(x, tokens(width))],
        [(shape, BF, fixed(shape))],
    )[0]


def split_sums_kernel(tab_ref, e_ref, xb_ref, out_ref, gain_ref, shift_ref, gain_acc, shift_acc, *, per):
    clear_first(gain_acc, shift_acc)
    rows = e_ref.shape[0]
    places = slot_places(tab_ref, rows, per)

    def finish(at, carry):
        e = e_ref[at, :]
        ex = e * xb_ref[at, :].astype(F32)
        gain_acc[at, :] += ex[:, :BLK] + ex[:, BLK:]
        shift_acc[at, :] += e[:, :BLK] + e[:, BLK:]
        store_slots(out_ref, places, at, e)
        return carry

    sweep(rows, finish, 0)

    @pl.when(pl.program_id(0) == pl.num_programs(0) - 1)
    def _():
        gain_ref[...] = jnp.sum(gain_acc[...], axis=1, keepdims=True)
        shift_ref[...] = jnp.sum(shift_acc[...], axis=1, keepdims=True)


def split_sums_call(tab, e, x, shards):
    width, group = e.shape
    tok = group // shards
    shape = (shards * width, tok)
    return call(
        functools.partial(split_sums_kernel, per=tok // BLK),
        (tab,),
        (group // TILE,),
        [(e, tokens(width)), (x, tokens(width))],
        [(shape, BF, fixed(shape))] + [((width, 1), F32, fixed((width, 1)))] * 2,
        [pltpu.VMEM((width, BLK), F32), pltpu.VMEM((width, BLK), F32)],
    )


def first_back_kernel(
    tab_ref, g_ref, h0_ref, h1_ref, w_ref, ea_ref, gain_ref, shift_ref, gain_acc, shift_acc, e_ref, *, per
):
    clear_first(gain_acc, shift_acc)
    rows = w_ref.shape[0]
    e_ref[...] = dot_nn(w_ref[...], g_ref[...])
    places = slot_places(tab_ref, rows, per)
    loads = [lambda at, ref=ref: ref[at, :].astype(F32) for ref in (h0_ref, h1_ref)]
    stats = [norm_stats(load, rows, BLK) for load in loads]

    def finish(at, carry):
        e = e_ref[at, :]
        store_slots(ea_ref, places, at, e)
        total = jnp.zeros((at.size, BLK), F32)
        for j, (load, (mean, rstd)) in enumerate(zip(loads, stats)):
            total = total + e[:, j * BLK : (j + 1) * BLK] * ((load(at) - mean) * rstd)
        gain_acc[at, :] += total
        shift_acc[at, :] += e[:, :BLK] + e[:, BLK:]
        return carry

    sweep(rows, finish, 0)

    @pl.when(pl.program_id(0) == pl.num_programs(0) - 1)
    def _():
        gain_ref[...] = jnp.sum(gain_acc[...], axis=1, keepdims=True)
        shift_ref[...] = jnp.sum(shift_acc[...], axis=1, keepdims=True)


def first_back_call(tab, g_mixed, hidden_all, w, shards):
    width = w.shape[0]
    inner, group = g_mixed.shape
    tok = group // shards
    per = tok // BLK
    return call(
        functools.partial(first_back_kernel, per=per),
        (tab,),
        (group // TILE,),
        [
            (g_mixed, tokens(inner)),
            (hidden_all, slot_block(width, per, 0)),
            (hidden_all, slot_block(width, per, 1)),
            (w, whole(w)),
        ],
        [
            ((shards * width, tok), BF, fixed((shards * width, tok))),
            ((width, 1), F32, fixed((width, 1))),
            ((width, 1), F32, fixed((width, 1))),
        ],
        [pltpu.VMEM((width, BLK), F32), pltpu.VMEM((width, BLK), F32), pltpu.VMEM((width, TILE), F32)],
        flops=LONG,
    )


def branch_kernel(
    eb_ref, mid_ref, cot_ref, small_ref, w_ref, mg_ref, gb_ref, send_ref, bias_ref, att_ref, *, cuts
):
    rows, tok = mid_ref.shape

    def write(at, value):
        grad = cot_ref[at, :].astype(F32) + value
        mg_ref[at, :] = grad
        low = grad.astype(BF)
        gb_ref[at, :] = low
        bias_ref[at, :] = jnp.sum(low.astype(F32), axis=1, keepdims=True)

    norm_back(
        lambda at: mid_ref[at, :], lambda at: eb_ref[at, :].astype(F32), small_ref, 5, rows, tok, write
    )
    att_ref[...] = dot_nn(w_ref[...], gb_ref[...]).astype(BF)
    send_ref[...] = jnp.zeros_like(send_ref)
    for to, lo, hi in cuts:
        send_ref[to : to + hi - lo, :] = att_ref[lo:hi, :]


def branch_call(e_b_own, middle_own, cot_own, small, w_out, cuts, send_rows):
    width, tok = middle_own.shape
    return call(
        functools.partial(branch_kernel, cuts=cuts),
        (),
        (1,),
        [(x, whole(x)) for x in (e_b_own, middle_own, cot_own, small, w_out)],
        [
            (shape, dtype, fixed(shape))
            for shape, dtype in (
                ((width, tok), F32),
                ((width, tok), BF),
                ((send_rows, tok), BF),
                ((width, 1), F32),
            )
        ],
        [pltpu.VMEM((w_out.shape[0], tok), BF)],
    )


def input_kernel(ea_ref, h_ref, mg_ref, small_ref, out_ref):
    def write(at, value):
        out_ref[at, :] = mg_ref[at, :] + value

    rows, tok = mg_ref.shape
    norm_back(
        lambda at: h_ref[at, :].astype(F32),
        lambda at: ea_ref[at, :].astype(F32),
        small_ref,
        0,
        rows,
        tok,
        write,
    )


def input_call(e_a_own, hidden_own, middle_grad, small):
    shape = middle_grad.shape
    return call(
        input_kernel,
        (),
        (1,),
        [(x, whole(x)) for x in (e_a_own, hidden_own, middle_grad, small)],
        [(shape, F32, fixed(shape))],
    )[0]


def half_of(acc_ref, bit, count):
    return acc_ref[pl.ds(pl.multiple_of(bit * count, 8), count), :].astype(BF)


def grad_kernel(core_ref, a_ref, b_ref, small_ref, keep_ref, *refs):
    sends, acc_ref = refs[:-1], refs[-1]
    rows = a_ref.shape[0]
    count = keep_ref.shape[1]
    extra = acc_ref.shape[0] - rows - SMALL_ROWS
    acc_ref[0:rows, :] = dot_nt(a_ref[...], b_ref[...])
    acc_ref[rows : rows + SMALL_ROWS, :] = small_ref[0]
    acc_ref[rows + SMALL_ROWS :, :] = jnp.zeros((extra, acc_ref.shape[1]), F32)
    keep_ref[0] = half_of(acc_ref, core_ref[0], count)
    for n, send_ref in enumerate(sends):

        @pl.when(pl.program_id(0) == n)
        def _(send_ref=send_ref):
            send_ref[...] = half_of(acc_ref, 1 - core_ref[0], count)


def grad_call(core, a, b, small, half, flops):
    lead, _, cols = small.shape
    rows, group = a.shape[0] // lead, a.shape[1]
    keep = ((lead, half, cols), BF, pl.BlockSpec((1, half, cols), lambda i, *_: (i, 0, 0)))
    outs = call(
        grad_kernel,
        (core,),
        (lead,),
        [
            (a, pl.BlockSpec((rows, group), lambda i, *_: (i, 0))),
            (b, whole(b)),
            (small, pl.BlockSpec((1, SMALL_ROWS, cols), lambda i, *_: (i, 0, 0))),
        ],
        [keep] + [((half, cols), BF, fixed((half, cols)))] * lead,
        [pltpu.VMEM((2 * half, cols), F32)],
        flops,
    )
    return outs[0], outs[1:]


def first_step_kernel(bit_ref, *refs, leads):
    ins, (keep_ref, send_ref, acc_ref) = refs[:-3], refs[-3:]
    count = keep_ref.shape[1]
    first = at = 0
    for lead in leads:
        for n in range(lead):

            @pl.when(pl.program_id(0) == first + n)
            def _(x_ref=ins[at], y_ref=ins[at + 1 + n]):
                acc_ref[...] = x_ref[0].astype(F32) + y_ref[...].astype(F32)

        first += lead
        at += 1 + lead
    keep_ref[0] = half_of(acc_ref, bit_ref[0], count)
    send_ref[0] = half_of(acc_ref, 1 - bit_ref[0], count)


def first_step_call(bit, sums):
    _, count, cols = sums[0][0].shape
    leads = [x.shape[0] for x, _ in sums]
    total = sum(leads)
    ins = []
    first = 0
    for (x, pieces), lead in zip(sums, leads):
        at = lambda i, *_, first=first, lead=lead: (jnp.clip(i - first, 0, lead - 1), 0, 0)
        ins.append((x, pl.BlockSpec((1, count, cols), at)))
        ins += [(y, whole(y)) for y in pieces]
        first += lead
    part = ((total, count // 2, cols), BF, pl.BlockSpec((1, count // 2, cols), lambda i, *_: (i, 0, 0)))
    return call(
        functools.partial(first_step_kernel, leads=leads),
        (bit,),
        (total,),
        ins,
        [part, part],
        [pltpu.VMEM((count, cols), F32)],
    )


def wide_step_kernel(bit_ref, *refs, lead, wide):
    ins, (keep_ref, send_ref, acc_ref) = refs[:-3], refs[-3:]
    count = keep_ref.shape[1]
    end = 0
    for x_at, lo, hi in wide:
        if lo > end:
            acc_ref[:, end:lo] = jnp.zeros((acc_ref.shape[0], lo - end), F32)
        end = hi
        for n in range(lead):

            @pl.when(pl.program_id(0) == n)
            def _(x_ref=ins[x_at], y_ref=ins[x_at + 1 + n], lo=lo, hi=hi):
                acc_ref[:, lo:hi] = x_ref[0].astype(F32) + y_ref[...].astype(F32)

    keep_ref[0] = half_of(acc_ref, bit_ref[0], count)
    send_ref[0] = half_of(acc_ref, 1 - bit_ref[0], count)


def wide_step_call(bit, sums, offsets, cols):
    lead, count, _ = sums[0][0].shape
    ins, wide = [], []
    for (x, pieces), lo in zip(sums, offsets):
        wide.append((len(ins), lo, lo + x.shape[2]))
        ins.append((x, pl.BlockSpec((1, count, x.shape[2]), lambda i, *_: (i, 0, 0))))
        ins += [(y, whole(y)) for y in pieces]
    part = ((lead, count // 2, cols), BF, pl.BlockSpec((1, count // 2, cols), lambda i, *_: (i, 0, 0)))
    return call(
        functools.partial(wide_step_kernel, lead=lead, wide=wide),
        (bit,),
        (lead,),
        ins,
        [part, part],
        [pltpu.VMEM((count, cols), F32)],
        flops=SHORT,
    )


def step_kernel(bit_ref, x_ref, y_ref, keep_ref, send_ref, acc_ref):
    count = keep_ref.shape[1]
    acc_ref[...] = x_ref[0].astype(F32) + y_ref[0].astype(F32)
    keep_ref[0] = half_of(acc_ref, bit_ref[0], count)
    send_ref[0] = half_of(acc_ref, 1 - bit_ref[0], count)


def step_call(bit, x, y, flops):
    lead, count, cols = x.shape
    block = pl.BlockSpec((1, count, cols), lambda i, *_: (i, 0, 0))
    part = ((lead, count // 2, cols), BF, pl.BlockSpec((1, count // 2, cols), lambda i, *_: (i, 0, 0)))
    return call(
        step_kernel, (bit,), (lead,), [(x, block), (y, block)], [part, part], [pltpu.VMEM((count, cols), F32)], flops
    )


def place_kernel(at_ref, mine_ref, theirs_ref, *refs, spans):
    outs, acc_ref = refs[:-1], refs[-1]
    pieces, _, count, _ = mine_ref.shape
    rows = outs[0].shape[1]
    for n in range(2 * pieces):
        at = pl.multiple_of(at_ref[n], 8)
        acc_ref[pl.ds(at, count), :] = (theirs_ref if n >= pieces else mine_ref)[n % pieces, 0].astype(F32)
    for n, (lo, hi) in enumerate(spans):
        outs[2 * n][0] = acc_ref[0:rows, lo:hi]
        outs[2 * n + 1][0] = acc_ref[rows : rows + SMALL_ROWS, lo:hi]


def place_call(places, mine, theirs, rows, spans):
    pieces, lead, count, cols = mine.shape
    cut = 1280 if cols % 1280 == 0 and len(spans) == 1 else cols
    block = pl.BlockSpec((pieces, 1, count, cut), lambda i, j, *_: (0, i, 0, j))
    outs = []
    for lo, hi in spans:
        lanes = min(hi - lo, cut)
        for height in (rows, SMALL_ROWS):
            spec = pl.BlockSpec((1, height, lanes), lambda i, j, *_: (i, 0, j))
            outs.append(((lead, height, hi - lo), F32, spec))
    inner = [(0, cut)] if len(spans) == 1 else spans
    return call(
        functools.partial(place_kernel, spans=inner),
        (places,),
        (lead, cols // cut),
        [(mine, block), (theirs, block)],
        outs,
        [pltpu.VMEM((2 * pieces * count, cut), F32)],
        flops=SHORT,
    )


ROOT = 0.7978845608028654
CUBE = 0.044715


def gelu(u):
    return 0.5 * u * (1.0 + jnp.tanh(ROOT * (u + CUBE * u * u * u)))


def gelu_slope(u):
    bend = jnp.tanh(ROOT * (u + CUBE * u * u * u))
    return 0.5 * (1.0 + bend) + 0.5 * u * (1.0 - bend * bend) * (ROOT * (1.0 + 3.0 * CUBE * u * u))


def token_sum(values_in):
    return jnp.sum(values_in.astype(F32), axis=1)


def after(x, *first):
    return lax.optimization_barrier((x,) + first)[0]


def together(*values):
    return lax.optimization_barrier(values)


def per_device(
    chips,
    shards,
    hidden_in,
    cotangent,
    slot_index,
    seq_lengths,
    attn_gain,
    attn_shift,
    attn_weight,
    query_bias,
    value_bias,
    out_weight,
    out_bias,
    mlp_gain,
    mlp_shift,
    up_weight,
    up_bias,
    down_weight,
    down_bias,
):
    tok, width = hidden_in.shape
    group = slot_index.shape[0]
    head = width // H
    rows = width // shards
    ff_own = down_weight.shape[0]
    counts, starts, windows, win = head_plan(shards)
    wc = win * head
    reps = 2 * chips
    piece = -(-(rows + SMALL_ROWS) // (8 * reps)) * 8
    half = chips * piece
    me = lax.axis_index("shard")
    chip = lax.axis_index("chip")
    core = lax.axis_index("core")
    blocks = group // BLK
    own_blocks = tok // BLK
    spans = []
    for s in range(shards):
        lo = (starts[s] - windows[s]) * head
        spans.append((s * wc + lo, s * wc + lo + counts[s] * head))

    def to_next(x, t):
        return lax.ppermute(x, "shard", [(i, (i + t) % shards) for i in range(shards)])

    def other_core(x):
        return lax.ppermute(x, "core", [(0, 1), (1, 0)])

    def pick(x, at):
        return lax.dynamic_index_in_dim(x, at, 0, keepdims=False)

    def turn(j):
        return lax.rem(j + 2 * shards, shards)

    def exchange(send):
        got = [pick(send, me)]
        for t in range(1, shards):
            got.append(to_next(pick(send, turn(me + t)), t))
        got = jnp.stack(got)
        return jnp.stack([pick(got, turn(me - j)) for j in range(shards)])

    def over_shard(x):
        return lax.all_gather(x, "shard", axis=0, tiled=True)

    def window(x, s):
        return x[..., windows[s] * head : windows[s] * head + wc]

    def scalar(x):
        return jnp.reshape(x, (1,)).astype(jnp.int32)

    square = chips == 4
    bits = (chip // 2, chip % 2)
    first_bit = jnp.where(core == 0, bits[1], bits[0])
    second_bit = jnp.where(core == 0, bits[0], bits[1])
    slot = 2 * first_bit + second_bit if square else chip
    other_slot = 2 * second_bit + first_bit

    def flip(x, step):
        pairs = []
        for q in range(chips):
            for c in range(2):
                partner = q ^ 1 if (c + step) % 2 == 0 else q ^ 2
                pairs.append((2 * q + c, 2 * partner + c))
        return lax.ppermute(x, ("chip", "core"), pairs)

    def add_low(x, y):
        return (x.astype(F32) + y.astype(F32)).astype(BF)

    def sum_start(a, b, small, *first, flops=1024):
        keep, sends = grad_call(after(scalar(core), *first), a, b, small, half, flops)
        return keep, [other_core(x) for x in sends]

    def chip_sum(state):
        x = add_low(state[0], jnp.stack(state[1]))
        x = jnp.swapaxes(x.reshape(x.shape[0], chips, piece, x.shape[2]), 0, 1)
        return lax.psum_scatter(x, "chip", scatter_dimension=0, tiled=False)

    def sum_second(state, *first, flops=1024):
        if not square:
            return state
        keep, send = step_call(after(scalar(second_bit), *first), *state, flops)
        return keep, flip(send, 1)

    def sum_last(state):
        return add_low(*state) if square else state[0]

    def spread_near(x):
        return jnp.stack([x, flip(x, 1)]) if square else x

    def spread_far(x):
        if not square:
            return lax.all_gather(x, "chip", axis=0, tiled=False)
        return jnp.concatenate([x, flip(x, 0)], axis=0)

    def spread_last(mine, spans, *first):
        places = []
        for c, at in ((core, slot), (1 - core, other_slot)):
            for j in range(chips):
                places.append(c * half + ((at ^ j) if square else j) * piece)
        places = after(jnp.stack(places).astype(jnp.int32), *first)
        return place_call(places, mine, other_core(mine), rows, spans)

    def in_order(bit, x, y):
        return jnp.concatenate([jnp.where(bit == 0, x, y), jnp.where(bit == 0, y, x)], axis=1)

    def my_piece(x):
        x = jnp.pad(x, ((0, 2 * half - x.shape[0]), (0, 0)))
        return lax.dynamic_slice_in_dim(x, core * half + slot * piece, piece, 0)

    def weight_near(x):
        return in_order(second_bit, x, flip(x, 1)) if square else x

    def weight_far(x, *first):
        if not square:
            x = jnp.swapaxes(lax.all_gather(x, "chip", axis=0, tiled=False), 0, 1)
            return x.reshape(x.shape[0], -1, x.shape[-1])
        return in_order(first_bit, after(x, *first) if first else x, flip(x, 0))

    def weight_rows(x):
        x = in_order(core, x, other_core(x))
        return x[:, :rows].reshape(shards * rows, x.shape[-1])

    def small_block(vectors, cols):
        x = jnp.stack(vectors).reshape(len(vectors), shards, rows)
        pad = ((0, 0), (0, SMALL_ROWS - len(vectors)), (0, cols - rows))
        return jnp.pad(jnp.swapaxes(x, 0, 1), pad)

    def with_sum(x, got):
        total = jnp.sum(got[:, :, :rows].astype(F32), axis=0).astype(BF)
        total = jnp.pad(total, ((0, 0), (0, x.shape[1] - rows)))
        row = core * half + slot * piece + lax.broadcasted_iota(jnp.int32, (piece, 1), 0)
        return jnp.where(row >= rows, total, x)[None]

    pos = (slot_index.reshape(blocks, BLK)[:, 0] // BLK).astype(jnp.int32)
    ids = jnp.arange(blocks, dtype=jnp.int32)
    tab = jnp.sum(jnp.where(pos[None, :] == ids[:, None], ids[None, :], 0), axis=1).astype(jnp.int32)
    first_len = seq_lengths[0, :1]

    hidden_own = hidden_in.T
    cot_own = cotangent.T
    small = jnp.stack(
        [attn_gain, attn_shift, query_bias, value_bias, out_bias, mlp_gain, mlp_shift, down_bias]
    )
    small = jnp.pad(small, ((0, 0), (0, 3 * wc - rows)))
    attn_piece = my_piece(attn_weight)
    parts = []
    for s in range(shards):
        cut = [window(attn_piece[:, j * width : (j + 1) * width], s) for j in range(3)]
        parts.append(jnp.concatenate([jnp.concatenate(cut, axis=1), small], axis=0))
    attn_got = exchange(jnp.stack(parts))
    small = jnp.swapaxes(attn_got[:, piece:, :rows], 0, 1).reshape(SMALL_ROWS, width)
    small = small.astype(F32).T
    hidden_all = over_shard(hidden_own)
    attn_near = after(weight_near(attn_got[:, :piece]), hidden_all)
    attn_far = weight_far(attn_near)
    normed_a, hidden = first_norm_call(tab, hidden_all, small, shards)
    w_qkv = weight_rows(after(attn_far, normed_a))
    out_piece = after(my_piece(out_weight), hidden_all)
    out_got = exchange(jnp.stack([out_piece] * shards))
    out_near = weight_near(after(out_got, attn_far))
    up_piece = after(my_piece(up_weight), out_got)
    up_got = exchange(jnp.stack([up_piece[:, s * ff_own : (s + 1) * ff_own] for s in range(shards)]))

    bias_rows = jnp.stack(
        [
            jnp.concatenate(
                [window(small[:, 2], s), jnp.zeros((wc,), F32), window(small[:, 3], s)]
            )
            for s in range(shards)
        ]
    )
    bias_qkv = after(pick(bias_rows, me)[:, None], up_got)
    qkv = (dot_tn(w_qkv, normed_a) + bias_qkv).astype(BF)
    w_out = weight_rows(weight_far(out_near, qkv))
    attended, attended_low, lse = attend(after(first_len, w_out), qkv, win)
    att_all = over_shard(attended_low)
    up_near = weight_near(after(up_got, attended_low))
    w_up = weight_rows(weight_far(after(up_near, att_all)))

    cot_all = over_shard(after(cot_own, att_all))
    att_full = jnp.concatenate([att_all[lo:hi] for lo, hi in spans], axis=0)
    middle = hidden.astype(F32) + dot_tn(w_out, att_full) + small[:, 4:5]
    average = jnp.mean(middle, axis=0, keepdims=True)
    centred = middle - average
    variance = jnp.mean(centred * centred, axis=0, keepdims=True)
    x_b = centred * lax.rsqrt(variance + EPSILON)
    normed_b = (x_b * small[:, 5:6] + small[:, 6:7]).astype(BF)
    x_b = x_b.astype(BF)

    def own_tokens(x):
        parts = [
            lax.dynamic_slice_in_dim(x, pos[me * own_blocks + j] * BLK, BLK, 1)
            for j in range(own_blocks)
        ]
        return jnp.concatenate(parts, axis=1)

    pre = dot_tn(w_up, normed_b) + up_bias.astype(F32)[:, None]
    act = gelu(pre).astype(BF)
    ffn_part = split_call(tab, dot_tn(down_weight, act).astype(BF), shards)
    ffn_chunks = ffn_part.reshape(shards, width, tok)

    def ffn_send(t, part, *first):
        return to_next(after(pick(ffn_chunks, turn(me + t))[part], *first), t)

    ffn_own = pick(ffn_chunks, me).astype(F32)
    ffn_near = ffn_send(1, slice(None))
    cot = join_blocks(after(pos, ffn_part), cot_all, shards)
    g_pre = (dot_nn(down_weight, cot) * gelu_slope(pre)).astype(BF)
    e_b = dot_nn(w_up, g_pre) + after(jnp.zeros((), F32), ffn_near)
    e_b, g_mlp_gain, g_mlp_shift = split_sums_call(tab, e_b, x_b, shards)
    ffn_own = ffn_own + ffn_near.astype(F32)
    middle_own = own_tokens(after(middle, e_b))
    g_up_bias = token_sum(after(g_pre, e_b))[:, None]

    def token_scatter(x):
        return lax.psum_scatter(x, "shard", scatter_dimension=0, tiled=True)

    e_b_own = token_scatter(e_b)
    lead = ff_own // rows
    small_down = jnp.pad(
        g_up_bias[:, 0][None, None], ((0, lead - 1), (0, SMALL_ROWS - 1), (0, width - ff_own))
    )
    down_sum = sum_start(act, cot, small_down, e_b)
    small_up = small_block([g_mlp_gain[:, 0], g_mlp_shift[:, 0], token_sum(cot_own)], ff_own)
    up_sum = sum_start(normed_b, g_pre, small_up, down_sum[0])
    merged = square and ff_own == width
    if merged:
        keep, send = first_step_call(scalar(first_bit), [down_sum, up_sum])
        ffn_sum = (keep, flip(send, 0))
    else:
        ffn_sum = (chip_sum(down_sum), chip_sum(up_sum))
    e_b_own, keep = together(e_b_own, ffn_sum[0])
    ffn_sum = (keep,) + ffn_sum[1:]

    cuts = [(lo, lo - s * wc + windows[s] * head, hi - s * wc + windows[s] * head) for s, (lo, hi) in enumerate(spans)]
    middle_grad, g_branch, sends, g_out_bias = branch_call(
        e_b_own, middle_own, cot_own, small, w_out, cuts, shards * wc
    )
    g_att = exchange(sends.reshape(shards, wc, tok)).reshape(shards * wc, tok)
    att_own = own_tokens(att_full)
    if merged:
        ffn_sum = sum_second(ffn_sum, sends)
    out_sum = sum_start(att_own, g_branch, small_block([g_out_bias[:, 0]], width), ffn_sum[0])
    keep_out = out_sum[0]
    ffn_back = ffn_send(shards - 1, slice(None), g_att)
    g_att = join_blocks(pos, g_att, shards)
    g_mixed = attend_back(first_len, qkv, g_att, attended, lse, win)
    g_mixed_rows = g_mixed.reshape(3 * wc, group)

    e_a, g_attn_gain, g_attn_shift = first_back_call(
        after(tab, keep_out, ffn_back), g_mixed_rows, hidden_all, w_qkv, shards
    )
    e_a_own = token_scatter(e_a)
    ffn_own = ffn_own + ffn_back.astype(F32)
    if merged:
        ffn_last = after(sum_last(ffn_sum), e_a)
        down_own, up_own = ffn_last[:lead], ffn_last[lead:]
    else:
        down_own, up_own = ffn_sum
    up_got = exchange(up_own)
    down_near = spread_near(down_own)
    up_row = with_sum(jnp.concatenate([up_got[s] for s in range(shards)], axis=-1), up_got)
    up_near = spread_near(up_row)
    cut = width // 2
    ffn_top = [ffn_send(t, slice(0, cut), e_a_own) for t in range(2, shards - 1)]
    ffn_low = [ffn_send(t, slice(cut, None), *ffn_top) for t in range(2, shards - 1)]
    for top, low in zip(ffn_top, ffn_low):
        ffn_own = ffn_own + jnp.concatenate([top, low], axis=0).astype(F32)

    def place(x):
        outs = [
            jnp.pad(x, (windows[s] * head, width - windows[s] * head - wc)) for s in range(shards)
        ]
        return pick(jnp.stack(outs), me)

    sums = jnp.sum(g_mixed.astype(F32), axis=2)
    small_mix = small_block(
        [g_attn_gain[:, 0], g_attn_shift[:, 0], place(sums[0]), place(sums[2])], 3 * wc
    )
    mix_sum = sum_start(normed_a, g_mixed_rows, small_mix)
    down_mine = spread_far(down_near)

    skip = -(-width // BLK) * BLK
    if square:
        keep, send = wide_step_call(
            after(scalar(first_bit), down_near), [(keep_out, out_sum[1]), mix_sum], (0, skip), skip + 3 * wc
        )
        g_down_full, down_small = spread_last(down_mine, [(0, width)], keep)
        wide_sum = sum_second((keep, flip(send, 0)), g_down_full, up_near, *ffn_top, flops=SHORT)
        wide_own = sum_last(wide_sum)
    else:
        gap = jnp.zeros((shards, piece, skip - width), BF)
        wide_own = jnp.concatenate([chip_sum((keep_out, out_sum[1])), gap, chip_sum(mix_sum)], axis=-1)
        g_down_full, down_small = spread_last(down_mine, [(0, width)])
    wide_own = after(wide_own, e_a_own, *ffn_low)
    wide_got = exchange(wide_own)
    up_mine = spread_far(after(up_near, wide_own))
    g_up_full, up_small = spread_last(up_mine, [(0, shards * ff_own)])
    columns = []
    for j in range(3):
        for s in range(shards):
            lo, hi = skip + j * wc + spans[s][0] - s * wc, skip + j * wc + spans[s][1] - s * wc
            columns.append(wide_got[s, :, lo:hi])
    mix_row = with_sum(jnp.concatenate(columns, axis=-1), wide_got[:, :, skip:])
    out_row = jnp.sum(wide_got[:, :, :skip].astype(F32), axis=0).astype(BF)
    wide_row = jnp.concatenate([out_row[None], mix_row], axis=-1)
    wide_near = after(spread_near(wide_row), g_up_full)
    g_out_full, out_small, g_mix_full, mix_small = spread_last(
        spread_far(wide_near), [(0, width), (skip, skip + 3 * width)]
    )

    block_out = (middle_own + ffn_own + small[:, 7:8]).astype(BF).T
    input_grad = input_call(e_a_own, hidden_own, middle_grad, small).T

    return (
        block_out,
        input_grad,
        mix_small[0, 0, :rows],
        mix_small[0, 1, :rows],
        g_mix_full[0],
        mix_small[0, 2, :rows],
        mix_small[0, 3, :rows],
        g_out_full[0],
        out_small[0, 0, :rows],
        up_small[0, 0, :rows],
        up_small[0, 1, :rows],
        g_up_full[0],
        down_small[0, 0, :ff_own],
        g_down_full.reshape(ff_own, width),
        up_small[0, 2, :rows],
    )


def solution(mesh):
    reps, shards = mesh.shape["rep"], mesh.shape["shard"]
    fine = Mesh(mesh.devices.reshape(reps // 2, 2, shards), ("chip", "core", "shard"))
    rep = ("chip", "core")
    both = ("chip", "core", "shard")
    return jax.shard_map(
        functools.partial(per_device, reps // 2, shards),
        mesh=fine,
        in_specs=(
            P(both, None),
            P(both, None),
            P(rep),
            P(rep, None),
            P("shard"),
            P("shard"),
            P("shard", None),
            P("shard"),
            P("shard"),
            P("shard", None),
            P("shard"),
            P("shard"),
            P("shard"),
            P("shard", None),
            P("shard"),
            P("shard", None),
            P("shard"),
        ),
        out_specs=(
            P(both, None),
            P(both, None),
            P("shard"),
            P("shard"),
            P("shard", None),
            P("shard"),
            P("shard"),
            P("shard", None),
            P("shard"),
            P("shard"),
            P("shard"),
            P("shard", None),
            P("shard"),
            P("shard", None),
            P("shard"),
        ),
        check_vma=False,
    )
```

time: 2800 us -> 771 us (0.28)
  waiting for transfers between devices: 2350 us -> 328 us
  Pallas kernels: 0 us -> 194 us
  matrix products: 227 us -> 55 us
  blocking collectives: 65.7 us -> 0 us
  starting transfers between devices: 1.63 us -> 56.1 us
    reduce_scatter x6 -> x2, waiting for transfers between devices: 1130 us -> 4.25 us  [token_scatter(): return lax.psum_scatter(x, 'shard', scatter_dimension=0, tiled=True)]
    all_gather x6 -> x3, waiting for transfers between devices: 1090 us -> 82.8 us  [over_shard(): return lax.all_gather(x, 'shard', axis=0, tiled=True)]
    ppermute x0 -> x60, waiting for transfers between devices: none -> 241 us  [the longest x22 118 us: to_next(): lax.ppermute(x, 'shard', [(i, (i + t) % shards) for i in range(shards)])]
    pallas_call x0 -> x21, Pallas kernels: none -> 194 us  [call(): pl.pallas_call(kernel, out_shape=[jax.ShapeDtypeStruct(shape, dtype) for...]
    dot_general x26 -> x6, matrix products: 227 us -> 55 us  [the longest x4 33.5 us: dot_tn(): lax.dot_general(a, b, (((0,), (0,)), ((), ())), preferred_element_type=F32)]
    psum x1 -> x0, waiting for transfers between devices: 126 us -> none  [per_device(): lax.psum(attn_owned[2].astype(jnp.bfloat16), 'rep').astype(jnp.float32)]
    ppermute x0 -> x60, starting transfers between devices: none -> 55.7 us  [the longest x22 26.5 us: to_next(): lax.ppermute(x, 'shard', [(i, (i + t) % shards) for i in range(shards)])]
    unnamed x2 -> x0, blocking collectives: 41.6 us -> none
  transfers between devices with their start and end apart: 13 -> 65, of which waited for: 13 -> 33; matrix products, arithmetic and copies ran while one was open for 7% -> 17% of each run, Pallas kernels for 0% -> 19%
where the time goes in v1:
time: 771 us; the launch traced here: 763 us
  waiting for transfers between devices  328 us (43%)
  Pallas kernels  194 us (25%)
  local copies, waits for them, and re-layouts  65.6 us (9%)
  starting transfers between devices  56.1 us (7%)
  matrix products  55 us (7%)
  other arithmetic  47 us (6%)
  between operations  16.7 us (2%)
    pallas_call x21, Pallas kernels, call(): pl.pallas_call(kernel, out_shape=[jax.ShapeDtypeStruct(shape, dtype) for...  194 us
    ppermute x22, waiting for transfers between devices, to_next(): lax.ppermute(x, 'shard', [(i, (i + t) % shards) for i in range(shards)])  118 us
    ppermute x16, waiting for transfers between devices, flip(): return lax.ppermute(x, ('chip', 'core'), pairs)  109 us
    all_gather x3, waiting for transfers between devices, over_shard(): return lax.all_gather(x, 'shard', axis=0, tiled=True)  82.8 us
    dot_general x4, matrix products, dot_tn(): lax.dot_general(a, b, (((0,), (0,)), ((), ())), preferred_element_type=F32)  33.5 us
    ppermute x22, starting transfers between devices, to_next(): lax.ppermute(x, 'shard', [(i, (i + t) % shards) for i in range(shards)])  26.5 us
    ppermute x16, starting transfers between devices, flip(): return lax.ppermute(x, ('chip', 'core'), pairs)  25.7 us
    dot_general x2, matrix products, dot_nn(): lax.dot_general(a, b, (((1,), (0,)), ((), ())), preferred_element_type=F32)  21.5 us
  transfers between devices with their start and end apart: 65, of which 33 were waited for; matrix products, arithmetic and copies ran while one was open for 17% of the time, Pallas kernels for 19%

profile of v1, /device:TPU:0, one launch (start us, length us, event | category | flops | bytes accessed | tf_op | source)
XLA Modules:
  0.0 762.8 jit_solution(10371909861962309321)
XLA Ops:
  30.7 21.4 %collective-permute-done.1 = bf16[64,1344]{1,0:T(8,128)(2,1)S(1)} collective-permute-done((bf16[64,1344]{1,0:T(8,128)(2,1)S(1)}, bf16[64,1344]{1,0:T(8,128)(2,1)S(1)}, u32[]{:S(2)}, u32[]{:S(2)}) %collective-permute-start.1) | collective-permute-done | bytes 172064 | tf_op jit(solution)/shard_map/ppermute | solution.py:721
  67.0 23.5 %all-gather.4.cloned.1.call-done.h0_ref.h1_ref = bf16[6400,256]{1,0:T(8,128)(2,1)} async-done(((bf16[1600,256]{1,0:T(8,128)(2,1)}), bf16[6400,256]{1,0:T(8,128)(2,1)}) %all-gather.4.cloned.1.call-update) | async-done | bytes 3276816 | tf_op jit(solution)/shard_map/all_gather | solution.py:740
  120.8 13.1 %collective-permute-done.11 = bf16[56,1600]{1,0:T(8,128)(2,1)S(1)} collective-permute-done((bf16[56,1600]{1,0:T(8,128)(2,1)S(1)}, bf16[56,1600]{1,0:T(8,128)(2,1)S(1)}, u32[]{:S(2)}, u32[]{:S(2)}) %collective-permute-start.11) | collective-permute-done | bytes 179232 | tf_op jit(solution)/shard_map/ppermute | solution.py:721
  165.4 19.9 %shard_map.281 = (f32[448,1024]{1,0:T(8,128)}, bf16[448,1024]{1,0:T(8,128)(2,1)}, f32[7,1,1024]{2,1,0:T(1,128)}) custom-call(s32[1]{0:T(128)} %bitcast.252, bf16[1344,1024]{1,0:T(8,128)(2,1)} %add_convert_fusion.1.q_ref.k_ref.v_ref, bf16[1344,1024]{1,0:T(8,128)(2,1)} %add_convert_fusion.1.q_ref.k_ref.v_ref, ...), custom_call_target="tpu_custom_call" | custom-call | flops 20000000000 | bytes 1024 | tf_op jit(solution)/shard_map/pallas_call | solution.py:47
  187.2 9.8 %collective-permute-done.15 = bf16[4,56,1600]{2,1,0:T(8,128)(2,1)S(1)} collective-permute-done((bf16[4,56,1600]{2,1,0:T(8,128)(2,1)S(1)}, bf16[4,56,1600]{2,1,0:T(8,128)(2,1)S(1)}, u32[]{:S(2)}, u32[]{:S(2)}) %collective-permute-start.15) | collective-permute-done | bytes 716832 | tf_op jit(solution)/shard_map/ppermute | solution.py:761
  197.3 59.4 %all-gather.6.cloned.1.call-done = bf16[1792,1024]{1,0:T(8,128)(2,1)} async-done(((bf16[448,1024]{1,0:T(8,128)(2,1)}), bf16[1792,1024]{1,0:T(8,128)(2,1)}) %all-gather.6.cloned.1.call-update) | async-done | bytes 3670032 | tf_op jit(solution)/shard_map/all_gather | solution.py:740
  264.1 12.2 %collective-permute-done.16 = bf16[4,112,1600]{2,1,0:T(8,128)(2,1)} collective-permute-done((bf16[4,112,1600]{2,1,0:T(8,128)(2,1)S(1)}, bf16[4,112,1600]{2,1,0:T(8,128)(2,1)}, u32[]{:S(2)}, u32[]{:S(2)}) %collective-permute-start.16) | collective-permute-done | bytes 1433632 | tf_op jit(solution)/shard_map/ppermute | solution.py:761
  294.1 9.8 %multiply_convert_fusion = (bf16[1600,1024]{1,0:T(8,128)(2,1)S(1)}, f32[1600,1024]{1,0:T(8,128)}) fusion(f32[1600]{0:T(1024)S(1)} %convert_element_type.121, bf16[1600,1600]{1,0:T(8,128)(2,1)S(1)} %bitcast.203, bf16[1600,1024]{1,0:T(8,128)(2,1)S(1)} %get-tuple-element.194.a_ref), kind=kOutput, calls=%fused_computation.11 | convolution fusion | flops 5259264000 | bytes 18233600 | tf_op jit(solution)/shard_map/dot_general | solution.py:26
  305.7 10.3 %fusion.8.x_ref = bf16[1600,1024]{1,0:T(8,128)(2,1)} fusion(bf16[1600,1024]{1,0:T(8,128)(2,1)S(1)} %get-tuple-element.327.a_ref, bf16[1600,1600]{1,0:T(8,128)(2,1)} %param.32), kind=kOutput, calls=%fused_computation.25 | convolution fusion | flops 5244518400 | bytes 11673600 | tf_op jit(solution)/shard_map/dot_general | solution.py:26
  329.5 13.5 %fusion.7.b_ref = bf16[1600,1024]{1,0:T(8,128)(2,1)S(1)} fusion(f32[1600,1024]{1,0:T(8,128)} %get-tuple-element.328, bf16[1600,1600]{1,0:T(8,128)(2,1)} %param.32, bf16[1600,1024]{1,0:T(8,128)(2,1)} %shard_map.283.b_ref, f32[1600]{0:T(1024)S(1)} %convert_element_type.121), kind=kOutput, calls=%fused_computation.9 | convolution fusion | flops 5275648000 | bytes 18233600 | tf_op jit(solution)/shard_map/dot_general | solution.py:30
  364.8 12.1 %shard_map.285 = (bf16[4,224,1600]{2,1,0:T(8,128)(2,1)}, bf16[224,1600]{1,0:T(8,128)(2,1)}, bf16[224,1600]{1,0:T(8,128)(2,1)}, bf16[224,1600]{1,0:T(8,128)(2,1)}, bf16[224,1600]{1,0:T(8,128)(2,1)}) custom-call(s32[1]{0:T(128)} %bitcast.45.core_ref, bf16[1600,1024]{1,0:T(8,128)(2,1)} %copy-done.19, bf16[1600,1024]{1,0:T(8,128)(2,1)} %shard_map.283.b_ref, ...), custom_call_target="tpu_custom_call" | custom-call | flops 1024 | bytes 1024 | tf_op jit(solution)/shard_map/pallas_call | solution.py:47
  378.4 11.9 %shard_map.286 = (bf16[4,224,1600]{2,1,0:T(8,128)(2,1)}, bf16[224,1600]{1,0:T(8,128)(2,1)}, bf16[224,1600]{1,0:T(8,128)(2,1)}, bf16[224,1600]{1,0:T(8,128)(2,1)}, bf16[224,1600]{1,0:T(8,128)(2,1)}) custom-call(s32[1]{0:T(128)} %bitcast.45.core_ref, bf16[1600,1024]{1,0:T(8,128)(2,1)} %copy-done.4, bf16[1600,1024]{1,0:T(8,128)(2,1)} %copy-done.5, ...), custom_call_target="tpu_custom_call" | custom-call | flops 1024 | bytes 1024 | tf_op jit(solution)/shard_map/pallas_call | solution.py:47
  401.1 10.4 %shard_map.287 = (bf16[8,112,1600]{2,1,0:T(8,128)(2,1)}, bf16[8,112,1600]{2,1,0:T(8,128)(2,1)}) custom-call(s32[1]{0:T(128)} %bitcast.44.bit_ref, bf16[4,224,1600]{2,1,0:T(8,128)(2,1)} %get-tuple-element.118.refs_0_, bf16[224,1600]{1,0:T(8,128)(2,1)} %copy-done.40, bf16[224,1600]{1,0:T(8,128)(2,1)} %copy-done.41, bf16[224,1600]{1,0:T(8,128)(2,1)} %copy-done.42, ...), custom_call_target="tpu_custom_call" | custom-call | flops 1024 | bytes 1024 | tf_op jit(solution)/shard_map/pallas_call | solution.py:47
  470.4 19.6 %shard_map.292 = bf16[3,448,1024]{2,1,0:T(8,128)(2,1)} custom-call(s32[1]{0:T(128)} %bitcast.253, bf16[1344,1024]{1,0:T(8,128)(2,1)} %add_convert_fusion.1.q_ref.k_ref.v_ref, bf16[1344,1024]{1,0:T(8,128)(2,1)} %add_convert_fusion.1.q_ref.k_ref.v_ref, bf16[1344,1024]{1,0:T(8,128)(2,1)} %add_convert_fusion.1.q_ref.k_ref.v_ref, ...), custom_call_target="tpu_custom_call" | custom-call | flops 20000000000 | bytes 1024 | tf_op jit(solution)/shard_map/pallas_call | solution.py:47
  492.4 14.1 %shard_map.293 = (bf16[6400,256]{1,0:T(8,128)(2,1)}, f32[1600,1]{1,0:T(8,128)}, f32[1600,1]{1,0:T(8,128)}) custom-call(s32[8]{0:T(128)} %select_reduce_fusion.tab_ref, bf16[1344,1024]{1,0:T(8,128)(2,1)} %bitcast.199, bf16[6400,256]{1,0:T(8,128)(2,1)} %all-gather.4.cloned.1.call-done.h0_ref.h1_ref, ...), custom_call_target="tpu_custom_call" | custom-call | flops 20000000000 | bytes 1024 | tf_op jit(solution)/shard_map/pallas_call | solution.py:47
  515.5 10.5 %shard_map.295 = (bf16[4,224,1344]{2,1,0:T(8,128)(2,1)}, bf16[224,1344]{1,0:T(8,128)(2,1)}, bf16[224,1344]{1,0:T(8,128)(2,1)}, bf16[224,1344]{1,0:T(8,128)(2,1)}, bf16[224,1344]{1,0:T(8,128)(2,1)}) custom-call(s32[1]{0:T(128)} %bitcast.45.core_ref, bf16[1600,1024]{1,0:T(8,128)(2,1)} %get-tuple-element.102.a_ref, bf16[1344,1024]{1,0:T(8,128)(2,1)} %bitcast.200, ...), custom_call_target="tpu_custom_call" | custom-call | flops 1024 | bytes 1024 | tf_op jit(solution)/shard_map/pallas_call | solution.py:47
  527.1 20.6 %collective-permute-done.47 = bf16[56,1600]{1,0:T(8,128)(2,1)S(1)} collective-permute-done((bf16[56,1600]{1,0:T(8,128)(2,1)S(1)}, bf16[56,1600]{1,0:T(8,128)(2,1)S(1)}, u32[]{:S(2)}, u32[]{:S(2)}) %collective-permute-start.47) | collective-permute-done | bytes 179232 | tf_op jit(solution)/shard_map/ppermute | solution.py:721
  549.2 11.9 %collective-permute-done.46 = bf16[56,1600]{1,0:T(8,128)(2,1)S(1)} collective-permute-done((bf16[56,1600]{1,0:T(8,128)(2,1)S(1)}, bf16[56,1600]{1,0:T(8,128)(2,1)S(1)}, u32[]{:S(2)}, u32[]{:S(2)}) %collective-permute-start.46) | collective-permute-done | bytes 179232 | tf_op jit(solution)/shard_map/ppermute | solution.py:721
  590.2 15.7 %collective-permute-done.49 = bf16[1,56,6400]{2,1,0:T(8,128)(2,1)} collective-permute-done((bf16[1,56,6400]{2,1,0:T(8,128)(2,1)}, bf16[1,56,6400]{2,1,0:T(8,128)(2,1)}, u32[]{:S(2)}, u32[]{:S(2)}) %collective-permute-start.49) | collective-permute-done | bytes 716832 | tf_op jit(solution)/shard_map/ppermute | solution.py:761
  617.0 10.4 %collective-permute-done.32 = bf16[800,256]{1,0:T(8,128)(2,1)S(1)} collective-permute-done((bf16[800,256]{1,0:T(8,128)(2,1)}, bf16[800,256]{1,0:T(8,128)(2,1)S(1)}, u32[]{:S(2)}, u32[]{:S(2)}) %collective-permute-start.32) | collective-permute-done | bytes 409632 | tf_op jit(solution)/shard_map/ppermute | solution.py:721
  634.6 16.6 %collective-permute-done.51 = bf16[4,56,3008]{2,1,0:T(8,128)(2,1)} collective-permute-done((bf16[4,56,3008]{2,1,0:T(8,128)(2,1)}, bf16[4,56,3008]{2,1,0:T(8,128)(2,1)}, u32[]{:S(2)}, u32[]{:S(2)}) %collective-permute-start.51) | collective-permute-done | bytes 1347616 | tf_op jit(solution)/shard_map/ppermute | solution.py:761
  666.1 19.2 %collective-permute-done.53 = bf16[56,3008]{1,0:T(8,128)(2,1)S(1)} collective-permute-done((bf16[56,3008]{1,0:T(8,128)(2,1)S(1)}, bf16[56,3008]{1,0:T(8,128)(2,1)S(1)}, u32[]{:S(2)}, u32[]{:S(2)}) %collective-permute-start.53) | collective-permute-done | bytes 336928 | tf_op jit(solution)/shard_map/ppermute | solution.py:721
  695.4 10.0 %collective-permute-done.55 = bf16[1,56,6464]{2,1,0:T(8,128)(2,1)S(1)} collective-permute-done((bf16[1,56,6464]{2,1,0:T(8,128)(2,1)S(1)}, bf16[1,56,6464]{2,1,0:T(8,128)(2,1)S(1)}, u32[]{:S(2)}, u32[]{:S(2)}) %collective-permute-start.55) | collective-permute-done | bytes 724000 | tf_op jit(solution)/shard_map/ppermute | solution.py:761
  715.6 17.6 %collective-permute-done.58 = bf16[2,1,56,6464]{3,2,1,0:T(8,128)(2,1)S(1)} collective-permute-done((bf16[2,1,56,6464]{3,2,1,0:T(8,128)(2,1)S(1)}, bf16[2,1,56,6464]{3,2,1,0:T(8,128)(2,1)S(1)}, u32[]{:S(2)}, u32[]{:S(2)}) %collective-permute-start.58) | collective-permute-done | bytes 1447968 | tf_op jit(solution)/shard_map/ppermute | solution.py:761
  (425 shorter events, 352.7 us)
Async XLA Ops:
  7.2 83.3 %all-gather.4.cloned.1.call-start = ((), (), s32[]{:S(2)}) async-start(), calls=%async_computation.2 | async-start | bytes 4096000 | tf_op jit(solution)/shard_map/all_gather | solution.py:740
  7.9 248.7 %all-gather.6.cloned.1.call-start = ((), (), s32[]{:S(2)}) async-start(), calls=%async_computation.3 | async-start | bytes 4587520 | tf_op jit(solution)/shard_map/all_gather | solution.py:740
  21.9 30.2 %collective-permute-start.1 = (bf16[64,1344]{1,0:T(8,128)(2,1)S(1)}, bf16[64,1344]{1,0:T(8,128)(2,1)S(1)}, u32[]{:S(2)}, u32[]{:S(2)}) collective-permute-start(bf16[64,1344]{1,0:T(8,128)(2,1)S(1)} %get-tuple-element.296), channel_id=1, source_target_pairs={{0,2},{1,3},{2,0},{3,1},{4,6},{5,7},{6,4},{7,5},{8,10},{9,11},{10,... | collective-permute-start | bytes 516104 | tf_op jit(solution)/shard_map/ppermute | solution.py:721
  21.9 30.2 %collective-permute-start = (bf16[64,1344]{1,0:T(8,128)(2,1)S(1)}, bf16[64,1344]{1,0:T(8,128)(2,1)S(1)}, u32[]{:S(2)}, u32[]{:S(2)}) collective-permute-start(bf16[64,1344]{1,0:T(8,128)(2,1)S(1)} %get-tuple-element.297), channel_id=1, source_target_pairs={{0,1},{1,2},{2,3},{3,0},{4,5},{5,6},{6,7},{7,4},{8,9},{9,10},{10,1... | collective-permute-start | bytes 516104 | tf_op jit(solution)/shard_map/ppermute | solution.py:721
  185.3 138.7 %all-gather.8.cloned.1.call-start = ((), (), s32[]{:S(2)}) async-start(), calls=%async_computation.4 | async-start | bytes 4096000 | tf_op jit(solution)/shard_map/all_gather | solution.py:740
  260.0 163.6 %reduce-scatter.3.cloned.1.call-start = ((), (), s32[]{:S(2)}) async-start(), calls=%async_computation.5 | async-start | bytes 4096000 | tf_op jit(solution)/shard_map/reduce_scatter | solution.py:913
  361.9 246.5 %reduce-scatter.5.cloned.1.call-start = ((), (), s32[]{:S(2)}) async-start(), calls=%async_computation.6 | async-start | bytes 4096000 | tf_op jit(solution)/shard_map/reduce_scatter | solution.py:913
  411.5 35.8 %collective-permute-start.31 = (bf16[8,112,1600]{2,1,0:T(8,128)(2,1)}, bf16[8,112,1600]{2,1,0:T(8,128)(2,1)}, u32[]{:S(2)}, u32[]{:S(2)}) collective-permute-start(bf16[8,112,1600]{2,1,0:T(8,128)(2,1)} %get-tuple-element.137), channel_id=1, source_target_pairs={{0,8},{4,20},{8,0},{12,28},{16,24},{20,4},{24,16},{28,12},{1,9},{5... | collective-permute-start | bytes 8601608 | tf_op jit(solution)/shard_map/ppermute | solution.py:761
  433.3 30.6 %collective-permute-start.29 = (bf16[448,256]{1,0:T(8,128)(2,1)}, bf16[448,256]{1,0:T(8,128)(2,1)S(1)}, u32[]{:S(2)}, u32[]{:S(2)}) collective-permute-start(bf16[448,256]{1,0:T(8,128)(2,1)} %get-tuple-element.263), channel_id=1, source_target_pairs={{0,3},{1,0},{2,1},{3,2},{4,7},{5,4},{6,5},{7,6},{8,11},{9,8},{10,9... | collective-permute-start | bytes 688136 | tf_op jit(solution)/shard_map/ppermute | solution.py:721
  435.5 28.9 %collective-permute-start.28 = (bf16[448,256]{1,0:T(8,128)(2,1)}, bf16[448,256]{1,0:T(8,128)(2,1)S(1)}, u32[]{:S(2)}, u32[]{:S(2)}) collective-permute-start(bf16[448,256]{1,0:T(8,128)(2,1)} %get-tuple-element.264), channel_id=1, source_target_pairs={{0,2},{1,3},{2,0},{3,1},{4,6},{5,7},{6,4},{7,5},{8,10},{9,11},{10,... | collective-permute-start | bytes 688136 | tf_op jit(solution)/shard_map/ppermute | solution.py:721
  455.9 50.7 %collective-permute-start.34 = (bf16[8,56,1600]{2,1,0:T(8,128)(2,1)}, bf16[8,56,1600]{2,1,0:T(8,128)(2,1)S(1)}, u32[]{:S(2)}, u32[]{:S(2)}) collective-permute-start(bf16[8,56,1600]{2,1,0:T(8,128)(2,1)} %get-tuple-element.150), channel_id=1, source_target_pairs={{0,16},{4,12},{8,24},{12,4},{16,0},{20,28},{24,8},{28,20},{1,17},{... | collective-permute-start | bytes 4300808 | tf_op jit(solution)/shard_map/ppermute | solution.py:761
  463.9 48.5 %collective-permute-start.36 = (bf16[224,1600]{1,0:T(8,128)(2,1)}, bf16[224,1600]{1,0:T(8,128)(2,1)}, u32[]{:S(2)}, u32[]{:S(2)}) collective-permute-start(bf16[224,1600]{1,0:T(8,128)(2,1)} %get-tuple-element.153), channel_id=1, source_target_pairs={{0,4},{4,0},{1,5},{5,1},{2,6},{6,2},{3,7},{7,3},{8,12},{12,8},{9,1... | collective-permute-start | bytes 2150408 | tf_op jit(solution)/shard_map/ppermute | solution.py:724
  463.9 48.9 %collective-permute-start.37 = (bf16[224,1600]{1,0:T(8,128)(2,1)}, bf16[224,1600]{1,0:T(8,128)(2,1)}, u32[]{:S(2)}, u32[]{:S(2)}) collective-permute-start(bf16[224,1600]{1,0:T(8,128)(2,1)} %get-tuple-element.154), channel_id=1, source_target_pairs={{0,4},{4,0},{1,5},{5,1},{2,6},{6,2},{3,7},{7,3},{8,12},{12,8},{9,1... | collective-permute-start | bytes 2150408 | tf_op jit(solution)/shard_map/ppermute | solution.py:724
  464.4 61.6 %collective-permute-start.38 = (bf16[224,1600]{1,0:T(8,128)(2,1)}, bf16[224,1600]{1,0:T(8,128)(2,1)}, u32[]{:S(2)}, u32[]{:S(2)}) collective-permute-start(bf16[224,1600]{1,0:T(8,128)(2,1)} %get-tuple-element.155), channel_id=1, source_target_pairs={{0,4},{4,0},{1,5},{5,1},{2,6},{6,2},{3,7},{7,3},{8,12},{12,8},{9,1... | collective-permute-start | bytes 2150408 | tf_op jit(solution)/shard_map/ppermute | solution.py:724
  492.2 34.2 %collective-permute-start.39 = (bf16[224,1600]{1,0:T(8,128)(2,1)}, bf16[224,1600]{1,0:T(8,128)(2,1)}, u32[]{:S(2)}, u32[]{:S(2)}) collective-permute-start(bf16[224,1600]{1,0:T(8,128)(2,1)} %get-tuple-element.156), channel_id=1, source_target_pairs={{0,4},{4,0},{1,5},{5,1},{2,6},{6,2},{3,7},{7,3},{8,12},{12,8},{9,1... | collective-permute-start | bytes 2150408 | tf_op jit(solution)/shard_map/ppermute | solution.py:724
  509.3 38.6 %collective-permute-start.35 = (bf16[4,56,1600]{2,1,0:T(8,128)(2,1)}, bf16[4,56,1600]{2,1,0:T(8,128)(2,1)S(1)}, u32[]{:S(2)}, u32[]{:S(2)}) collective-permute-start(bf16[4,56,1600]{2,1,0:T(8,128)(2,1)} %get-tuple-element.231), channel_id=1, source_target_pairs={{0,16},{4,12},{8,24},{12,4},{16,0},{20,28},{24,8},{28,20},{1,17},{... | collective-permute-start | bytes 2150408 | tf_op jit(solution)/shard_map/ppermute | solution.py:761
  512.9 34.9 %collective-permute-start.47 = (bf16[56,1600]{1,0:T(8,128)(2,1)S(1)}, bf16[56,1600]{1,0:T(8,128)(2,1)S(1)}, u32[]{:S(2)}, u32[]{:S(2)}) collective-permute-start(bf16[56,1600]{1,0:T(8,128)(2,1)S(1)} %get-tuple-element.274), channel_id=1, source_target_pairs={{0,2},{1,3},{2,0},{3,1},{4,6},{5,7},{6,4},{7,5},{8,10},{9,11},{10,... | collective-permute-start | bytes 537608 | tf_op jit(solution)/shard_map/ppermute | solution.py:721
  526.0 38.3 %collective-permute-start.40 = (bf16[224,1344]{1,0:T(8,128)(2,1)}, bf16[224,1344]{1,0:T(8,128)(2,1)S(1)}, u32[]{:S(2)}, u32[]{:S(2)}) collective-permute-start(bf16[224,1344]{1,0:T(8,128)(2,1)} %get-tuple-element.160), channel_id=1, source_target_pairs={{0,4},{4,0},{1,5},{5,1},{2,6},{6,2},{3,7},{7,3},{8,12},{12,8},{9,1... | collective-permute-start | bytes 1806344 | tf_op jit(solution)/shard_map/ppermute | solution.py:724
  526.4 38.0 %collective-permute-start.41 = (bf16[224,1344]{1,0:T(8,128)(2,1)}, bf16[224,1344]{1,0:T(8,128)(2,1)S(1)}, u32[]{:S(2)}, u32[]{:S(2)}) collective-permute-start(bf16[224,1344]{1,0:T(8,128)(2,1)} %get-tuple-element.161), channel_id=1, source_target_pairs={{0,4},{4,0},{1,5},{5,1},{2,6},{6,2},{3,7},{7,3},{8,12},{12,8},{9,1... | collective-permute-start | bytes 1806344 | tf_op jit(solution)/shard_map/ppermute | solution.py:724
  526.9 37.5 %collective-permute-start.42 = (bf16[224,1344]{1,0:T(8,128)(2,1)}, bf16[224,1344]{1,0:T(8,128)(2,1)}, u32[]{:S(2)}, u32[]{:S(2)}) collective-permute-start(bf16[224,1344]{1,0:T(8,128)(2,1)} %get-tuple-element.162), channel_id=1, source_target_pairs={{0,4},{4,0},{1,5},{5,1},{2,6},{6,2},{3,7},{7,3},{8,12},{12,8},{9,1... | collective-permute-start | bytes 1806344 | tf_op jit(solution)/shard_map/ppermute | solution.py:724
  573.2 54.2 %collective-permute-start.50 = (bf16[4,112,3008]{2,1,0:T(8,128)(2,1)}, bf16[4,112,3008]{2,1,0:T(8,128)(2,1)}, u32[]{:S(2)}, u32[]{:S(2)}) collective-permute-start(bf16[4,112,3008]{2,1,0:T(8,128)(2,1)} %get-tuple-element.168), channel_id=1, source_target_pairs={{0,8},{4,20},{8,0},{12,28},{16,24},{20,4},{24,16},{28,12},{1,9},{5... | collective-permute-start | bytes 8085512 | tf_op jit(solution)/shard_map/ppermute | solution.py:761
  656.6 28.7 %collective-permute-start.53 = (bf16[56,3008]{1,0:T(8,128)(2,1)S(1)}, bf16[56,3008]{1,0:T(8,128)(2,1)S(1)}, u32[]{:S(2)}, u32[]{:S(2)}) collective-permute-start(bf16[56,3008]{1,0:T(8,128)(2,1)S(1)} %get-tuple-element.254), channel_id=1, source_target_pairs={{0,2},{1,3},{2,0},{3,1},{4,6},{5,7},{6,4},{7,5},{8,10},{9,11},{10,... | collective-permute-start | bytes 1010696 | tf_op jit(solution)/shard_map/ppermute | solution.py:721
  656.7 28.7 %collective-permute-start.52 = (bf16[56,3008]{1,0:T(8,128)(2,1)S(1)}, bf16[56,3008]{1,0:T(8,128)(2,1)S(1)}, u32[]{:S(2)}, u32[]{:S(2)}) collective-permute-start(bf16[56,3008]{1,0:T(8,128)(2,1)S(1)} %get-tuple-element.255), channel_id=1, source_target_pairs={{0,1},{1,2},{2,3},{3,0},{4,5},{5,6},{6,7},{7,4},{8,9},{9,10},{10,1... | collective-permute-start | bytes 1010696 | tf_op jit(solution)/shard_map/ppermute | solution.py:721
  657.3 34.0 %collective-permute-start.56 = (bf16[2,1,56,6400]{3,2,1,0:T(8,128)(2,1)}, bf16[2,1,56,6400]{3,2,1,0:T(8,128)(2,1)}, u32[]{:S(2)}, u32[]{:S(2)}) collective-permute-start(bf16[2,1,56,6400]{3,2,1,0:T(8,128)(2,1)} %pad_maximum_fusion.13), channel_id=1, source_target_pairs={{0,8},{4,20},{8,0},{12,28},{16,24},{20,4},{24,16},{28,12},{1,9},{5... | collective-permute-start | bytes 4300808 | tf_op jit(solution)/shard_map/ppermute | solution.py:761
  (105 other events, 1305.9 us)
Sparse Core Ops, SparseCore 0:
  9.6 80.8 all-gather.3
  185.4 71.1 all-gather.5
  260.1 63.3 all-gather.7
  362.0 61.5 reduce-scatter.2
  506.7 71.3 reduce-scatter.4

commit v2 on v1

--- a/solution.py
+++ b/solution.py
@@ -498,6 +498,9 @@
     acc_ref[rows : rows + SMALL_ROWS, :] = small_ref[0]
     acc_ref[rows + SMALL_ROWS :, :] = jnp.zeros((extra, acc_ref.shape[1]), F32)
     keep_ref[0] = half_of(acc_ref, core_ref[0], count)
+    if len(sends) == 1:
+        sends[0][0] = half_of(acc_ref, 1 - core_ref[0], count)
+        return
     for n, send_ref in enumerate(sends):
 
         @pl.when(pl.program_id(0) == n)
@@ -505,7 +508,7 @@
             send_ref[...] = half_of(acc_ref, 1 - core_ref[0], count)
 
 
-def grad_call(core, a, b, small, half, flops):
+def grad_call(core, a, b, small, half, pieces):
     lead, _, cols = small.shape
     rows, group = a.shape[0] // lead, a.shape[1]
     keep = ((lead, half, cols), BF, pl.BlockSpec((1, half, cols), lambda i, *_: (i, 0, 0)))
@@ -518,11 +521,10 @@
             (b, whole(b)),
             (small, pl.BlockSpec((1, SMALL_ROWS, cols), lambda i, *_: (i, 0, 0))),
         ],
-        [keep] + [((half, cols), BF, fixed((half, cols)))] * lead,
+        [keep] + ([((half, cols), BF, fixed((half, cols)))] * lead if pieces else [keep]),
         [pltpu.VMEM((2 * half, cols), F32)],
-        flops,
-    )
-    return outs[0], outs[1:]
+    )
+    return outs[0], outs[1:] if pieces else outs[1]
 
 
 def first_step_kernel(bit_ref, *refs, leads):
@@ -564,20 +566,15 @@
     )
 
 
-def wide_step_kernel(bit_ref, *refs, lead, wide):
+def wide_step_kernel(bit_ref, *refs, wide):
     ins, (keep_ref, send_ref, acc_ref) = refs[:-3], refs[-3:]
     count = keep_ref.shape[1]
     end = 0
-    for x_at, lo, hi in wide:
+    for n, (lo, hi) in enumerate(wide):
         if lo > end:
             acc_ref[:, end:lo] = jnp.zeros((acc_ref.shape[0], lo - end), F32)
         end = hi
-        for n in range(lead):
-
-            @pl.when(pl.program_id(0) == n)
-            def _(x_ref=ins[x_at], y_ref=ins[x_at + 1 + n], lo=lo, hi=hi):
-                acc_ref[:, lo:hi] = x_ref[0].astype(F32) + y_ref[...].astype(F32)
-
+        acc_ref[:, lo:hi] = ins[2 * n][0].astype(F32) + ins[2 * n + 1][0].astype(F32)
     keep_ref[0] = half_of(acc_ref, bit_ref[0], count)
     send_ref[0] = half_of(acc_ref, 1 - bit_ref[0], count)
 
@@ -585,13 +582,12 @@
 def wide_step_call(bit, sums, offsets, cols):
     lead, count, _ = sums[0][0].shape
     ins, wide = [], []
-    for (x, pieces), lo in zip(sums, offsets):
-        wide.append((len(ins), lo, lo + x.shape[2]))
-        ins.append((x, pl.BlockSpec((1, count, x.shape[2]), lambda i, *_: (i, 0, 0))))
-        ins += [(y, whole(y)) for y in pieces]
+    for (x, y), lo in zip(sums, offsets):
+        wide.append((lo, lo + x.shape[2]))
+        ins += [(z, pl.BlockSpec((1, count, z.shape[2]), lambda i, *_: (i, 0, 0))) for z in (x, y)]
     part = ((lead, count // 2, cols), BF, pl.BlockSpec((1, count // 2, cols), lambda i, *_: (i, 0, 0)))
     return call(
-        functools.partial(wide_step_kernel, lead=lead, wide=wide),
+        functools.partial(wide_step_kernel, wide=wide),
         (bit,),
         (lead,),
         ins,
@@ -763,12 +759,12 @@
     def add_low(x, y):
         return (x.astype(F32) + y.astype(F32)).astype(BF)
 
-    def sum_start(a, b, small, *first, flops=1024):
-        keep, sends = grad_call(after(scalar(core), *first), a, b, small, half, flops)
-        return keep, [other_core(x) for x in sends]
+    def sum_start(a, b, small, *first, pieces=False):
+        keep, sends = grad_call(after(scalar(core), *first), a, b, small, half, pieces)
+        return keep, [other_core(x) for x in sends] if pieces else other_core(sends)
 
     def chip_sum(state):
-        x = add_low(state[0], jnp.stack(state[1]))
+        x = add_low(state[0], jnp.stack(state[1]) if isinstance(state[1], list) else state[1])
         x = jnp.swapaxes(x.reshape(x.shape[0], chips, piece, x.shape[2]), 0, 1)
         return lax.psum_scatter(x, "chip", scatter_dimension=0, tiled=False)
 
@@ -917,9 +913,9 @@
     small_down = jnp.pad(
         g_up_bias[:, 0][None, None], ((0, lead - 1), (0, SMALL_ROWS - 1), (0, width - ff_own))
     )
-    down_sum = sum_start(act, cot, small_down, e_b)
+    down_sum = sum_start(act, cot, small_down, e_b, pieces=True)
     small_up = small_block([g_mlp_gain[:, 0], g_mlp_shift[:, 0], token_sum(cot_own)], ff_own)
-    up_sum = sum_start(normed_b, g_pre, small_up, down_sum[0])
+    up_sum = sum_start(normed_b, g_pre, small_up, down_sum[0], pieces=True)
     merged = square and ff_own == width
     if merged:
         keep, send = first_step_call(scalar(first_bit), [down_sum, up_sum])
@@ -982,16 +978,15 @@
         keep, send = wide_step_call(
             after(scalar(first_bit), down_near), [(keep_out, out_sum[1]), mix_sum], (0, skip), skip + 3 * wc
         )
-        g_down_full, down_small = spread_last(down_mine, [(0, width)], keep)
-        wide_sum = sum_second((keep, flip(send, 0)), g_down_full, up_near, *ffn_top, flops=SHORT)
+        wide_sum = sum_second((keep, flip(send, 0)), up_near, *ffn_top, flops=SHORT)
         wide_own = sum_last(wide_sum)
     else:
         gap = jnp.zeros((shards, piece, skip - width), BF)
         wide_own = jnp.concatenate([chip_sum((keep_out, out_sum[1])), gap, chip_sum(mix_sum)], axis=-1)
-        g_down_full, down_small = spread_last(down_mine, [(0, width)])
     wide_own = after(wide_own, e_a_own, *ffn_low)
     wide_got = exchange(wide_own)
     up_mine = spread_far(after(up_near, wide_own))
+    g_down_full, down_small = spread_last(down_mine, [(0, width)], wide_own)
     g_up_full, up_small = spread_last(up_mine, [(0, shards * ff_own)])
     columns = []
     for j in range(3):
@@ -1001,7 +996,7 @@
     mix_row = with_sum(jnp.concatenate(columns, axis=-1), wide_got[:, :, skip:])
     out_row = jnp.sum(wide_got[:, :, :skip].astype(F32), axis=0).astype(BF)
     wide_row = jnp.concatenate([out_row[None], mix_row], axis=-1)
-    wide_near = after(spread_near(wide_row), g_up_full)
+    wide_near = spread_near(after(wide_row, g_down_full))
     g_out_full, out_small, g_mix_full, mix_small = spread_last(
         spread_far(wide_near), [(0, width), (skip, skip + 3 * width)]
     )

time: 771 us -> 782 us (1.014)
  waiting for transfers between devices: 328 us -> 341 us
  local copies, waits for them, and re-layouts: 65.6 us -> 57.3 us
    ppermute x16, waiting for transfers between devices: 109 us -> 138 us  [flip(): return lax.ppermute(x, ('chip', 'core'), pairs)]
    ppermute x22, waiting for transfers between devices: 118 us -> 100 us  [to_next(): lax.ppermute(x, 'shard', [(i, (i + t) % shards) for i in range(shards)])]
    ppermute x22, starting transfers between devices: 26.5 us -> 34.8 us  [to_next(): lax.ppermute(x, 'shard', [(i, (i + t) % shards) for i in range(shards)])]
    unnamed x130 -> x121, local copies, waits for them, and re-layouts: 19.7 us -> 15.5 us
  transfers between devices with their start and end apart: 65 -> 59, of which waited for: 33 -> 33; matrix products, arithmetic and copies ran while one was open for 17% -> 16% of each run, Pallas kernels for 19% -> 20%
where the time goes in v2:
time: 782 us; the launch traced here: 774 us
  waiting for transfers between devices  341 us (44%)
  Pallas kernels  193 us (25%)
  starting transfers between devices  63.6 us (8%)
  local copies, waits for them, and re-layouts  57.3 us (7%)
  matrix products  52.5 us (7%)
  other arithmetic  49.8 us (6%)
  between operations  16.5 us (2%)
    pallas_call x21, Pallas kernels, call(): pl.pallas_call(kernel, out_shape=[jax.ShapeDtypeStruct(shape, dtype) for...  193 us
    ppermute x16, waiting for transfers between devices, flip(): return lax.ppermute(x, ('chip', 'core'), pairs)  138 us
    ppermute x22, waiting for transfers between devices, to_next(): lax.ppermute(x, 'shard', [(i, (i + t) % shards) for i in range(shards)])  100 us
    all_gather x3, waiting for transfers between devices, over_shard(): return lax.all_gather(x, 'shard', axis=0, tiled=True)  84.7 us
    ppermute x22, starting transfers between devices, to_next(): lax.ppermute(x, 'shard', [(i, (i + t) % shards) for i in range(shards)])  34.8 us
    dot_general x4, matrix products, dot_tn(): lax.dot_general(a, b, (((0,), (0,)), ((), ())), preferred_element_type=F32)  31 us
    ppermute x16, starting transfers between devices, flip(): return lax.ppermute(x, ('chip', 'core'), pairs)  24.6 us
    dot_general x2, matrix products, dot_nn(): lax.dot_general(a, b, (((1,), (0,)), ((), ())), preferred_element_type=F32)  21.5 us
  transfers between devices with their start and end apart: 59, of which 33 were waited for; matrix products, arithmetic and copies ran while one was open for 16% of the time, Pallas kernels for 20%

profile of v2, /device:TPU:0, one launch (start us, length us, event | category | flops | bytes accessed | tf_op | source)
XLA Modules:
  0.0 774.2 jit_solution(16006817132265769420)
XLA Ops:
  30.7 21.4 %collective-permute-done.1 = bf16[64,1344]{1,0:T(8,128)(2,1)S(1)} collective-permute-done((bf16[64,1344]{1,0:T(8,128)(2,1)S(1)}, bf16[64,1344]{1,0:T(8,128)(2,1)S(1)}, u32[]{:S(2)}, u32[]{:S(2)}) %collective-permute-start.1) | collective-permute-done | bytes 172064 | tf_op jit(solution)/shard_map/ppermute | solution.py:717
  67.0 23.5 %all-gather.4.cloned.1.call-done.h0_ref.h1_ref = bf16[6400,256]{1,0:T(8,128)(2,1)} async-done(((bf16[1600,256]{1,0:T(8,128)(2,1)}), bf16[6400,256]{1,0:T(8,128)(2,1)}) %all-gather.4.cloned.1.call-update) | async-done | bytes 3276816 | tf_op jit(solution)/shard_map/all_gather | solution.py:736
  120.8 13.1 %collective-permute-done.11 = bf16[56,1600]{1,0:T(8,128)(2,1)S(1)} collective-permute-done((bf16[56,1600]{1,0:T(8,128)(2,1)S(1)}, bf16[56,1600]{1,0:T(8,128)(2,1)S(1)}, u32[]{:S(2)}, u32[]{:S(2)}) %collective-permute-start.11) | collective-permute-done | bytes 179232 | tf_op jit(solution)/shard_map/ppermute | solution.py:717
  165.4 19.9 %shard_map.281 = (f32[448,1024]{1,0:T(8,128)}, bf16[448,1024]{1,0:T(8,128)(2,1)}, f32[7,1,1024]{2,1,0:T(1,128)}) custom-call(s32[1]{0:T(128)} %bitcast.256, bf16[1344,1024]{1,0:T(8,128)(2,1)} %add_convert_fusion.1.q_ref.k_ref.v_ref, bf16[1344,1024]{1,0:T(8,128)(2,1)} %add_convert_fusion.1.q_ref.k_ref.v_ref, ...), custom_call_target="tpu_custom_call" | custom-call | flops 20000000000 | bytes 1024 | tf_op jit(solution)/shard_map/pallas_call | solution.py:47
  187.2 9.8 %collective-permute-done.15 = bf16[4,56,1600]{2,1,0:T(8,128)(2,1)S(1)} collective-permute-done((bf16[4,56,1600]{2,1,0:T(8,128)(2,1)S(1)}, bf16[4,56,1600]{2,1,0:T(8,128)(2,1)S(1)}, u32[]{:S(2)}, u32[]{:S(2)}) %collective-permute-start.15) | collective-permute-done | bytes 716832 | tf_op jit(solution)/shard_map/ppermute | solution.py:757
  197.3 59.3 %all-gather.6.cloned.1.call-done = bf16[1792,1024]{1,0:T(8,128)(2,1)} async-done(((bf16[448,1024]{1,0:T(8,128)(2,1)}), bf16[1792,1024]{1,0:T(8,128)(2,1)}) %all-gather.6.cloned.1.call-update) | async-done | bytes 3670032 | tf_op jit(solution)/shard_map/all_gather | solution.py:736
  264.0 12.2 %collective-permute-done.16 = bf16[4,112,1600]{2,1,0:T(8,128)(2,1)} collective-permute-done((bf16[4,112,1600]{2,1,0:T(8,128)(2,1)S(1)}, bf16[4,112,1600]{2,1,0:T(8,128)(2,1)}, u32[]{:S(2)}, u32[]{:S(2)}) %collective-permute-start.16) | collective-permute-done | bytes 1433632 | tf_op jit(solution)/shard_map/ppermute | solution.py:757
  294.1 9.8 %multiply_convert_fusion = (bf16[1600,1024]{1,0:T(8,128)(2,1)S(1)}, f32[1600,1024]{1,0:T(8,128)}) fusion(f32[1600]{0:T(1024)S(1)} %convert_element_type.121, bf16[1600,1600]{1,0:T(8,128)(2,1)S(1)} %bitcast.204, bf16[1600,1024]{1,0:T(8,128)(2,1)S(1)} %get-tuple-element.182.a_ref), kind=kOutput, calls=%fused_computation.11 | convolution fusion | flops 5259264000 | bytes 18233600 | tf_op jit(solution)/shard_map/dot_general | solution.py:26
  328.9 13.5 %fusion.7.b_ref = bf16[1600,1024]{1,0:T(8,128)(2,1)S(1)} fusion(f32[1600,1024]{1,0:T(8,128)} %get-tuple-element.314, bf16[1600,1600]{1,0:T(8,128)(2,1)} %param.32, bf16[1600,1024]{1,0:T(8,128)(2,1)} %shard_map.283.b_ref, f32[1600]{0:T(1024)S(1)} %convert_element_type.121), kind=kOutput, calls=%fused_computation.9 | convolution fusion | flops 5275648000 | bytes 18233600 | tf_op jit(solution)/shard_map/dot_general | solution.py:30
  362.2 12.1 %shard_map.285 = (bf16[4,224,1600]{2,1,0:T(8,128)(2,1)}, bf16[224,1600]{1,0:T(8,128)(2,1)}, bf16[224,1600]{1,0:T(8,128)(2,1)}, bf16[224,1600]{1,0:T(8,128)(2,1)}, bf16[224,1600]{1,0:T(8,128)(2,1)}) custom-call(s32[1]{0:T(128)} %bitcast.45.core_ref, bf16[1600,1024]{1,0:T(8,128)(2,1)} %copy-done.20, bf16[1600,1024]{1,0:T(8,128)(2,1)} %shard_map.283.b_ref, ...), custom_call_target="tpu_custom_call" | custom-call | flops 1024 | bytes 1024 | tf_op jit(solution)/shard_map/pallas_call | solution.py:47
  375.8 11.9 %shard_map.286 = (bf16[4,224,1600]{2,1,0:T(8,128)(2,1)}, bf16[224,1600]{1,0:T(8,128)(2,1)}, bf16[224,1600]{1,0:T(8,128)(2,1)}, bf16[224,1600]{1,0:T(8,128)(2,1)}, bf16[224,1600]{1,0:T(8,128)(2,1)}) custom-call(s32[1]{0:T(128)} %bitcast.45.core_ref, bf16[1600,1024]{1,0:T(8,128)(2,1)} %copy-done.4, bf16[1600,1024]{1,0:T(8,128)(2,1)} %copy-done.5, ...), custom_call_target="tpu_custom_call" | custom-call | flops 1024 | bytes 1024 | tf_op jit(solution)/shard_map/pallas_call | solution.py:47
  398.5 10.4 %shard_map.287 = (bf16[8,112,1600]{2,1,0:T(8,128)(2,1)}, bf16[8,112,1600]{2,1,0:T(8,128)(2,1)}) custom-call(s32[1]{0:T(128)} %bitcast.44.bit_ref, bf16[4,224,1600]{2,1,0:T(8,128)(2,1)} %get-tuple-element.112.refs_0_, bf16[224,1600]{1,0:T(8,128)(2,1)} %copy-done.39, bf16[224,1600]{1,0:T(8,128)(2,1)} %copy-done.40, bf16[224,1600]{1,0:T(8,128)(2,1)} %copy-done.41, ...), custom_call_target="tpu_custom_call" | custom-call | flops 1024 | bytes 1024 | tf_op jit(solution)/shard_map/pallas_call | solution.py:47
  435.6 9.2 %collective-permute-done.31.y_ref = bf16[8,112,1600]{2,1,0:T(8,128)(2,1)} collective-permute-done((bf16[8,112,1600]{2,1,0:T(8,128)(2,1)}, bf16[8,112,1600]{2,1,0:T(8,128)(2,1)}, u32[]{:S(2)}, u32[]{:S(2)}) %collective-permute-start.31) | collective-permute-done | bytes 2867232 | tf_op jit(solution)/shard_map/ppermute | solution.py:757
  466.5 19.5 %shard_map.292 = bf16[3,448,1024]{2,1,0:T(8,128)(2,1)} custom-call(s32[1]{0:T(128)} %bitcast.257, bf16[1344,1024]{1,0:T(8,128)(2,1)} %add_convert_fusion.1.q_ref.k_ref.v_ref, bf16[1344,1024]{1,0:T(8,128)(2,1)} %add_convert_fusion.1.q_ref.k_ref.v_ref, bf16[1344,1024]{1,0:T(8,128)(2,1)} %add_convert_fusion.1.q_ref.k_ref.v_ref, ...), custom_call_target="tpu_custom_call" | custom-call | flops 20000000000 | bytes 1024 | tf_op jit(solution)/shard_map/pallas_call | solution.py:47
  486.0 14.1 %shard_map.293 = (bf16[6400,256]{1,0:T(8,128)(2,1)}, f32[1600,1]{1,0:T(8,128)}, f32[1600,1]{1,0:T(8,128)}) custom-call(s32[8]{0:T(128)} %select_reduce_fusion.tab_ref, bf16[1344,1024]{1,0:T(8,128)(2,1)} %bitcast.198, bf16[6400,256]{1,0:T(8,128)(2,1)} %all-gather.4.cloned.1.call-done.h0_ref.h1_ref, ...), custom_call_target="tpu_custom_call" | custom-call | flops 20000000000 | bytes 1024 | tf_op jit(solution)/shard_map/pallas_call | solution.py:47
  506.9 9.6 %shard_map.295 = (bf16[4,224,1344]{2,1,0:T(8,128)(2,1)}, bf16[4,224,1344]{2,1,0:T(8,128)(2,1)}) custom-call(s32[1]{0:T(128)} %bitcast.45.core_ref, bf16[1600,1024]{1,0:T(8,128)(2,1)} %get-tuple-element.96.a_ref, bf16[1344,1024]{1,0:T(8,128)(2,1)} %bitcast.199, f32[4,8,1344]{2,1,0:T(8,128)} %pad.84.small_ref), custom_call_target="tpu_custom_call" | custom-call | flops 1024 | bytes 1024 | tf_op jit(solution)/shard_map/pallas_call | solution.py:47
  521.4 11.9 %collective-permute-done.37 = bf16[56,1600]{1,0:T(8,128)(2,1)S(1)} collective-permute-done((bf16[56,1600]{1,0:T(8,128)(2,1)S(1)}, bf16[56,1600]{1,0:T(8,128)(2,1)S(1)}, u32[]{:S(2)}, u32[]{:S(2)}) %collective-permute-start.37) | collective-permute-done | bytes 179232 | tf_op jit(solution)/shard_map/ppermute | solution.py:717
  539.1 19.7 %collective-permute-done.36 = bf16[56,1600]{1,0:T(8,128)(2,1)S(1)} collective-permute-done((bf16[56,1600]{1,0:T(8,128)(2,1)S(1)}, bf16[56,1600]{1,0:T(8,128)(2,1)S(1)}, u32[]{:S(2)}, u32[]{:S(2)}) %collective-permute-start.36) | collective-permute-done | bytes 179232 | tf_op jit(solution)/shard_map/ppermute | solution.py:717
  577.7 14.6 %collective-permute-done.38 = bf16[1,56,6400]{2,1,0:T(8,128)(2,1)} collective-permute-done((bf16[1,56,6400]{2,1,0:T(8,128)(2,1)}, bf16[1,56,6400]{2,1,0:T(8,128)(2,1)}, u32[]{:S(2)}, u32[]{:S(2)}) %collective-permute-start.38) | collective-permute-done | bytes 716832 | tf_op jit(solution)/shard_map/ppermute | solution.py:757
  594.9 32.3 %collective-permute-done.47 = bf16[2,4,56,1600]{3,2,1,0:T(8,128)(2,1)} collective-permute-done((bf16[2,4,56,1600]{3,2,1,0:T(8,128)(2,1)}, bf16[2,4,56,1600]{3,2,1,0:T(8,128)(2,1)}, u32[]{:S(2)}, u32[]{:S(2)}) %collective-permute-start.47) | collective-permute-done | bytes 1433632 | tf_op jit(solution)/shard_map/ppermute | solution.py:757
  639.4 14.9 %collective-permute-done.43 = bf16[4,56,3008]{2,1,0:T(8,128)(2,1)} collective-permute-done((bf16[4,56,3008]{2,1,0:T(8,128)(2,1)}, bf16[4,56,3008]{2,1,0:T(8,128)(2,1)}, u32[]{:S(2)}, u32[]{:S(2)}) %collective-permute-start.43) | collective-permute-done | bytes 1347616 | tf_op jit(solution)/shard_map/ppermute | solution.py:757
  670.2 18.8 %collective-permute-done.45 = bf16[56,3008]{1,0:T(8,128)(2,1)S(1)} collective-permute-done((bf16[56,3008]{1,0:T(8,128)(2,1)S(1)}, bf16[56,3008]{1,0:T(8,128)(2,1)S(1)}, u32[]{:S(2)}, u32[]{:S(2)}) %collective-permute-start.45) | collective-permute-done | bytes 336928 | tf_op jit(solution)/shard_map/ppermute | solution.py:717
  697.4 16.3 %collective-permute-done.49 = bf16[1,56,6464]{2,1,0:T(8,128)(2,1)S(1)} collective-permute-done((bf16[1,56,6464]{2,1,0:T(8,128)(2,1)S(1)}, bf16[1,56,6464]{2,1,0:T(8,128)(2,1)S(1)}, u32[]{:S(2)}, u32[]{:S(2)}) %collective-permute-start.49) | collective-permute-done | bytes 724000 | tf_op jit(solution)/shard_map/ppermute | solution.py:757
  722.0 13.4 %collective-permute-done.50 = bf16[2,1,56,6464]{3,2,1,0:T(8,128)(2,1)S(1)} collective-permute-done((bf16[2,1,56,6464]{3,2,1,0:T(8,128)(2,1)S(1)}, bf16[2,1,56,6464]{3,2,1,0:T(8,128)(2,1)S(1)}, u32[]{:S(2)}, u32[]{:S(2)}) %collective-permute-start.50) | collective-permute-done | bytes 1447968 | tf_op jit(solution)/shard_map/ppermute | solution.py:757
  (405 shorter events, 346.5 us)
Async XLA Ops:
  7.2 83.3 %all-gather.4.cloned.1.call-start = ((), (), s32[]{:S(2)}) async-start(), calls=%async_computation.2 | async-start | bytes 4096000 | tf_op jit(solution)/shard_map/all_gather | solution.py:736
  7.9 248.7 %all-gather.6.cloned.1.call-start = ((), (), s32[]{:S(2)}) async-start(), calls=%async_computation.3 | async-start | bytes 4587520 | tf_op jit(solution)/shard_map/all_gather | solution.py:736
  21.9 30.2 %collective-permute-start.1 = (bf16[64,1344]{1,0:T(8,128)(2,1)S(1)}, bf16[64,1344]{1,0:T(8,128)(2,1)S(1)}, u32[]{:S(2)}, u32[]{:S(2)}) collective-permute-start(bf16[64,1344]{1,0:T(8,128)(2,1)S(1)} %get-tuple-element.282), channel_id=1, source_target_pairs={{0,2},{1,3},{2,0},{3,1},{4,6},{5,7},{6,4},{7,5},{8,10},{9,11},{10,... | collective-permute-start | bytes 516104 | tf_op jit(solution)/shard_map/ppermute | solution.py:717
  21.9 30.2 %collective-permute-start = (bf16[64,1344]{1,0:T(8,128)(2,1)S(1)}, bf16[64,1344]{1,0:T(8,128)(2,1)S(1)}, u32[]{:S(2)}, u32[]{:S(2)}) collective-permute-start(bf16[64,1344]{1,0:T(8,128)(2,1)S(1)} %get-tuple-element.283), channel_id=1, source_target_pairs={{0,1},{1,2},{2,3},{3,0},{4,5},{5,6},{6,7},{7,4},{8,9},{9,10},{10,1... | collective-permute-start | bytes 516104 | tf_op jit(solution)/shard_map/ppermute | solution.py:717
  111.9 25.8 %collective-permute-start.9 = (bf16[4,224,1344]{2,1,0:T(8,128)(2,1)S(1)}, bf16[4,224,1344]{2,1,0:T(8,128)(2,1)}, u32[]{:S(2)}, u32[]{:S(2)}) collective-permute-start(bf16[4,224,1344]{2,1,0:T(8,128)(2,1)S(1)} %pad_maximum_fusion.8), channel_id=1, source_target_pairs={{0,4},{4,0},{1,5},{5,1},{2,6},{6,2},{3,7},{7,3},{8,12},{12,8},{9,1... | collective-permute-start | bytes 7225352 | tf_op jit(solution)/shard_map/ppermute | solution.py:720
  185.3 138.1 %all-gather.8.cloned.1.call-start = ((), (), s32[]{:S(2)}) async-start(), calls=%async_computation.4 | async-start | bytes 4096000 | tf_op jit(solution)/shard_map/all_gather | solution.py:736
  259.9 161.1 %reduce-scatter.3.cloned.1.call-start = ((), (), s32[]{:S(2)}) async-start(), calls=%async_computation.5 | async-start | bytes 4096000 | tf_op jit(solution)/shard_map/reduce_scatter | solution.py:909
  359.4 215.9 %reduce-scatter.5.cloned.1.call-start = ((), (), s32[]{:S(2)}) async-start(), calls=%async_computation.6 | async-start | bytes 4096000 | tf_op jit(solution)/shard_map/reduce_scatter | solution.py:909
  408.9 35.8 %collective-permute-start.31 = (bf16[8,112,1600]{2,1,0:T(8,128)(2,1)}, bf16[8,112,1600]{2,1,0:T(8,128)(2,1)}, u32[]{:S(2)}, u32[]{:S(2)}) collective-permute-start(bf16[8,112,1600]{2,1,0:T(8,128)(2,1)} %get-tuple-element.131), channel_id=1, source_target_pairs={{0,8},{4,20},{8,0},{12,28},{16,24},{20,4},{24,16},{28,12},{1,9},{5... | collective-permute-start | bytes 8601608 | tf_op jit(solution)/shard_map/ppermute | solution.py:757
  430.0 30.6 %collective-permute-start.29 = (bf16[448,256]{1,0:T(8,128)(2,1)S(1)}, bf16[448,256]{1,0:T(8,128)(2,1)S(1)}, u32[]{:S(2)}, u32[]{:S(2)}) collective-permute-start(bf16[448,256]{1,0:T(8,128)(2,1)S(1)} %get-tuple-element.251), channel_id=1, source_target_pairs={{0,3},{1,0},{2,1},{3,2},{4,7},{5,4},{6,5},{7,6},{8,11},{9,8},{10,9... | collective-permute-start | bytes 688136 | tf_op jit(solution)/shard_map/ppermute | solution.py:717
  432.2 28.4 %collective-permute-start.28 = (bf16[448,256]{1,0:T(8,128)(2,1)S(1)}, bf16[448,256]{1,0:T(8,128)(2,1)S(1)}, u32[]{:S(2)}, u32[]{:S(2)}) collective-permute-start(bf16[448,256]{1,0:T(8,128)(2,1)S(1)} %get-tuple-element.252), channel_id=1, source_target_pairs={{0,2},{1,3},{2,0},{3,1},{4,6},{5,7},{6,4},{7,5},{8,10},{9,11},{10,... | collective-permute-start | bytes 688136 | tf_op jit(solution)/shard_map/ppermute | solution.py:717
  432.6 27.9 %collective-permute-start.27 = (bf16[448,256]{1,0:T(8,128)(2,1)S(1)}, bf16[448,256]{1,0:T(8,128)(2,1)S(1)}, u32[]{:S(2)}, u32[]{:S(2)}) collective-permute-start(bf16[448,256]{1,0:T(8,128)(2,1)S(1)} %get-tuple-element.253), channel_id=1, source_target_pairs={{0,1},{1,2},{2,3},{3,0},{4,5},{5,6},{6,7},{7,4},{8,9},{9,10},{10,1... | collective-permute-start | bytes 688136 | tf_op jit(solution)/shard_map/ppermute | solution.py:717
  453.3 63.2 %collective-permute-start.34 = (bf16[8,56,1600]{2,1,0:T(8,128)(2,1)}, bf16[8,56,1600]{2,1,0:T(8,128)(2,1)}, u32[]{:S(2)}, u32[]{:S(2)}) collective-permute-start(bf16[8,56,1600]{2,1,0:T(8,128)(2,1)} %get-tuple-element.144), channel_id=1, source_target_pairs={{0,16},{4,12},{8,24},{12,4},{16,0},{20,28},{24,8},{28,20},{1,17},{... | collective-permute-start | bytes 4300808 | tf_op jit(solution)/shard_map/ppermute | solution.py:757
  500.1 61.9 %collective-permute-start.40 = (bf16[4,224,1600]{2,1,0:T(8,128)(2,1)}, bf16[4,224,1600]{2,1,0:T(8,128)(2,1)}, u32[]{:S(2)}, u32[]{:S(2)}) collective-permute-start(bf16[4,224,1600]{2,1,0:T(8,128)(2,1)} %get-tuple-element.148), channel_id=1, source_target_pairs={{0,4},{4,0},{1,5},{5,1},{2,6},{6,2},{3,7},{7,3},{8,12},{12,8},{9,1... | collective-permute-start | bytes 8601608 | tf_op jit(solution)/shard_map/ppermute | solution.py:720
  516.5 45.6 %collective-permute-start.41 = (bf16[4,224,1344]{2,1,0:T(8,128)(2,1)}, bf16[4,224,1344]{2,1,0:T(8,128)(2,1)}, u32[]{:S(2)}, u32[]{:S(2)}) collective-permute-start(bf16[4,224,1344]{2,1,0:T(8,128)(2,1)} %get-tuple-element.152), channel_id=1, source_target_pairs={{0,4},{4,0},{1,5},{5,1},{2,6},{6,2},{3,7},{7,3},{8,12},{12,8},{9,1... | collective-permute-start | bytes 7225352 | tf_op jit(solution)/shard_map/ppermute | solution.py:720
  519.9 40.8 %collective-permute-start.39 = (bf16[4,56,1600]{2,1,0:T(8,128)(2,1)S(1)}, bf16[4,56,1600]{2,1,0:T(8,128)(2,1)S(1)}, u32[]{:S(2)}, u32[]{:S(2)}) collective-permute-start(bf16[4,56,1600]{2,1,0:T(8,128)(2,1)S(1)} %get-tuple-element.218), channel_id=1, source_target_pairs={{0,16},{4,12},{8,24},{12,4},{16,0},{20,28},{24,8},{28,20},{1,17},{... | collective-permute-start | bytes 2150408 | tf_op jit(solution)/shard_map/ppermute | solution.py:757
  521.4 37.4 %collective-permute-start.36 = (bf16[56,1600]{1,0:T(8,128)(2,1)S(1)}, bf16[56,1600]{1,0:T(8,128)(2,1)S(1)}, u32[]{:S(2)}, u32[]{:S(2)}) collective-permute-start(bf16[56,1600]{1,0:T(8,128)(2,1)S(1)} %get-tuple-element.262), channel_id=1, source_target_pairs={{0,2},{1,3},{2,0},{3,1},{4,6},{5,7},{6,4},{7,5},{8,10},{9,11},{10,... | collective-permute-start | bytes 537608 | tf_op jit(solution)/shard_map/ppermute | solution.py:717
  570.2 60.4 %collective-permute-start.42 = (bf16[4,112,3008]{2,1,0:T(8,128)(2,1)}, bf16[4,112,3008]{2,1,0:T(8,128)(2,1)}, u32[]{:S(2)}, u32[]{:S(2)}) collective-permute-start(bf16[4,112,3008]{2,1,0:T(8,128)(2,1)} %get-tuple-element.154), channel_id=1, source_target_pairs={{0,8},{4,20},{8,0},{12,28},{16,24},{20,4},{24,16},{28,12},{1,9},{5... | collective-permute-start | bytes 8085512 | tf_op jit(solution)/shard_map/ppermute | solution.py:757
  573.6 53.6 %collective-permute-start.47 = (bf16[2,4,56,1600]{3,2,1,0:T(8,128)(2,1)}, bf16[2,4,56,1600]{3,2,1,0:T(8,128)(2,1)}, u32[]{:S(2)}, u32[]{:S(2)}) collective-permute-start(bf16[2,4,56,1600]{3,2,1,0:T(8,128)(2,1)} %pad_maximum_fusion.12), channel_id=1, source_target_pairs={{0,8},{4,20},{8,0},{12,28},{16,24},{20,4},{24,16},{28,12},{1,9},{5... | collective-permute-start | bytes 4300808 | tf_op jit(solution)/shard_map/ppermute | solution.py:757
  575.3 55.3 %collective-permute-start.32 = (bf16[800,256]{1,0:T(8,128)(2,1)}, bf16[800,256]{1,0:T(8,128)(2,1)}, u32[]{:S(2)}, u32[]{:S(2)}) collective-permute-start(bf16[800,256]{1,0:T(8,128)(2,1)} %get-tuple-element.141), channel_id=1, source_target_pairs={{0,2},{1,3},{2,0},{3,1},{4,6},{5,7},{6,4},{7,5},{8,10},{9,11},{10,... | collective-permute-start | bytes 1228808 | tf_op jit(solution)/shard_map/ppermute | solution.py:717
  630.6 30.3 %collective-permute-start.48 = (bf16[4,4,56,1600]{3,2,1,0:T(8,128)(2,1)}, bf16[4,4,56,1600]{3,2,1,0:T(8,128)(2,1)}, u32[]{:S(2)}, u32[]{:S(2)}) collective-permute-start(bf16[4,4,56,1600]{3,2,1,0:T(8,128)(2,1)} %pad_maximum_fusion.6.mine_ref), channel_id=1, source_target_pairs={{0,4},{4,0},{1,5},{5,1},{2,6},{6,2},{3,7},{7,3},{8,12},{12,8},{9,1... | collective-permute-start | bytes 8601608 | tf_op jit(solution)/shard_map/ppermute | solution.py:720
  659.1 29.8 %collective-permute-start.45 = (bf16[56,3008]{1,0:T(8,128)(2,1)S(1)}, bf16[56,3008]{1,0:T(8,128)(2,1)S(1)}, u32[]{:S(2)}, u32[]{:S(2)}) collective-permute-start(bf16[56,3008]{1,0:T(8,128)(2,1)S(1)} %get-tuple-element.242), channel_id=1, source_target_pairs={{0,2},{1,3},{2,0},{3,1},{4,6},{5,7},{6,4},{7,5},{8,10},{9,11},{10,... | collective-permute-start | bytes 1010696 | tf_op jit(solution)/shard_map/ppermute | solution.py:717
  659.1 29.8 %collective-permute-start.44 = (bf16[56,3008]{1,0:T(8,128)(2,1)S(1)}, bf16[56,3008]{1,0:T(8,128)(2,1)S(1)}, u32[]{:S(2)}, u32[]{:S(2)}) collective-permute-start(bf16[56,3008]{1,0:T(8,128)(2,1)S(1)} %get-tuple-element.243), channel_id=1, source_target_pairs={{0,1},{1,2},{2,3},{3,0},{4,5},{5,6},{6,7},{7,4},{8,9},{9,10},{10,1... | collective-permute-start | bytes 1010696 | tf_op jit(solution)/shard_map/ppermute | solution.py:717
  720.9 25.6 %collective-permute-start.53 = (bf16[4,1,56,6400]{3,2,1,0:T(8,128)(2,1)}, bf16[4,1,56,6400]{3,2,1,0:T(8,128)(2,1)}, u32[]{:S(2)}, u32[]{:S(2)}) collective-permute-start(bf16[4,1,56,6400]{3,2,1,0:T(8,128)(2,1)} %constant_dynamic-update-slice_fusion.mine_ref), channel_id=1, source_target_pairs={{0,4},{4,0},{1,5},{5,1},{2,6},{6,2},{3,7},{7,3},{8,12},{12,8},{9,1... | collective-permute-start | bytes 8601608 | tf_op jit(solution)/shard_map/ppermute | solution.py:720
  (95 other events, 1290.9 us)
Sparse Core Ops, SparseCore 0:
  9.6 80.8 all-gather.3
  185.4 71.0 all-gather.5
  260.1 63.3 all-gather.7
  359.5 61.5 reduce-scatter.2
  500.2 72.1 reduce-scatter.4

commit v3 on v2

--- a/solution.py
+++ b/solution.py
@@ -943,7 +943,6 @@
     e_a, g_attn_gain, g_attn_shift = first_back_call(
         after(tab, keep_out, ffn_back), g_mixed_rows, hidden_all, w_qkv, shards
     )
-    e_a_own = token_scatter(e_a)
     ffn_own = ffn_own + ffn_back.astype(F32)
     if merged:
         ffn_last = after(sum_last(ffn_sum), e_a)
@@ -951,6 +950,7 @@
     else:
         down_own, up_own = ffn_sum
     up_got = exchange(up_own)
+    e_a_own = token_scatter(after(e_a, up_got))
     down_near = spread_near(down_own)
     up_row = with_sum(jnp.concatenate([up_got[s] for s in range(shards)], axis=-1), up_got)
     up_near = spread_near(up_row)
@@ -978,12 +978,12 @@
         keep, send = wide_step_call(
             after(scalar(first_bit), down_near), [(keep_out, out_sum[1]), mix_sum], (0, skip), skip + 3 * wc
         )
-        wide_sum = sum_second((keep, flip(send, 0)), up_near, *ffn_top, flops=SHORT)
+        wide_sum = sum_second((keep, flip(send, 0)), up_near, flops=SHORT)
         wide_own = sum_last(wide_sum)
     else:
         gap = jnp.zeros((shards, piece, skip - width), BF)
         wide_own = jnp.concatenate([chip_sum((keep_out, out_sum[1])), gap, chip_sum(mix_sum)], axis=-1)
-    wide_own = after(wide_own, e_a_own, *ffn_low)
+    wide_own = after(wide_own, e_a_own, *ffn_top)
     wide_got = exchange(wide_own)
     up_mine = spread_far(after(up_near, wide_own))
     g_down_full, down_small = spread_last(down_mine, [(0, width)], wide_own)
@@ -996,9 +996,9 @@
     mix_row = with_sum(jnp.concatenate(columns, axis=-1), wide_got[:, :, skip:])
     out_row = jnp.sum(wide_got[:, :, :skip].astype(F32), axis=0).astype(BF)
     wide_row = jnp.concatenate([out_row[None], mix_row], axis=-1)
-    wide_near = spread_near(after(wide_row, g_down_full))
+    wide_near = after(spread_near(after(wide_row, g_down_full, up_mine)), *ffn_low)
     g_out_full, out_small, g_mix_full, mix_small = spread_last(
-        spread_far(wide_near), [(0, width), (skip, skip + 3 * width)]
+        spread_far(wide_near), [(0, width), (skip, skip + 3 * width)], g_up_full
     )
 
     block_out = (middle_own + ffn_own + small[:, 7:8]).astype(BF).T

time: 782 us -> 770 us (0.985)
  waiting for transfers between devices: 341 us -> 328 us
    unnamed x121 -> x118, local copies, waits for them, and re-layouts: 15.5 us -> 18 us
  transfers between devices with their start and end apart: 59 -> 59, of which waited for: 33 -> 31; matrix products, arithmetic and copies ran while one was open for 16% -> 18% of each run, Pallas kernels for 20% -> 20%
where the time goes in v3:
time: 770 us; the launch traced here: 762 us
  waiting for transfers between devices  328 us (43%)
  Pallas kernels  193 us (25%)
  local copies, waits for them, and re-layouts  62.2 us (8%)
  starting transfers between devices  58.8 us (8%)
  matrix products  54.9 us (7%)
  other arithmetic  48.7 us (6%)
  between operations  16.6 us (2%)
    pallas_call x21, Pallas kernels, call(): pl.pallas_call(kernel, out_shape=[jax.ShapeDtypeStruct(shape, dtype) for...  193 us
    ppermute x16, waiting for transfers between devices, flip(): return lax.ppermute(x, ('chip', 'core'), pairs)  131 us
    ppermute x22, waiting for transfers between devices, to_next(): lax.ppermute(x, 'shard', [(i, (i + t) % shards) for i in range(shards)])  96 us
    all_gather x3, waiting for transfers between devices, over_shard(): return lax.all_gather(x, 'shard', axis=0, tiled=True)  82.8 us
    ppermute x22, starting transfers between devices, to_next(): lax.ppermute(x, 'shard', [(i, (i + t) % shards) for i in range(shards)])  33.4 us
    dot_general x4, matrix products, dot_tn(): lax.dot_general(a, b, (((0,), (0,)), ((), ())), preferred_element_type=F32)  33.4 us
    ppermute x16, starting transfers between devices, flip(): return lax.ppermute(x, ('chip', 'core'), pairs)  23 us
    dot_general x2, matrix products, dot_nn(): lax.dot_general(a, b, (((1,), (0,)), ((), ())), preferred_element_type=F32)  21.5 us
  transfers between devices with their start and end apart: 59, of which 31 were waited for; matrix products, arithmetic and copies ran while one was open for 18% of the time, Pallas kernels for 20%

profile of v3, /device:TPU:0, one launch (start us, length us, event | category | flops | bytes accessed | tf_op | source)
XLA Modules:
  0.0 762.0 jit_solution(1699966531750531951)
XLA Ops:
  30.7 21.4 %collective-permute-done.1 = bf16[64,1344]{1,0:T(8,128)(2,1)S(1)} collective-permute-done((bf16[64,1344]{1,0:T(8,128)(2,1)S(1)}, bf16[64,1344]{1,0:T(8,128)(2,1)S(1)}, u32[]{:S(2)}, u32[]{:S(2)}) %collective-permute-start.1) | collective-permute-done | bytes 172064 | tf_op jit(solution)/shard_map/ppermute | solution.py:717
  67.0 23.5 %all-gather.4.cloned.1.call-done.h0_ref.h1_ref = bf16[6400,256]{1,0:T(8,128)(2,1)} async-done(((bf16[1600,256]{1,0:T(8,128)(2,1)}), bf16[6400,256]{1,0:T(8,128)(2,1)}) %all-gather.4.cloned.1.call-update) | async-done | bytes 3276816 | tf_op jit(solution)/shard_map/all_gather | solution.py:736
  120.8 13.1 %collective-permute-done.11 = bf16[56,1600]{1,0:T(8,128)(2,1)S(1)} collective-permute-done((bf16[56,1600]{1,0:T(8,128)(2,1)S(1)}, bf16[56,1600]{1,0:T(8,128)(2,1)S(1)}, u32[]{:S(2)}, u32[]{:S(2)}) %collective-permute-start.11) | collective-permute-done | bytes 179232 | tf_op jit(solution)/shard_map/ppermute | solution.py:717
  165.4 19.9 %shard_map.281 = (f32[448,1024]{1,0:T(8,128)}, bf16[448,1024]{1,0:T(8,128)(2,1)}, f32[7,1,1024]{2,1,0:T(1,128)}) custom-call(s32[1]{0:T(128)} %bitcast.253, bf16[1344,1024]{1,0:T(8,128)(2,1)} %add_convert_fusion.1.q_ref.k_ref.v_ref, bf16[1344,1024]{1,0:T(8,128)(2,1)} %add_convert_fusion.1.q_ref.k_ref.v_ref, ...), custom_call_target="tpu_custom_call" | custom-call | flops 20000000000 | bytes 1024 | tf_op jit(solution)/shard_map/pallas_call | solution.py:47
  187.2 9.8 %collective-permute-done.15 = bf16[4,56,1600]{2,1,0:T(8,128)(2,1)S(1)} collective-permute-done((bf16[4,56,1600]{2,1,0:T(8,128)(2,1)S(1)}, bf16[4,56,1600]{2,1,0:T(8,128)(2,1)S(1)}, u32[]{:S(2)}, u32[]{:S(2)}) %collective-permute-start.15) | collective-permute-done | bytes 716832 | tf_op jit(solution)/shard_map/ppermute | solution.py:757
  197.3 59.3 %all-gather.6.cloned.1.call-done = bf16[1792,1024]{1,0:T(8,128)(2,1)} async-done(((bf16[448,1024]{1,0:T(8,128)(2,1)}), bf16[1792,1024]{1,0:T(8,128)(2,1)}) %all-gather.6.cloned.1.call-update) | async-done | bytes 3670032 | tf_op jit(solution)/shard_map/all_gather | solution.py:736
  264.0 12.2 %collective-permute-done.16 = bf16[4,112,1600]{2,1,0:T(8,128)(2,1)} collective-permute-done((bf16[4,112,1600]{2,1,0:T(8,128)(2,1)S(1)}, bf16[4,112,1600]{2,1,0:T(8,128)(2,1)}, u32[]{:S(2)}, u32[]{:S(2)}) %collective-permute-start.16) | collective-permute-done | bytes 1433632 | tf_op jit(solution)/shard_map/ppermute | solution.py:757
  294.1 9.8 %multiply_convert_fusion = (bf16[1600,1024]{1,0:T(8,128)(2,1)S(1)}, f32[1600,1024]{1,0:T(8,128)}) fusion(f32[1600]{0:T(1024)S(1)} %convert_element_type.121, bf16[1600,1600]{1,0:T(8,128)(2,1)S(1)} %bitcast.202, bf16[1600,1024]{1,0:T(8,128)(2,1)S(1)} %get-tuple-element.188.a_ref), kind=kOutput, calls=%fused_computation.11 | convolution fusion | flops 5259264000 | bytes 18233600 | tf_op jit(solution)/shard_map/dot_general | solution.py:26
  305.7 10.2 %fusion.8.x_ref = bf16[1600,1024]{1,0:T(8,128)(2,1)} fusion(bf16[1600,1024]{1,0:T(8,128)(2,1)S(1)} %get-tuple-element.319.a_ref, bf16[1600,1600]{1,0:T(8,128)(2,1)} %param.32), kind=kOutput, calls=%fused_computation.25 | convolution fusion | flops 5244518400 | bytes 11673600 | tf_op jit(solution)/shard_map/dot_general | solution.py:26
  329.4 13.5 %fusion.7.b_ref = bf16[1600,1024]{1,0:T(8,128)(2,1)S(1)} fusion(f32[1600,1024]{1,0:T(8,128)} %get-tuple-element.320, bf16[1600,1600]{1,0:T(8,128)(2,1)} %param.32, bf16[1600,1024]{1,0:T(8,128)(2,1)} %shard_map.283.b_ref, f32[1600]{0:T(1024)S(1)} %convert_element_type.121), kind=kOutput, calls=%fused_computation.9 | convolution fusion | flops 5275648000 | bytes 18233600 | tf_op jit(solution)/shard_map/dot_general | solution.py:30
  364.6 12.1 %shard_map.285 = (bf16[4,224,1600]{2,1,0:T(8,128)(2,1)}, bf16[224,1600]{1,0:T(8,128)(2,1)}, bf16[224,1600]{1,0:T(8,128)(2,1)}, bf16[224,1600]{1,0:T(8,128)(2,1)}, bf16[224,1600]{1,0:T(8,128)(2,1)}) custom-call(s32[1]{0:T(128)} %bitcast.45.core_ref, bf16[1600,1024]{1,0:T(8,128)(2,1)} %copy-done.16, bf16[1600,1024]{1,0:T(8,128)(2,1)} %shard_map.283.b_ref, ...), custom_call_target="tpu_custom_call" | custom-call | flops 1024 | bytes 1024 | tf_op jit(solution)/shard_map/pallas_call | solution.py:47
  378.2 11.9 %shard_map.286 = (bf16[4,224,1600]{2,1,0:T(8,128)(2,1)}, bf16[224,1600]{1,0:T(8,128)(2,1)}, bf16[224,1600]{1,0:T(8,128)(2,1)}, bf16[224,1600]{1,0:T(8,128)(2,1)}, bf16[224,1600]{1,0:T(8,128)(2,1)}) custom-call(s32[1]{0:T(128)} %bitcast.45.core_ref, bf16[1600,1024]{1,0:T(8,128)(2,1)} %copy-done.4, bf16[1600,1024]{1,0:T(8,128)(2,1)} %copy-done.5, ...), custom_call_target="tpu_custom_call" | custom-call | flops 1024 | bytes 1024 | tf_op jit(solution)/shard_map/pallas_call | solution.py:47
  400.9 10.4 %shard_map.287 = (bf16[8,112,1600]{2,1,0:T(8,128)(2,1)}, bf16[8,112,1600]{2,1,0:T(8,128)(2,1)}) custom-call(s32[1]{0:T(128)} %bitcast.44.bit_ref, bf16[4,224,1600]{2,1,0:T(8,128)(2,1)} %get-tuple-element.115.refs_0_, bf16[224,1600]{1,0:T(8,128)(2,1)} %copy-done.36, bf16[224,1600]{1,0:T(8,128)(2,1)} %copy-done.37, bf16[224,1600]{1,0:T(8,128)(2,1)} %copy-done.38, ...), custom_call_target="tpu_custom_call" | custom-call | flops 1024 | bytes 1024 | tf_op jit(solution)/shard_map/pallas_call | solution.py:47
  437.9 9.3 %collective-permute-done.31.y_ref = bf16[8,112,1600]{2,1,0:T(8,128)(2,1)} collective-permute-done((bf16[8,112,1600]{2,1,0:T(8,128)(2,1)}, bf16[8,112,1600]{2,1,0:T(8,128)(2,1)}, u32[]{:S(2)}, u32[]{:S(2)}) %collective-permute-start.31) | collective-permute-done | bytes 2867232 | tf_op jit(solution)/shard_map/ppermute | solution.py:757
  468.9 19.6 %shard_map.292 = bf16[3,448,1024]{2,1,0:T(8,128)(2,1)} custom-call(s32[1]{0:T(128)} %bitcast.254, bf16[1344,1024]{1,0:T(8,128)(2,1)} %add_convert_fusion.1.q_ref.k_ref.v_ref, bf16[1344,1024]{1,0:T(8,128)(2,1)} %add_convert_fusion.1.q_ref.k_ref.v_ref, bf16[1344,1024]{1,0:T(8,128)(2,1)} %add_convert_fusion.1.q_ref.k_ref.v_ref, ...), custom_call_target="tpu_custom_call" | custom-call | flops 20000000000 | bytes 1024 | tf_op jit(solution)/shard_map/pallas_call | solution.py:47
  491.4 14.1 %shard_map.293 = (bf16[6400,256]{1,0:T(8,128)(2,1)}, f32[1600,1]{1,0:T(8,128)}, f32[1600,1]{1,0:T(8,128)}) custom-call(s32[8]{0:T(128)} %select_reduce_fusion.tab_ref, bf16[1344,1024]{1,0:T(8,128)(2,1)} %bitcast.198, bf16[6400,256]{1,0:T(8,128)(2,1)} %all-gather.4.cloned.1.call-done.h0_ref.h1_ref, ...), custom_call_target="tpu_custom_call" | custom-call | flops 20000000000 | bytes 1024 | tf_op jit(solution)/shard_map/pallas_call | solution.py:47
  509.3 9.6 %shard_map.295 = (bf16[4,224,1344]{2,1,0:T(8,128)(2,1)}, bf16[4,224,1344]{2,1,0:T(8,128)(2,1)}) custom-call(s32[1]{0:T(128)} %bitcast.45.core_ref, bf16[1600,1024]{1,0:T(8,128)(2,1)} %get-tuple-element.99.a_ref, bf16[1344,1024]{1,0:T(8,128)(2,1)} %bitcast.199, f32[4,8,1344]{2,1,0:T(8,128)} %pad.84.small_ref), custom_call_target="tpu_custom_call" | custom-call | flops 1024 | bytes 1024 | tf_op jit(solution)/shard_map/pallas_call | solution.py:47
  529.4 11.4 %collective-permute-done.34 = bf16[56,1600]{1,0:T(8,128)(2,1)S(1)} collective-permute-done((bf16[56,1600]{1,0:T(8,128)(2,1)S(1)}, bf16[56,1600]{1,0:T(8,128)(2,1)S(1)}, u32[]{:S(2)}, u32[]{:S(2)}) %collective-permute-start.34) | collective-permute-done | bytes 179232 | tf_op jit(solution)/shard_map/ppermute | solution.py:717
  554.8 17.7 %collective-permute-done.38 = bf16[1,56,6400]{2,1,0:T(8,128)(2,1)S(1)} collective-permute-done((bf16[1,56,6400]{2,1,0:T(8,128)(2,1)S(1)}, bf16[1,56,6400]{2,1,0:T(8,128)(2,1)S(1)}, u32[]{:S(2)}, u32[]{:S(2)}) %collective-permute-start.38) | collective-permute-done | bytes 716832 | tf_op jit(solution)/shard_map/ppermute | solution.py:757
  573.8 34.1 %collective-permute-done.49 = bf16[2,4,56,1600]{3,2,1,0:T(8,128)(2,1)S(1)} collective-permute-done((bf16[2,4,56,1600]{3,2,1,0:T(8,128)(2,1)S(1)}, bf16[2,4,56,1600]{3,2,1,0:T(8,128)(2,1)S(1)}, u32[]{:S(2)}, u32[]{:S(2)}) %collective-permute-start.49) | collective-permute-done | bytes 1433632 | tf_op jit(solution)/shard_map/ppermute | solution.py:757
  622.6 12.7 %collective-permute-done.43 = bf16[4,56,3008]{2,1,0:T(8,128)(2,1)} collective-permute-done((bf16[4,56,3008]{2,1,0:T(8,128)(2,1)}, bf16[4,56,3008]{2,1,0:T(8,128)(2,1)}, u32[]{:S(2)}, u32[]{:S(2)}) %collective-permute-start.43) | collective-permute-done | bytes 1347616 | tf_op jit(solution)/shard_map/ppermute | solution.py:757
  657.7 16.9 %collective-permute-done.47 = bf16[56,3008]{1,0:T(8,128)(2,1)S(1)} collective-permute-done((bf16[56,3008]{1,0:T(8,128)(2,1)S(1)}, bf16[56,3008]{1,0:T(8,128)(2,1)S(1)}, u32[]{:S(2)}, u32[]{:S(2)}) %collective-permute-start.47) | collective-permute-done | bytes 336928 | tf_op jit(solution)/shard_map/ppermute | solution.py:717
  695.2 9.7 %collective-permute-done.37 = bf16[800,256]{1,0:T(8,128)(2,1)S(1)} collective-permute-done((bf16[800,256]{1,0:T(8,128)(2,1)S(1)}, bf16[800,256]{1,0:T(8,128)(2,1)S(1)}, u32[]{:S(2)}, u32[]{:S(2)}) %collective-permute-start.37) | collective-permute-done | bytes 409632 | tf_op jit(solution)/shard_map/ppermute | solution.py:717
  707.6 16.5 %collective-permute-done.52 = bf16[2,1,56,6464]{3,2,1,0:T(8,128)(2,1)S(1)} collective-permute-done((bf16[2,1,56,6464]{3,2,1,0:T(8,128)(2,1)S(1)}, bf16[2,1,56,6464]{3,2,1,0:T(8,128)(2,1)S(1)}, u32[]{:S(2)}, u32[]{:S(2)}) %collective-permute-start.52) | collective-permute-done | bytes 1447968 | tf_op jit(solution)/shard_map/ppermute | solution.py:757
  (402 shorter events, 346.6 us)
Async XLA Ops:
  7.2 83.3 %all-gather.4.cloned.1.call-start = ((), (), s32[]{:S(2)}) async-start(), calls=%async_computation.2 | async-start | bytes 4096000 | tf_op jit(solution)/shard_map/all_gather | solution.py:736
  7.9 248.7 %all-gather.6.cloned.1.call-start = ((), (), s32[]{:S(2)}) async-start(), calls=%async_computation.3 | async-start | bytes 4587520 | tf_op jit(solution)/shard_map/all_gather | solution.py:736
  21.9 30.2 %collective-permute-start.1 = (bf16[64,1344]{1,0:T(8,128)(2,1)S(1)}, bf16[64,1344]{1,0:T(8,128)(2,1)S(1)}, u32[]{:S(2)}, u32[]{:S(2)}) collective-permute-start(bf16[64,1344]{1,0:T(8,128)(2,1)S(1)} %get-tuple-element.288), channel_id=1, source_target_pairs={{0,2},{1,3},{2,0},{3,1},{4,6},{5,7},{6,4},{7,5},{8,10},{9,11},{10,... | collective-permute-start | bytes 516104 | tf_op jit(solution)/shard_map/ppermute | solution.py:717
  21.9 30.2 %collective-permute-start = (bf16[64,1344]{1,0:T(8,128)(2,1)S(1)}, bf16[64,1344]{1,0:T(8,128)(2,1)S(1)}, u32[]{:S(2)}, u32[]{:S(2)}) collective-permute-start(bf16[64,1344]{1,0:T(8,128)(2,1)S(1)} %get-tuple-element.289), channel_id=1, source_target_pairs={{0,1},{1,2},{2,3},{3,0},{4,5},{5,6},{6,7},{7,4},{8,9},{9,10},{10,1... | collective-permute-start | bytes 516104 | tf_op jit(solution)/shard_map/ppermute | solution.py:717
  111.9 25.8 %collective-permute-start.9 = (bf16[4,224,1344]{2,1,0:T(8,128)(2,1)S(1)}, bf16[4,224,1344]{2,1,0:T(8,128)(2,1)}, u32[]{:S(2)}, u32[]{:S(2)}) collective-permute-start(bf16[4,224,1344]{2,1,0:T(8,128)(2,1)S(1)} %pad_maximum_fusion.7), channel_id=1, source_target_pairs={{0,4},{4,0},{1,5},{5,1},{2,6},{6,2},{3,7},{7,3},{8,12},{12,8},{9,1... | collective-permute-start | bytes 7225352 | tf_op jit(solution)/shard_map/ppermute | solution.py:720
  185.3 138.5 %all-gather.8.cloned.1.call-start = ((), (), s32[]{:S(2)}) async-start(), calls=%async_computation.4 | async-start | bytes 4096000 | tf_op jit(solution)/shard_map/all_gather | solution.py:736
  259.9 163.5 %reduce-scatter.3.cloned.1.call-start = ((), (), s32[]{:S(2)}) async-start(), calls=%async_computation.5 | async-start | bytes 4096000 | tf_op jit(solution)/shard_map/reduce_scatter | solution.py:909
  361.8 257.7 %reduce-scatter.5.cloned.1.call-start = ((), (), s32[]{:S(2)}) async-start(), calls=%async_computation.6 | async-start | bytes 4096000 | tf_op jit(solution)/shard_map/reduce_scatter | solution.py:909
  411.4 35.8 %collective-permute-start.31 = (bf16[8,112,1600]{2,1,0:T(8,128)(2,1)}, bf16[8,112,1600]{2,1,0:T(8,128)(2,1)}, u32[]{:S(2)}, u32[]{:S(2)}) collective-permute-start(bf16[8,112,1600]{2,1,0:T(8,128)(2,1)} %get-tuple-element.134), channel_id=1, source_target_pairs={{0,8},{4,20},{8,0},{12,28},{16,24},{20,4},{24,16},{28,12},{1,9},{5... | collective-permute-start | bytes 8601608 | tf_op jit(solution)/shard_map/ppermute | solution.py:757
  432.3 30.6 %collective-permute-start.29 = (bf16[448,256]{1,0:T(8,128)(2,1)S(1)}, bf16[448,256]{1,0:T(8,128)(2,1)S(1)}, u32[]{:S(2)}, u32[]{:S(2)}) collective-permute-start(bf16[448,256]{1,0:T(8,128)(2,1)S(1)} %get-tuple-element.257), channel_id=1, source_target_pairs={{0,3},{1,0},{2,1},{3,2},{4,7},{5,4},{6,5},{7,6},{8,11},{9,8},{10,9... | collective-permute-start | bytes 688136 | tf_op jit(solution)/shard_map/ppermute | solution.py:717
  434.6 28.4 %collective-permute-start.28 = (bf16[448,256]{1,0:T(8,128)(2,1)S(1)}, bf16[448,256]{1,0:T(8,128)(2,1)S(1)}, u32[]{:S(2)}, u32[]{:S(2)}) collective-permute-start(bf16[448,256]{1,0:T(8,128)(2,1)S(1)} %get-tuple-element.258), channel_id=1, source_target_pairs={{0,2},{1,3},{2,0},{3,1},{4,6},{5,7},{6,4},{7,5},{8,10},{9,11},{10,... | collective-permute-start | bytes 688136 | tf_op jit(solution)/shard_map/ppermute | solution.py:717
  435.0 28.0 %collective-permute-start.27 = (bf16[448,256]{1,0:T(8,128)(2,1)S(1)}, bf16[448,256]{1,0:T(8,128)(2,1)S(1)}, u32[]{:S(2)}, u32[]{:S(2)}) collective-permute-start(bf16[448,256]{1,0:T(8,128)(2,1)S(1)} %get-tuple-element.259), channel_id=1, source_target_pairs={{0,1},{1,2},{2,3},{3,0},{4,5},{5,6},{6,7},{7,4},{8,9},{9,10},{10,1... | collective-permute-start | bytes 688136 | tf_op jit(solution)/shard_map/ppermute | solution.py:717
  455.7 63.3 %collective-permute-start.32 = (bf16[8,56,1600]{2,1,0:T(8,128)(2,1)}, bf16[8,56,1600]{2,1,0:T(8,128)(2,1)}, u32[]{:S(2)}, u32[]{:S(2)}) collective-permute-start(bf16[8,56,1600]{2,1,0:T(8,128)(2,1)} %get-tuple-element.144), channel_id=1, source_target_pairs={{0,16},{4,12},{8,24},{12,4},{16,0},{20,28},{24,8},{28,20},{1,17},{... | collective-permute-start | bytes 4300808 | tf_op jit(solution)/shard_map/ppermute | solution.py:757
  463.0 81.2 %collective-permute-start.40 = (bf16[4,224,1600]{2,1,0:T(8,128)(2,1)}, bf16[4,224,1600]{2,1,0:T(8,128)(2,1)}, u32[]{:S(2)}, u32[]{:S(2)}) collective-permute-start(bf16[4,224,1600]{2,1,0:T(8,128)(2,1)} %get-tuple-element.152), channel_id=1, source_target_pairs={{0,4},{4,0},{1,5},{5,1},{2,6},{6,2},{3,7},{7,3},{8,12},{12,8},{9,1... | collective-permute-start | bytes 8601608 | tf_op jit(solution)/shard_map/ppermute | solution.py:720
  467.4 24.0 %collective-permute-start.30 = (bf16[1600,256]{1,0:T(8,128)(2,1)S(1)}, bf16[1600,256]{1,0:T(8,128)(2,1)S(1)}, u32[]{:S(2)}, u32[]{:S(2)}) collective-permute-start(bf16[1600,256]{1,0:T(8,128)(2,1)S(1)} %copy-done.26), channel_id=1, source_target_pairs={{0,3},{1,0},{2,1},{3,2},{4,7},{5,4},{6,5},{7,6},{8,11},{9,8},{10,9... | collective-permute-start | bytes 2457608 | tf_op jit(solution)/shard_map/ppermute | solution.py:717
  518.9 25.3 %collective-permute-start.41 = (bf16[4,224,1344]{2,1,0:T(8,128)(2,1)}, bf16[4,224,1344]{2,1,0:T(8,128)(2,1)}, u32[]{:S(2)}, u32[]{:S(2)}) collective-permute-start(bf16[4,224,1344]{2,1,0:T(8,128)(2,1)} %get-tuple-element.156), channel_id=1, source_target_pairs={{0,4},{4,0},{1,5},{5,1},{2,6},{6,2},{3,7},{7,3},{8,12},{12,8},{9,1... | collective-permute-start | bytes 7225352 | tf_op jit(solution)/shard_map/ppermute | solution.py:720
  552.0 57.9 %collective-permute-start.42 = (bf16[4,112,3008]{2,1,0:T(8,128)(2,1)}, bf16[4,112,3008]{2,1,0:T(8,128)(2,1)S(1)}, u32[]{:S(2)}, u32[]{:S(2)}) collective-permute-start(bf16[4,112,3008]{2,1,0:T(8,128)(2,1)} %get-tuple-element.158), channel_id=1, source_target_pairs={{0,8},{4,20},{8,0},{12,28},{16,24},{20,4},{24,16},{28,12},{1,9},{5... | collective-permute-start | bytes 8085512 | tf_op jit(solution)/shard_map/ppermute | solution.py:757
  554.2 53.7 %collective-permute-start.49 = (bf16[2,4,56,1600]{3,2,1,0:T(8,128)(2,1)S(1)}, bf16[2,4,56,1600]{3,2,1,0:T(8,128)(2,1)S(1)}, u32[]{:S(2)}, u32[]{:S(2)}) collective-permute-start(bf16[2,4,56,1600]{3,2,1,0:T(8,128)(2,1)S(1)} %pad_maximum_fusion.11), channel_id=1, source_target_pairs={{0,8},{4,20},{8,0},{12,28},{16,24},{20,4},{24,16},{28,12},{1,9},{5... | collective-permute-start | bytes 4300808 | tf_op jit(solution)/shard_map/ppermute | solution.py:757
  609.9 37.1 %collective-permute-start.50 = (bf16[4,4,56,1600]{3,2,1,0:T(8,128)(2,1)}, bf16[4,4,56,1600]{3,2,1,0:T(8,128)(2,1)}, u32[]{:S(2)}, u32[]{:S(2)}) collective-permute-start(bf16[4,4,56,1600]{3,2,1,0:T(8,128)(2,1)} %pad_maximum_fusion.6.mine_ref), channel_id=1, source_target_pairs={{0,4},{4,0},{1,5},{5,1},{2,6},{6,2},{3,7},{7,3},{8,12},{12,8},{9,1... | collective-permute-start | bytes 8601608 | tf_op jit(solution)/shard_map/ppermute | solution.py:720
  619.5 21.9 %collective-permute-start.36 = (bf16[800,256]{1,0:T(8,128)(2,1)}, bf16[800,256]{1,0:T(8,128)(2,1)S(1)}, u32[]{:S(2)}, u32[]{:S(2)}) collective-permute-start(bf16[800,256]{1,0:T(8,128)(2,1)} %get-tuple-element.147), channel_id=1, source_target_pairs={{0,2},{1,3},{2,0},{3,1},{4,6},{5,7},{6,4},{7,5},{8,10},{9,11},{10,... | collective-permute-start | bytes 1228808 | tf_op jit(solution)/shard_map/ppermute | solution.py:717
  645.7 28.9 %collective-permute-start.47 = (bf16[56,3008]{1,0:T(8,128)(2,1)S(1)}, bf16[56,3008]{1,0:T(8,128)(2,1)S(1)}, u32[]{:S(2)}, u32[]{:S(2)}) collective-permute-start(bf16[56,3008]{1,0:T(8,128)(2,1)S(1)} %get-tuple-element.248), channel_id=1, source_target_pairs={{0,2},{1,3},{2,0},{3,1},{4,6},{5,7},{6,4},{7,5},{8,10},{9,11},{10,... | collective-permute-start | bytes 1010696 | tf_op jit(solution)/shard_map/ppermute | solution.py:717
  645.7 28.9 %collective-permute-start.46 = (bf16[56,3008]{1,0:T(8,128)(2,1)S(1)}, bf16[56,3008]{1,0:T(8,128)(2,1)S(1)}, u32[]{:S(2)}, u32[]{:S(2)}) collective-permute-start(bf16[56,3008]{1,0:T(8,128)(2,1)S(1)} %get-tuple-element.249), channel_id=1, source_target_pairs={{0,1},{1,2},{2,3},{3,0},{4,5},{5,6},{6,7},{7,4},{8,9},{9,10},{10,1... | collective-permute-start | bytes 1010696 | tf_op jit(solution)/shard_map/ppermute | solution.py:717
  646.3 34.7 %collective-permute-start.44 = (bf16[2,1,56,6400]{3,2,1,0:T(8,128)(2,1)}, bf16[2,1,56,6400]{3,2,1,0:T(8,128)(2,1)}, u32[]{:S(2)}, u32[]{:S(2)}) collective-permute-start(bf16[2,1,56,6400]{3,2,1,0:T(8,128)(2,1)} %pad_maximum_fusion.13), channel_id=1, source_target_pairs={{0,8},{4,20},{8,0},{12,28},{16,24},{20,4},{24,16},{28,12},{1,9},{5... | collective-permute-start | bytes 4300808 | tf_op jit(solution)/shard_map/ppermute | solution.py:757
  706.3 28.0 %collective-permute-start.45 = (bf16[4,1,56,6400]{3,2,1,0:T(8,128)(2,1)}, bf16[4,1,56,6400]{3,2,1,0:T(8,128)(2,1)}, u32[]{:S(2)}, u32[]{:S(2)}) collective-permute-start(bf16[4,1,56,6400]{3,2,1,0:T(8,128)(2,1)} %constant_dynamic-update-slice_fusion.mine_ref), channel_id=1, source_target_pairs={{0,4},{4,0},{1,5},{5,1},{2,6},{6,2},{3,7},{7,3},{8,12},{12,8},{9,1... | collective-permute-start | bytes 8601608 | tf_op jit(solution)/shard_map/ppermute | solution.py:720
  (93 other events, 1064.6 us)
Sparse Core Ops, SparseCore 0:
  9.6 80.8 all-gather.3
  185.4 71.0 all-gather.5
  260.1 63.3 all-gather.7
  361.9 61.4 reduce-scatter.2
  542.1 60.1 reduce-scatter.4

commit v4 on v3

--- a/solution.py
+++ b/solution.py
@@ -971,7 +971,6 @@
         [g_attn_gain[:, 0], g_attn_shift[:, 0], place(sums[0]), place(sums[2])], 3 * wc
     )
     mix_sum = sum_start(normed_a, g_mixed_rows, small_mix)
-    down_mine = spread_far(down_near)
 
     skip = -(-width // BLK) * BLK
     if square:
@@ -986,7 +985,8 @@
     wide_own = after(wide_own, e_a_own, *ffn_top)
     wide_got = exchange(wide_own)
     up_mine = spread_far(after(up_near, wide_own))
-    g_down_full, down_small = spread_last(down_mine, [(0, width)], wide_own)
+    down_mine = spread_far(after(down_near, wide_own))
+    g_down_full, down_small = spread_last(down_mine, [(0, width)])
     g_up_full, up_small = spread_last(up_mine, [(0, shards * ff_own)])
     columns = []
     for j in range(3):
@@ -996,9 +996,9 @@
     mix_row = with_sum(jnp.concatenate(columns, axis=-1), wide_got[:, :, skip:])
     out_row = jnp.sum(wide_got[:, :, :skip].astype(F32), axis=0).astype(BF)
     wide_row = jnp.concatenate([out_row[None], mix_row], axis=-1)
-    wide_near = after(spread_near(after(wide_row, g_down_full, up_mine)), *ffn_low)
+    wide_near = spread_near(after(wide_row, up_mine))
     g_out_full, out_small, g_mix_full, mix_small = spread_last(
-        spread_far(wide_near), [(0, width), (skip, skip + 3 * width)], g_up_full
+        spread_far(wide_near), [(0, width), (skip, skip + 3 * width)], g_up_full, g_down_full, *ffn_low
     )
 
     block_out = (middle_own + ffn_own + small[:, 7:8]).astype(BF).T

time: 770 us -> 762 us (0.990)
  waiting for transfers between devices: 328 us -> 318 us
    ppermute x16, waiting for transfers between devices: 131 us -> 120 us  [flip(): return lax.ppermute(x, ('chip', 'core'), pairs)]
    unnamed x118 -> x110, local copies, waits for them, and re-layouts: 18 us -> 17.3 us
  transfers between devices with their start and end apart: 59 -> 59, of which waited for: 31 -> 33; matrix products, arithmetic and copies ran while one was open for 18% -> 18% of each run, Pallas kernels for 20% -> 21%
where the time goes in v4:
time: 762 us; the launch traced here: 754 us
  waiting for transfers between devices  318 us (42%)
  Pallas kernels  193 us (25%)
  local copies, waits for them, and re-layouts  62.4 us (8%)
  starting transfers between devices  62 us (8%)
  matrix products  54.8 us (7%)
  other arithmetic  48.2 us (6%)
  between operations  16.5 us (2%)
    pallas_call x21, Pallas kernels, call(): pl.pallas_call(kernel, out_shape=[jax.ShapeDtypeStruct(shape, dtype) for...  193 us
    ppermute x16, waiting for transfers between devices, flip(): return lax.ppermute(x, ('chip', 'core'), pairs)  120 us
    ppermute x22, waiting for transfers between devices, to_next(): lax.ppermute(x, 'shard', [(i, (i + t) % shards) for i in range(shards)])  96.6 us
    all_gather x3, waiting for transfers between devices, over_shard(): return lax.all_gather(x, 'shard', axis=0, tiled=True)  82.8 us
    ppermute x22, starting transfers between devices, to_next(): lax.ppermute(x, 'shard', [(i, (i + t) % shards) for i in range(shards)])  35.9 us
    dot_general x4, matrix products, dot_tn(): lax.dot_general(a, b, (((0,), (0,)), ((), ())), preferred_element_type=F32)  33.4 us
    ppermute x16, starting transfers between devices, flip(): return lax.ppermute(x, ('chip', 'core'), pairs)  22.8 us
    dot_general x2, matrix products, dot_nn(): lax.dot_general(a, b, (((1,), (0,)), ((), ())), preferred_element_type=F32)  21.5 us
  transfers between devices with their start and end apart: 59, of which 33 were waited for; matrix products, arithmetic and copies ran while one was open for 18% of the time, Pallas kernels for 21%

profile of v4, /device:TPU:0, one launch (start us, length us, event | category | flops | bytes accessed | tf_op | source)
XLA Modules:
  0.0 754.3 jit_solution(12678143814037551530)
XLA Ops:
  30.7 21.4 %collective-permute-done.1 = bf16[64,1344]{1,0:T(8,128)(2,1)S(1)} collective-permute-done((bf16[64,1344]{1,0:T(8,128)(2,1)S(1)}, bf16[64,1344]{1,0:T(8,128)(2,1)S(1)}, u32[]{:S(2)}, u32[]{:S(2)}) %collective-permute-start.1) | collective-permute-done | bytes 172064 | tf_op jit(solution)/shard_map/ppermute | solution.py:717
  67.0 23.5 %all-gather.4.cloned.1.call-done.h0_ref.h1_ref = bf16[6400,256]{1,0:T(8,128)(2,1)} async-done(((bf16[1600,256]{1,0:T(8,128)(2,1)}), bf16[6400,256]{1,0:T(8,128)(2,1)}) %all-gather.4.cloned.1.call-update) | async-done | bytes 3276816 | tf_op jit(solution)/shard_map/all_gather | solution.py:736
  96.1 8.8 %shard_map.280 = (bf16[1600,1024]{1,0:T(8,128)(2,1)}, bf16[1600,1024]{1,0:T(8,128)(2,1)}) custom-call(s32[8]{0:T(128)} %select_reduce_fusion.tab_ref, bf16[6400,256]{1,0:T(8,128)(2,1)} %all-gather.4.cloned.1.call-done.h0_ref.h1_ref, bf16[6400,256]{1,0:T(8,128)(2,1)} %all-gather.4.cloned.1.call-done.h0_ref.h1_ref, f32[1600,8]{1,0:T(8,128)} %bitcast.187), custom_call_target="tpu_custom_call" | custom-call | flops 20000000000 | bytes 1024 | tf_op jit(solution)/shard_map/pallas_call | solution.py:47
  120.8 13.1 %collective-permute-done.11 = bf16[56,1600]{1,0:T(8,128)(2,1)S(1)} collective-permute-done((bf16[56,1600]{1,0:T(8,128)(2,1)S(1)}, bf16[56,1600]{1,0:T(8,128)(2,1)S(1)}, u32[]{:S(2)}, u32[]{:S(2)}) %collective-permute-start.11) | collective-permute-done | bytes 179232 | tf_op jit(solution)/shard_map/ppermute | solution.py:717
  165.4 19.9 %shard_map.281 = (f32[448,1024]{1,0:T(8,128)}, bf16[448,1024]{1,0:T(8,128)(2,1)}, f32[7,1,1024]{2,1,0:T(1,128)}) custom-call(s32[1]{0:T(128)} %bitcast.253, bf16[1344,1024]{1,0:T(8,128)(2,1)} %add_convert_fusion.1.q_ref.k_ref.v_ref, bf16[1344,1024]{1,0:T(8,128)(2,1)} %add_convert_fusion.1.q_ref.k_ref.v_ref, ...), custom_call_target="tpu_custom_call" | custom-call | flops 20000000000 | bytes 1024 | tf_op jit(solution)/shard_map/pallas_call | solution.py:47
  187.2 9.8 %collective-permute-done.15 = bf16[4,56,1600]{2,1,0:T(8,128)(2,1)S(1)} collective-permute-done((bf16[4,56,1600]{2,1,0:T(8,128)(2,1)S(1)}, bf16[4,56,1600]{2,1,0:T(8,128)(2,1)S(1)}, u32[]{:S(2)}, u32[]{:S(2)}) %collective-permute-start.15) | collective-permute-done | bytes 716832 | tf_op jit(solution)/shard_map/ppermute | solution.py:757
  197.3 59.3 %all-gather.6.cloned.1.call-done = bf16[1792,1024]{1,0:T(8,128)(2,1)} async-done(((bf16[448,1024]{1,0:T(8,128)(2,1)}), bf16[1792,1024]{1,0:T(8,128)(2,1)}) %all-gather.6.cloned.1.call-update) | async-done | bytes 3670032 | tf_op jit(solution)/shard_map/all_gather | solution.py:736
  264.0 12.2 %collective-permute-done.16 = bf16[4,112,1600]{2,1,0:T(8,128)(2,1)} collective-permute-done((bf16[4,112,1600]{2,1,0:T(8,128)(2,1)S(1)}, bf16[4,112,1600]{2,1,0:T(8,128)(2,1)}, u32[]{:S(2)}, u32[]{:S(2)}) %collective-permute-start.16) | collective-permute-done | bytes 1433632 | tf_op jit(solution)/shard_map/ppermute | solution.py:757
  294.1 9.8 %multiply_convert_fusion = (bf16[1600,1024]{1,0:T(8,128)(2,1)S(1)}, f32[1600,1024]{1,0:T(8,128)}) fusion(f32[1600]{0:T(1024)S(1)} %convert_element_type.121, bf16[1600,1600]{1,0:T(8,128)(2,1)S(1)} %bitcast.204, bf16[1600,1024]{1,0:T(8,128)(2,1)S(1)} %get-tuple-element.186.a_ref), kind=kOutput, calls=%fused_computation.11 | convolution fusion | flops 5259264000 | bytes 18233600 | tf_op jit(solution)/shard_map/dot_general | solution.py:26
  305.7 10.2 %fusion.8.x_ref = bf16[1600,1024]{1,0:T(8,128)(2,1)} fusion(bf16[1600,1024]{1,0:T(8,128)(2,1)S(1)} %get-tuple-element.317.a_ref, bf16[1600,1600]{1,0:T(8,128)(2,1)} %param.32), kind=kOutput, calls=%fused_computation.25 | convolution fusion | flops 5244518400 | bytes 11673600 | tf_op jit(solution)/shard_map/dot_general | solution.py:26
  329.3 13.5 %fusion.7.b_ref = bf16[1600,1024]{1,0:T(8,128)(2,1)S(1)} fusion(f32[1600,1024]{1,0:T(8,128)} %get-tuple-element.318, bf16[1600,1600]{1,0:T(8,128)(2,1)} %param.32, bf16[1600,1024]{1,0:T(8,128)(2,1)} %shard_map.283.b_ref, f32[1600]{0:T(1024)S(1)} %convert_element_type.121), kind=kOutput, calls=%fused_computation.9 | convolution fusion | flops 5275648000 | bytes 18233600 | tf_op jit(solution)/shard_map/dot_general | solution.py:30
  364.6 12.0 %shard_map.285 = (bf16[4,224,1600]{2,1,0:T(8,128)(2,1)}, bf16[224,1600]{1,0:T(8,128)(2,1)}, bf16[224,1600]{1,0:T(8,128)(2,1)}, bf16[224,1600]{1,0:T(8,128)(2,1)}, bf16[224,1600]{1,0:T(8,128)(2,1)}) custom-call(s32[1]{0:T(128)} %bitcast.45.core_ref, bf16[1600,1024]{1,0:T(8,128)(2,1)} %copy-done.17, bf16[1600,1024]{1,0:T(8,128)(2,1)} %shard_map.283.b_ref, ...), custom_call_target="tpu_custom_call" | custom-call | flops 1024 | bytes 1024 | tf_op jit(solution)/shard_map/pallas_call | solution.py:47
  378.2 11.9 %shard_map.286 = (bf16[4,224,1600]{2,1,0:T(8,128)(2,1)}, bf16[224,1600]{1,0:T(8,128)(2,1)}, bf16[224,1600]{1,0:T(8,128)(2,1)}, bf16[224,1600]{1,0:T(8,128)(2,1)}, bf16[224,1600]{1,0:T(8,128)(2,1)}) custom-call(s32[1]{0:T(128)} %bitcast.45.core_ref, bf16[1600,1024]{1,0:T(8,128)(2,1)} %copy-done.4, bf16[1600,1024]{1,0:T(8,128)(2,1)} %copy-done.5, ...), custom_call_target="tpu_custom_call" | custom-call | flops 1024 | bytes 1024 | tf_op jit(solution)/shard_map/pallas_call | solution.py:47
  400.8 10.4 %shard_map.287 = (bf16[8,112,1600]{2,1,0:T(8,128)(2,1)}, bf16[8,112,1600]{2,1,0:T(8,128)(2,1)}) custom-call(s32[1]{0:T(128)} %bitcast.44.bit_ref, bf16[4,224,1600]{2,1,0:T(8,128)(2,1)} %get-tuple-element.114.refs_0_, bf16[224,1600]{1,0:T(8,128)(2,1)} %copy-done.35, bf16[224,1600]{1,0:T(8,128)(2,1)} %copy-done.36, bf16[224,1600]{1,0:T(8,128)(2,1)} %copy-done.37, ...), custom_call_target="tpu_custom_call" | custom-call | flops 1024 | bytes 1024 | tf_op jit(solution)/shard_map/pallas_call | solution.py:47
  468.8 19.6 %shard_map.292 = bf16[3,448,1024]{2,1,0:T(8,128)(2,1)} custom-call(s32[1]{0:T(128)} %bitcast.254, bf16[1344,1024]{1,0:T(8,128)(2,1)} %add_convert_fusion.1.q_ref.k_ref.v_ref, bf16[1344,1024]{1,0:T(8,128)(2,1)} %add_convert_fusion.1.q_ref.k_ref.v_ref, bf16[1344,1024]{1,0:T(8,128)(2,1)} %add_convert_fusion.1.q_ref.k_ref.v_ref, ...), custom_call_target="tpu_custom_call" | custom-call | flops 20000000000 | bytes 1024 | tf_op jit(solution)/shard_map/pallas_call | solution.py:47
  491.2 14.1 %shard_map.293 = (bf16[6400,256]{1,0:T(8,128)(2,1)}, f32[1600,1]{1,0:T(8,128)}, f32[1600,1]{1,0:T(8,128)}) custom-call(s32[8]{0:T(128)} %select_reduce_fusion.tab_ref, bf16[1344,1024]{1,0:T(8,128)(2,1)} %bitcast.198, bf16[6400,256]{1,0:T(8,128)(2,1)} %all-gather.4.cloned.1.call-done.h0_ref.h1_ref, ...), custom_call_target="tpu_custom_call" | custom-call | flops 20000000000 | bytes 1024 | tf_op jit(solution)/shard_map/pallas_call | solution.py:47
  509.1 9.6 %shard_map.295 = (bf16[4,224,1344]{2,1,0:T(8,128)(2,1)}, bf16[4,224,1344]{2,1,0:T(8,128)(2,1)}) custom-call(s32[1]{0:T(128)} %bitcast.45.core_ref, bf16[1600,1024]{1,0:T(8,128)(2,1)} %get-tuple-element.98.a_ref, bf16[1344,1024]{1,0:T(8,128)(2,1)} %bitcast.199, f32[4,8,1344]{2,1,0:T(8,128)} %pad.84.small_ref), custom_call_target="tpu_custom_call" | custom-call | flops 1024 | bytes 1024 | tf_op jit(solution)/shard_map/pallas_call | solution.py:47
  527.8 11.4 %collective-permute-done.34 = bf16[56,1600]{1,0:T(8,128)(2,1)S(1)} collective-permute-done((bf16[56,1600]{1,0:T(8,128)(2,1)S(1)}, bf16[56,1600]{1,0:T(8,128)(2,1)S(1)}, u32[]{:S(2)}, u32[]{:S(2)}) %collective-permute-start.34) | collective-permute-done | bytes 179232 | tf_op jit(solution)/shard_map/ppermute | solution.py:717
  553.1 18.8 %collective-permute-done.38 = bf16[1,56,6400]{2,1,0:T(8,128)(2,1)S(1)} collective-permute-done((bf16[1,56,6400]{2,1,0:T(8,128)(2,1)S(1)}, bf16[1,56,6400]{2,1,0:T(8,128)(2,1)S(1)}, u32[]{:S(2)}, u32[]{:S(2)}) %collective-permute-start.38) | collective-permute-done | bytes 716832 | tf_op jit(solution)/shard_map/ppermute | solution.py:757
  573.1 17.4 %collective-permute-done.42.y_ref = bf16[4,112,3008]{2,1,0:T(8,128)(2,1)S(1)} collective-permute-done((bf16[4,112,3008]{2,1,0:T(8,128)(2,1)}, bf16[4,112,3008]{2,1,0:T(8,128)(2,1)S(1)}, u32[]{:S(2)}, u32[]{:S(2)}) %collective-permute-start.42) | collective-permute-done | bytes 2695200 | tf_op jit(solution)/shard_map/ppermute | solution.py:757
  604.6 11.4 %collective-permute-done.43 = bf16[4,56,3008]{2,1,0:T(8,128)(2,1)} collective-permute-done((bf16[4,56,3008]{2,1,0:T(8,128)(2,1)}, bf16[4,56,3008]{2,1,0:T(8,128)(2,1)}, u32[]{:S(2)}, u32[]{:S(2)}) %collective-permute-start.43) | collective-permute-done | bytes 1347616 | tf_op jit(solution)/shard_map/ppermute | solution.py:757
  635.2 20.2 %collective-permute-done.49 = bf16[56,3008]{1,0:T(8,128)(2,1)S(1)} collective-permute-done((bf16[56,3008]{1,0:T(8,128)(2,1)S(1)}, bf16[56,3008]{1,0:T(8,128)(2,1)S(1)}, u32[]{:S(2)}, u32[]{:S(2)}) %collective-permute-start.49) | collective-permute-done | bytes 336928 | tf_op jit(solution)/shard_map/ppermute | solution.py:717
  666.3 17.4 %collective-permute-done.51 = bf16[1,56,6464]{2,1,0:T(8,128)(2,1)S(1)} collective-permute-done((bf16[1,56,6464]{2,1,0:T(8,128)(2,1)S(1)}, bf16[1,56,6464]{2,1,0:T(8,128)(2,1)S(1)}, u32[]{:S(2)}, u32[]{:S(2)}) %collective-permute-start.51) | collective-permute-done | bytes 724000 | tf_op jit(solution)/shard_map/ppermute | solution.py:757
  695.2 9.6 %collective-permute-done.52 = bf16[2,1,56,6464]{3,2,1,0:T(8,128)(2,1)S(1)} collective-permute-done((bf16[2,1,56,6464]{3,2,1,0:T(8,128)(2,1)S(1)}, bf16[2,1,56,6464]{3,2,1,0:T(8,128)(2,1)S(1)}, u32[]{:S(2)}, u32[]{:S(2)}) %collective-permute-start.52) | collective-permute-done | bytes 1447968 | tf_op jit(solution)/shard_map/ppermute | solution.py:757
  (394 shorter events, 352.5 us)
Async XLA Ops:
  7.2 83.3 %all-gather.4.cloned.1.call-start = ((), (), s32[]{:S(2)}) async-start(), calls=%async_computation.2 | async-start | bytes 4096000 | tf_op jit(solution)/shard_map/all_gather | solution.py:736
  7.9 248.7 %all-gather.6.cloned.1.call-start = ((), (), s32[]{:S(2)}) async-start(), calls=%async_computation.3 | async-start | bytes 4587520 | tf_op jit(solution)/shard_map/all_gather | solution.py:736
  21.9 30.2 %collective-permute-start.1 = (bf16[64,1344]{1,0:T(8,128)(2,1)S(1)}, bf16[64,1344]{1,0:T(8,128)(2,1)S(1)}, u32[]{:S(2)}, u32[]{:S(2)}) collective-permute-start(bf16[64,1344]{1,0:T(8,128)(2,1)S(1)} %get-tuple-element.286), channel_id=1, source_target_pairs={{0,2},{1,3},{2,0},{3,1},{4,6},{5,7},{6,4},{7,5},{8,10},{9,11},{10,... | collective-permute-start | bytes 516104 | tf_op jit(solution)/shard_map/ppermute | solution.py:717
  21.9 30.2 %collective-permute-start = (bf16[64,1344]{1,0:T(8,128)(2,1)S(1)}, bf16[64,1344]{1,0:T(8,128)(2,1)S(1)}, u32[]{:S(2)}, u32[]{:S(2)}) collective-permute-start(bf16[64,1344]{1,0:T(8,128)(2,1)S(1)} %get-tuple-element.287), channel_id=1, source_target_pairs={{0,1},{1,2},{2,3},{3,0},{4,5},{5,6},{6,7},{7,4},{8,9},{9,10},{10,1... | collective-permute-start | bytes 516104 | tf_op jit(solution)/shard_map/ppermute | solution.py:717
  111.9 25.8 %collective-permute-start.9 = (bf16[4,224,1344]{2,1,0:T(8,128)(2,1)S(1)}, bf16[4,224,1344]{2,1,0:T(8,128)(2,1)}, u32[]{:S(2)}, u32[]{:S(2)}) collective-permute-start(bf16[4,224,1344]{2,1,0:T(8,128)(2,1)S(1)} %pad_maximum_fusion.7), channel_id=1, source_target_pairs={{0,4},{4,0},{1,5},{5,1},{2,6},{6,2},{3,7},{7,3},{8,12},{12,8},{9,1... | collective-permute-start | bytes 7225352 | tf_op jit(solution)/shard_map/ppermute | solution.py:720
  185.3 138.5 %all-gather.8.cloned.1.call-start = ((), (), s32[]{:S(2)}) async-start(), calls=%async_computation.4 | async-start | bytes 4096000 | tf_op jit(solution)/shard_map/all_gather | solution.py:736
  259.9 163.5 %reduce-scatter.3.cloned.1.call-start = ((), (), s32[]{:S(2)}) async-start(), calls=%async_computation.5 | async-start | bytes 4096000 | tf_op jit(solution)/shard_map/reduce_scatter | solution.py:909
  361.8 238.3 %reduce-scatter.5.cloned.1.call-start = ((), (), s32[]{:S(2)}) async-start(), calls=%async_computation.6 | async-start | bytes 4096000 | tf_op jit(solution)/shard_map/reduce_scatter | solution.py:909
  411.2 35.8 %collective-permute-start.31 = (bf16[8,112,1600]{2,1,0:T(8,128)(2,1)}, bf16[8,112,1600]{2,1,0:T(8,128)(2,1)}, u32[]{:S(2)}, u32[]{:S(2)}) collective-permute-start(bf16[8,112,1600]{2,1,0:T(8,128)(2,1)} %get-tuple-element.133), channel_id=1, source_target_pairs={{0,8},{4,20},{8,0},{12,28},{16,24},{20,4},{24,16},{28,12},{1,9},{5... | collective-permute-start | bytes 8601608 | tf_op jit(solution)/shard_map/ppermute | solution.py:757
  433.2 29.7 %collective-permute-start.29 = (bf16[448,256]{1,0:T(8,128)(2,1)}, bf16[448,256]{1,0:T(8,128)(2,1)S(1)}, u32[]{:S(2)}, u32[]{:S(2)}) collective-permute-start(bf16[448,256]{1,0:T(8,128)(2,1)} %get-tuple-element.255), channel_id=1, source_target_pairs={{0,3},{1,0},{2,1},{3,2},{4,7},{5,4},{6,5},{7,6},{8,11},{9,8},{10,9... | collective-permute-start | bytes 688136 | tf_op jit(solution)/shard_map/ppermute | solution.py:717
  435.3 27.5 %collective-permute-start.28 = (bf16[448,256]{1,0:T(8,128)(2,1)}, bf16[448,256]{1,0:T(8,128)(2,1)S(1)}, u32[]{:S(2)}, u32[]{:S(2)}) collective-permute-start(bf16[448,256]{1,0:T(8,128)(2,1)} %get-tuple-element.256), channel_id=1, source_target_pairs={{0,2},{1,3},{2,0},{3,1},{4,6},{5,7},{6,4},{7,5},{8,10},{9,11},{10,... | collective-permute-start | bytes 688136 | tf_op jit(solution)/shard_map/ppermute | solution.py:717
  435.7 27.2 %collective-permute-start.27 = (bf16[448,256]{1,0:T(8,128)(2,1)}, bf16[448,256]{1,0:T(8,128)(2,1)S(1)}, u32[]{:S(2)}, u32[]{:S(2)}) collective-permute-start(bf16[448,256]{1,0:T(8,128)(2,1)} %get-tuple-element.257), channel_id=1, source_target_pairs={{0,1},{1,2},{2,3},{3,0},{4,5},{5,6},{6,7},{7,4},{8,9},{9,10},{10,1... | collective-permute-start | bytes 688136 | tf_op jit(solution)/shard_map/ppermute | solution.py:717
  455.6 63.4 %collective-permute-start.32 = (bf16[8,56,1600]{2,1,0:T(8,128)(2,1)}, bf16[8,56,1600]{2,1,0:T(8,128)(2,1)S(1)}, u32[]{:S(2)}, u32[]{:S(2)}) collective-permute-start(bf16[8,56,1600]{2,1,0:T(8,128)(2,1)} %get-tuple-element.143), channel_id=1, source_target_pairs={{0,16},{4,12},{8,24},{12,4},{16,0},{20,28},{24,8},{28,20},{1,17},{... | collective-permute-start | bytes 4300808 | tf_op jit(solution)/shard_map/ppermute | solution.py:757
  462.9 80.2 %collective-permute-start.40 = (bf16[4,224,1600]{2,1,0:T(8,128)(2,1)}, bf16[4,224,1600]{2,1,0:T(8,128)(2,1)}, u32[]{:S(2)}, u32[]{:S(2)}) collective-permute-start(bf16[4,224,1600]{2,1,0:T(8,128)(2,1)} %get-tuple-element.151), channel_id=1, source_target_pairs={{0,4},{4,0},{1,5},{5,1},{2,6},{6,2},{3,7},{7,3},{8,12},{12,8},{9,1... | collective-permute-start | bytes 8601608 | tf_op jit(solution)/shard_map/ppermute | solution.py:720
  467.2 24.0 %collective-permute-start.30 = (bf16[1600,256]{1,0:T(8,128)(2,1)S(1)}, bf16[1600,256]{1,0:T(8,128)(2,1)}, u32[]{:S(2)}, u32[]{:S(2)}) collective-permute-start(bf16[1600,256]{1,0:T(8,128)(2,1)S(1)} %copy-done.27), channel_id=1, source_target_pairs={{0,3},{1,0},{2,1},{3,2},{4,7},{5,4},{6,5},{7,6},{8,11},{9,8},{10,9... | collective-permute-start | bytes 2457608 | tf_op jit(solution)/shard_map/ppermute | solution.py:717
  518.7 24.4 %collective-permute-start.41 = (bf16[4,224,1344]{2,1,0:T(8,128)(2,1)}, bf16[4,224,1344]{2,1,0:T(8,128)(2,1)}, u32[]{:S(2)}, u32[]{:S(2)}) collective-permute-start(bf16[4,224,1344]{2,1,0:T(8,128)(2,1)} %get-tuple-element.155), channel_id=1, source_target_pairs={{0,4},{4,0},{1,5},{5,1},{2,6},{6,2},{3,7},{7,3},{8,12},{12,8},{9,1... | collective-permute-start | bytes 7225352 | tf_op jit(solution)/shard_map/ppermute | solution.py:720
  551.0 39.5 %collective-permute-start.42 = (bf16[4,112,3008]{2,1,0:T(8,128)(2,1)}, bf16[4,112,3008]{2,1,0:T(8,128)(2,1)S(1)}, u32[]{:S(2)}, u32[]{:S(2)}) collective-permute-start(bf16[4,112,3008]{2,1,0:T(8,128)(2,1)} %get-tuple-element.157), channel_id=1, source_target_pairs={{0,8},{4,20},{8,0},{12,28},{16,24},{20,4},{24,16},{28,12},{1,9},{5... | collective-permute-start | bytes 8085512 | tf_op jit(solution)/shard_map/ppermute | solution.py:757
  626.7 28.7 %collective-permute-start.49 = (bf16[56,3008]{1,0:T(8,128)(2,1)S(1)}, bf16[56,3008]{1,0:T(8,128)(2,1)S(1)}, u32[]{:S(2)}, u32[]{:S(2)}) collective-permute-start(bf16[56,3008]{1,0:T(8,128)(2,1)S(1)} %get-tuple-element.246), channel_id=1, source_target_pairs={{0,2},{1,3},{2,0},{3,1},{4,6},{5,7},{6,4},{7,5},{8,10},{9,11},{10,... | collective-permute-start | bytes 1010696 | tf_op jit(solution)/shard_map/ppermute | solution.py:717
  626.7 28.7 %collective-permute-start.48 = (bf16[56,3008]{1,0:T(8,128)(2,1)S(1)}, bf16[56,3008]{1,0:T(8,128)(2,1)S(1)}, u32[]{:S(2)}, u32[]{:S(2)}) collective-permute-start(bf16[56,3008]{1,0:T(8,128)(2,1)S(1)} %get-tuple-element.247), channel_id=1, source_target_pairs={{0,1},{1,2},{2,3},{3,0},{4,5},{5,6},{6,7},{7,4},{8,9},{9,10},{10,1... | collective-permute-start | bytes 1010696 | tf_op jit(solution)/shard_map/ppermute | solution.py:717
  627.3 34.5 %collective-permute-start.44 = (bf16[2,1,56,6400]{3,2,1,0:T(8,128)(2,1)}, bf16[2,1,56,6400]{3,2,1,0:T(8,128)(2,1)}, u32[]{:S(2)}, u32[]{:S(2)}) collective-permute-start(bf16[2,1,56,6400]{3,2,1,0:T(8,128)(2,1)} %pad_maximum_fusion.13), channel_id=1, source_target_pairs={{0,8},{4,20},{8,0},{12,28},{16,24},{20,4},{24,16},{28,12},{1,9},{5... | collective-permute-start | bytes 4300808 | tf_op jit(solution)/shard_map/ppermute | solution.py:757
  665.2 23.9 %collective-permute-start.46 = (bf16[2,4,56,1600]{3,2,1,0:T(8,128)(2,1)S(1)}, bf16[2,4,56,1600]{3,2,1,0:T(8,128)(2,1)S(1)}, u32[]{:S(2)}, u32[]{:S(2)}) collective-permute-start(bf16[2,4,56,1600]{3,2,1,0:T(8,128)(2,1)S(1)} %copy-done.13), channel_id=1, source_target_pairs={{0,8},{4,20},{8,0},{12,28},{16,24},{20,4},{24,16},{28,12},{1,9},{5... | collective-permute-start | bytes 4300808 | tf_op jit(solution)/shard_map/ppermute | solution.py:757
  685.1 32.0 %collective-permute-start.45 = (bf16[4,1,56,6400]{3,2,1,0:T(8,128)(2,1)}, bf16[4,1,56,6400]{3,2,1,0:T(8,128)(2,1)}, u32[]{:S(2)}, u32[]{:S(2)}) collective-permute-start(bf16[4,1,56,6400]{3,2,1,0:T(8,128)(2,1)} %constant_dynamic-update-slice_fusion.mine_ref), channel_id=1, source_target_pairs={{0,4},{4,0},{1,5},{5,1},{2,6},{6,2},{3,7},{7,3},{8,12},{12,8},{9,1... | collective-permute-start | bytes 8601608 | tf_op jit(solution)/shard_map/ppermute | solution.py:720
  690.3 35.1 %collective-permute-start.47 = (bf16[4,4,56,1600]{3,2,1,0:T(8,128)(2,1)}, bf16[4,4,56,1600]{3,2,1,0:T(8,128)(2,1)}, u32[]{:S(2)}, u32[]{:S(2)}) collective-permute-start(bf16[4,4,56,1600]{3,2,1,0:T(8,128)(2,1)} %constant_dynamic-update-slice_fusion.2.mine_ref), channel_id=1, source_target_pairs={{0,4},{4,0},{1,5},{5,1},{2,6},{6,2},{3,7},{7,3},{8,12},{12,8},{9,1... | collective-permute-start | bytes 8601608 | tf_op jit(solution)/shard_map/ppermute | solution.py:720
  706.7 29.7 %collective-permute-start.53 = (bf16[4,1,56,6464]{3,2,1,0:T(8,128)(2,1)}, bf16[4,1,56,6464]{3,2,1,0:T(8,128)(2,1)}, u32[]{:S(2)}, u32[]{:S(2)}) collective-permute-start(bf16[4,1,56,6464]{3,2,1,0:T(8,128)(2,1)} %pad_maximum_fusion.6.mine_ref), channel_id=1, source_target_pairs={{0,4},{4,0},{1,5},{5,1},{2,6},{6,2},{3,7},{7,3},{8,12},{12,8},{9,1... | collective-permute-start | bytes 8687624 | tf_op jit(solution)/shard_map/ppermute | solution.py:720
  (89 other events, 1047.6 us)
Sparse Core Ops, SparseCore 0:
  9.6 80.8 all-gather.3
  185.4 71.0 all-gather.5
  260.1 63.3 all-gather.7
  361.9 61.5 reduce-scatter.2
  539.7 60.2 reduce-scatter.4
